TPU v7x, 32 devices: a whole 2x2x4 slice. The times are simulated.
32 devices in a mesh: dp: 8 (over z, core), seq: 4 (over y, x).
Axes of the slice: x: 2, y: 2, z: 4, core: 2. Of those that a mesh axis runs over, the one named last changes fastest.
Arguments:
- image_tokens: bfloat16 [32, 1024, 1024], P('dp', 'seq'), may hold values from -6 to 6
- text_states: bfloat16 [32, 128, 1024], P('dp', 'seq'), may hold values from -6 to 6
- text_lengths: int32 [32], P('dp'), may hold values from 8 to 128, as said below
- out_grad: bfloat16 [32, 1024, 1024], P('dp', 'seq'), may hold values from -6 to 6
- norm1_gain: bfloat16 [1024], P(('dp', 'seq')), may hold values from 0.5 to 1.5
- norm1_bias: bfloat16 [1024], P(('dp', 'seq')), may hold values from -1.75 to 1.75
- self_qkv: bfloat16 [1024, 3072], P(('dp', 'seq')), may hold values from -0.1875 to 0.1875
- self_bias_qv: bfloat16 [2048], P(('dp', 'seq')), may hold values from -1.75 to 1.75
- self_out: bfloat16 [1024, 1024], P(('dp', 'seq')), may hold values from -0.75 to 0.75
- self_out_bias: bfloat16 [1024], P(('dp', 'seq')), may hold values from -1.75 to 1.75
- norm2_gain: bfloat16 [1024], P(('dp', 'seq')), may hold values from 0.5 to 1.5
- norm2_bias: bfloat16 [1024], P(('dp', 'seq')), may hold values from -1.75 to 1.75
- cross_query: bfloat16 [1024, 1024], P(('dp', 'seq')), may hold values from -0.1875 to 0.1875
- cross_kv: bfloat16 [1024, 2048], P(('dp', 'seq')), may hold values from -0.1875 to 0.1875
- cross_bias_qv: bfloat16 [2048], P(('dp', 'seq')), may hold values from -1.75 to 1.75
- cross_out: bfloat16 [1024, 1024], P(('dp', 'seq')), may hold values from -0.375 to 0.375
- cross_out_bias: bfloat16 [1024], P(('dp', 'seq')), may hold values from -1.75 to 1.75
- norm3_gain: bfloat16 [1024], P(('dp', 'seq')), may hold values from 0.5 to 1.5
- norm3_bias: bfloat16 [1024], P(('dp', 'seq')), may hold values from -1.75 to 1.75
- mlp_in: bfloat16 [1024, 4096], P(('dp', 'seq')), may hold values from -0.1875 to 0.1875
- mlp_in_bias: bfloat16 [4096], P(('dp', 'seq')), may hold values from -1.75 to 1.75
- mlp_out: bfloat16 [4096, 1024], P(('dp', 'seq')), may hold values from -0.09375 to 0.09375
- mlp_out_bias: bfloat16 [1024], P(('dp', 'seq')), may hold values from -1.75 to 1.75
Outputs:
- block_output: bfloat16 [32, 1024, 1024], P('dp', 'seq')
- image_grad: float32 [32, 1024, 1024], P('dp', 'seq')
- text_grad: float32 [32, 128, 1024], P('dp', 'seq')
- norm1_gain_grad: float32 [1024], P(('dp', 'seq'))
- norm1_bias_grad: float32 [1024], P(('dp', 'seq'))
- self_qkv_grad: float32 [1024, 3072], P(('dp', 'seq'))
- self_bias_qv_grad: float32 [2048], P(('dp', 'seq'))
- self_out_grad: float32 [1024, 1024], P(('dp', 'seq'))
- self_out_bias_grad: float32 [1024], P(('dp', 'seq'))
- norm2_gain_grad: float32 [1024], P(('dp', 'seq'))
- norm2_bias_grad: float32 [1024], P(('dp', 'seq'))
- cross_query_grad: float32 [1024, 1024], P(('dp', 'seq'))
- cross_kv_grad: float32 [1024, 2048], P(('dp', 'seq'))
- cross_bias_qv_grad: float32 [2048], P(('dp', 'seq'))
- cross_out_grad: float32 [1024, 1024], P(('dp', 'seq'))
- cross_out_bias_grad: float32 [1024], P(('dp', 'seq'))
- norm3_gain_grad: float32 [1024], P(('dp', 'seq'))
- norm3_bias_grad: float32 [1024], P(('dp', 'seq'))
- mlp_in_grad: float32 [1024, 4096], P(('dp', 'seq'))
- mlp_in_bias_grad: float32 [4096], P(('dp', 'seq'))
- mlp_out_grad: float32 [4096, 1024], P(('dp', 'seq'))
- mlp_out_bias_grad: float32 [1024], P(('dp', 'seq'))
Inputs may be any that keep to these rules, and one draw needn't show every extreme that they name: `text_lengths`: prompt positions at or beyond an image's length are padding. In every draw some image has exactly 128 prompt tokens and some exactly 8.
All inputs are finite; a program needn't handle non-finite values.
Results may differ from a plain program's by a relative error of at most 0.025.
Values may be sent and summed in bfloat16 or wider, within the bound.
No kernel may reach another device: no remote copies, remote signals or barrier semaphores. Data moves between devices by JAX's collectives and lax.ppermute only.
A program may use at most 256 MiB of HBM per device.

v0:
```python
import jax
import jax.numpy as jnp
from jax import lax
from jax.sharding import PartitionSpec as P

D = 1024
HEADS = 16
HEAD_DIM = 64


EPSILON = 1e-05
SCALING = 0.125
NEGATIVE = -1e30


def layer_norm(values, gain, shift):
    center = values - jnp.mean(values, axis=-1, keepdims=True)
    inverse = lax.rsqrt(jnp.mean(center * center, axis=-1, keepdims=True) + EPSILON)
    normed = center * inverse
    return (normed * gain + shift, normed, inverse)


def norm_back(grad_rows, normed, inverse, gain):
    scaled = grad_rows * gain
    back = inverse * (
        scaled
        - jnp.mean(scaled, axis=-1, keepdims=True)
        - normed * jnp.mean(scaled * normed, axis=-1, keepdims=True)
    )
    return (back, jnp.sum(grad_rows * normed, axis=(0, 1)), jnp.sum(grad_rows, axis=(0, 1)))


def project(left, weight):
    return jnp.einsum("bld,de->ble", left, weight, preferred_element_type=jnp.float32)


def project_back(grad_rows, weight):
    return jnp.einsum("ble,de->bld", grad_rows, weight, preferred_element_type=jnp.float32)


def weight_grad(left, grad_rows):
    return jnp.einsum("bld,ble->de", left, grad_rows, preferred_element_type=jnp.float32)


def column_sums(grad_rows):
    return jnp.sum(grad_rows.astype(jnp.float32), axis=(0, 1))


def split_heads(rows):
    return rows.reshape(rows.shape[0], rows.shape[1], HEADS, HEAD_DIM)


def gelu_tanh(values):
    return jax.nn.gelu(values, approximate=True)


def block_scores(queries, key_rows, start, width, mask_at):
    key_block = split_heads(lax.dynamic_slice_in_dim(key_rows, start, width, 1))
    scores = (
        jnp.einsum("bqhd,bkhd->bhqk", queries, key_block, preferred_element_type=jnp.float32)
        * SCALING
    )
    return (jnp.where(mask_at(start, width), scores, NEGATIVE), key_block)


def attend(query_rows, key_rows, value_rows, mask_at, width):
    queries = split_heads(query_rows)
    batch_size, length = (query_rows.shape[0], query_rows.shape[1])
    blocks = key_rows.shape[1] // width

    def stats(block_index, carry):
        running_max, running_sum = carry
        scores, key_block = block_scores(queries, key_rows, block_index * width, width, mask_at)
        new_max = jnp.maximum(running_max, jnp.max(scores, axis=-1))
        running_sum = running_sum * jnp.exp(running_max - new_max) + jnp.sum(
            jnp.exp(scores - new_max[..., None]), axis=-1
        )
        return (new_max, running_sum)

    start_max = jnp.full((batch_size, HEADS, length), NEGATIVE, jnp.float32)
    final_max, final_sum = lax.fori_loop(0, blocks, stats, (start_max, jnp.zeros_like(start_max)))
    log_total = final_max + jnp.log(final_sum)

    def accumulate(block_index, total):
        start = block_index * width
        scores, key_block = block_scores(queries, key_rows, start, width, mask_at)
        weights = jnp.exp(scores - log_total[..., None]).astype(jnp.bfloat16)
        value_block = split_heads(lax.dynamic_slice_in_dim(value_rows, start, width, 1))
        return total + jnp.einsum(
            "bhqk,bkhd->bqhd", weights, value_block, preferred_element_type=jnp.float32
        )

    total = lax.fori_loop(
        0, blocks, accumulate, jnp.zeros((batch_size, length, HEADS, HEAD_DIM), jnp.float32)
    )
    return (total.reshape(batch_size, length, HEADS * HEAD_DIM).astype(jnp.bfloat16), log_total)


def attend_back(query_rows, key_rows, value_rows, grad_rows, log_total, mask_at, width):
    queries = split_heads(query_rows)
    grad_heads = split_heads(grad_rows)
    batch_size, length = (query_rows.shape[0], query_rows.shape[1])
    blocks = key_rows.shape[1] // width

    def weights_at(start):
        scores, key_block = block_scores(queries, key_rows, start, width, mask_at)
        value_block = split_heads(lax.dynamic_slice_in_dim(value_rows, start, width, 1))
        probs = jnp.exp(scores - log_total[..., None])
        grad_probs = jnp.einsum(
            "bqhd,bkhd->bhqk", grad_heads, value_block, preferred_element_type=jnp.float32
        )
        return (probs, grad_probs, key_block)

    def inner(block_index, delta):
        probs, grad_probs, key_block = weights_at(block_index * width)
        return delta + jnp.sum(probs * grad_probs, axis=-1)

    delta = lax.fori_loop(0, blocks, inner, jnp.zeros((batch_size, HEADS, length), jnp.float32))
    start_grad = jnp.zeros((batch_size, length, HEADS, HEAD_DIM), jnp.float32)

    def step(grad_queries, block_index):
        probs, grad_probs, key_block = weights_at(block_index * width)
        grad_scores = (probs * (grad_probs - delta[..., None])).astype(jnp.bfloat16)
        grad_queries = grad_queries + jnp.einsum(
            "bhqk,bkhd->bqhd", grad_scores, key_block, preferred_element_type=jnp.float32
        )
        grad_keys = jnp.einsum(
            "bhqk,bqhd->bkhd", grad_scores, queries, preferred_element_type=jnp.float32
        )
        grad_values = jnp.einsum(
            "bhqk,bqhd->bkhd",
            probs.astype(jnp.bfloat16),
            grad_heads,
            preferred_element_type=jnp.float32,
        )
        return (grad_queries, (grad_keys, grad_values))

    grad_queries, (key_parts, value_parts) = lax.scan(
        step, start_grad, jnp.arange(blocks, dtype=jnp.int32)
    )

    def merge_blocks(parts):
        return jnp.moveaxis(parts, 0, 1).reshape(batch_size, blocks * width, HEADS * HEAD_DIM)

    return (
        (grad_queries * SCALING).reshape(batch_size, length, HEADS * HEAD_DIM),
        merge_blocks(key_parts) * SCALING,
        merge_blocks(value_parts),
        delta,
    )


def gather_self(gain, shift, weight_qkv, bias_qv, weight_out, bias_out):
    return (
        lax.all_gather(gain, ("dp", "seq"), axis=0, tiled=True),
        lax.all_gather(shift, ("dp", "seq"), axis=0, tiled=True),
        lax.all_gather(weight_qkv, ("dp", "seq"), axis=0, tiled=True),
        lax.all_gather(bias_qv, ("dp", "seq"), axis=0, tiled=True),
        lax.all_gather(weight_out, ("dp", "seq"), axis=0, tiled=True),
        lax.all_gather(bias_out, ("dp", "seq"), axis=0, tiled=True),
    )


def gather_cross(gain, shift, weight_query, weight_kv, bias_qv, weight_out, bias_out):
    return (
        lax.all_gather(gain, ("dp", "seq"), axis=0, tiled=True),
        lax.all_gather(shift, ("dp", "seq"), axis=0, tiled=True),
        lax.all_gather(weight_query, ("dp", "seq"), axis=0, tiled=True),
        lax.all_gather(weight_kv, ("dp", "seq"), axis=0, tiled=True),
        lax.all_gather(bias_qv, ("dp", "seq"), axis=0, tiled=True),
        lax.all_gather(weight_out, ("dp", "seq"), axis=0, tiled=True),
        lax.all_gather(bias_out, ("dp", "seq"), axis=0, tiled=True),
    )


def gather_mlp(gain, shift, weight_in, bias_in, weight_out, bias_out):
    return (
        lax.all_gather(gain, ("dp", "seq"), axis=0, tiled=True),
        lax.all_gather(shift, ("dp", "seq"), axis=0, tiled=True),
        lax.all_gather(weight_in, ("dp", "seq"), axis=0, tiled=True),
        lax.all_gather(bias_in, ("dp", "seq"), axis=0, tiled=True),
        lax.all_gather(weight_out, ("dp", "seq"), axis=0, tiled=True),
        lax.all_gather(bias_out, ("dp", "seq"), axis=0, tiled=True),
    )


def per_device(
    image_tokens,
    text_states,
    text_lengths,
    out_grad,
    norm1_gain,
    norm1_bias,
    self_qkv,
    self_bias_qv,
    self_out,
    self_out_bias,
    norm2_gain,
    norm2_bias,
    cross_query,
    cross_kv,
    cross_bias_qv,
    cross_out,
    cross_out_bias,
    norm3_gain,
    norm3_bias,
    mlp_in,
    mlp_in_bias,
    mlp_out,
    mlp_out_bias,
):
    length = image_tokens.shape[1]
    own_start = lax.axis_index("seq") * length
    query_pos = own_start + jnp.arange(length, dtype=jnp.int32)

    def causal_at(start, width):
        key_pos = start + jnp.arange(width, dtype=jnp.int32)
        return (key_pos[None, :] <= query_pos[:, None])[None, None]

    def padded_at(start, width):
        key_pos = start + jnp.arange(width, dtype=jnp.int32)
        return (key_pos[None, :] < text_lengths[:, None])[:, None, None, :]

    self_full = gather_self(norm1_gain, norm1_bias, self_qkv, self_bias_qv, self_out, self_out_bias)
    residual = image_tokens.astype(jnp.float32)
    normed_in, normed_one, inverse_one = layer_norm(
        residual, self_full[0].astype(jnp.float32), self_full[1].astype(jnp.float32)
    )
    hidden_one = normed_in.astype(jnp.bfloat16)
    mixed = project(hidden_one, self_full[2])
    bias_self = self_full[3].astype(jnp.float32)
    query_one = (mixed[..., :D] + bias_self[:D]).astype(jnp.bfloat16)
    key_one = mixed[..., D : 2 * D].astype(jnp.bfloat16)
    value_one = (mixed[..., 2 * D :] + bias_self[D:]).astype(jnp.bfloat16)
    key_all, value_all = (
        lax.all_gather(key_one, "seq", axis=1, tiled=True),
        lax.all_gather(value_one, "seq", axis=1, tiled=True),
    )
    self_width = min(128, key_all.shape[1])
    attended, log_one = attend(query_one, key_all, value_all, causal_at, self_width)
    after_self = residual + project(attended, self_full[4]) + self_full[5].astype(jnp.float32)
    cross_full = gather_cross(
        norm2_gain, norm2_bias, cross_query, cross_kv, cross_bias_qv, cross_out, cross_out_bias
    )
    normed_mid, normed_two, inverse_two = layer_norm(
        after_self, cross_full[0].astype(jnp.float32), cross_full[1].astype(jnp.float32)
    )
    hidden_two = normed_mid.astype(jnp.bfloat16)
    bias_cross = cross_full[4].astype(jnp.float32)
    query_two = (project(hidden_two, cross_full[2]) + bias_cross[:D]).astype(jnp.bfloat16)
    text_mixed = project(text_states, cross_full[3])
    text_key = text_mixed[..., :D].astype(jnp.bfloat16)
    text_value = (text_mixed[..., D:] + bias_cross[D:]).astype(jnp.bfloat16)
    key_two, value_two = (
        lax.all_gather(text_key, "seq", axis=1, tiled=True),
        lax.all_gather(text_value, "seq", axis=1, tiled=True),
    )
    text_width = key_two.shape[1]
    attended_two, log_two = attend(query_two, key_two, value_two, padded_at, text_width)
    after_cross = (
        after_self + project(attended_two, cross_full[5]) + cross_full[6].astype(jnp.float32)
    )
    mlp_full = gather_mlp(norm3_gain, norm3_bias, mlp_in, mlp_in_bias, mlp_out, mlp_out_bias)
    normed_last, normed_three, inverse_three = layer_norm(
        after_cross, mlp_full[0].astype(jnp.float32), mlp_full[1].astype(jnp.float32)
    )
    hidden_three = normed_last.astype(jnp.bfloat16)
    pre_act = project(hidden_three, mlp_full[2]) + mlp_full[3].astype(jnp.float32)
    activated, gelu_back = jax.vjp(gelu_tanh, pre_act)
    act_low = activated.astype(jnp.bfloat16)
    block_output = (
        after_cross + project(act_low, mlp_full[4]) + mlp_full[5].astype(jnp.float32)
    ).astype(jnp.bfloat16)
    mlp_back = gather_mlp(norm3_gain, norm3_bias, mlp_in, mlp_in_bias, mlp_out, mlp_out_bias)
    grad_top = out_grad.astype(jnp.float32)
    w_out_grad = weight_grad(act_low, out_grad)
    b_out_grad = column_sums(out_grad)
    grad_act = project_back(out_grad, mlp_back[4])
    grad_pre = gelu_back(grad_act)[0].astype(jnp.bfloat16)
    w_in_grad = weight_grad(hidden_three, grad_pre)
    b_in_grad = column_sums(grad_pre)
    back_three, gain_three_grad, shift_three_grad = norm_back(
        project_back(grad_pre, mlp_back[2]),
        normed_three,
        inverse_three,
        mlp_back[0].astype(jnp.float32),
    )
    grad_two = grad_top + back_three
    mlp_grads = (
        lax.psum_scatter(gain_three_grad, ("dp", "seq"), scatter_dimension=0, tiled=True),
        lax.psum_scatter(shift_three_grad, ("dp", "seq"), scatter_dimension=0, tiled=True),
        lax.psum_scatter(w_in_grad, ("dp", "seq"), scatter_dimension=0, tiled=True),
        lax.psum_scatter(b_in_grad, ("dp", "seq"), scatter_dimension=0, tiled=True),
        lax.psum_scatter(w_out_grad, ("dp", "seq"), scatter_dimension=0, tiled=True),
        lax.psum_scatter(b_out_grad, ("dp", "seq"), scatter_dimension=0, tiled=True),
    )
    cross_back = gather_cross(
        norm2_gain, norm2_bias, cross_query, cross_kv, cross_bias_qv, cross_out, cross_out_bias
    )
    grad_cross = grad_two.astype(jnp.bfloat16)
    cross_out_term = weight_grad(attended_two, grad_cross)
    cross_bias_term = column_sums(grad_cross)
    grad_att_two = project_back(grad_cross, cross_back[5]).astype(jnp.bfloat16)
    grad_query_two, grad_key_two, grad_value_two, delta_two = attend_back(
        query_two, key_two, value_two, grad_att_two, log_two, padded_at, text_width
    )
    query_two_low = grad_query_two.astype(jnp.bfloat16)
    text_key_grad, text_value_grad = (
        lax.psum_scatter(
            grad_key_two.astype(jnp.bfloat16), "seq", scatter_dimension=1, tiled=True
        ).astype(jnp.float32),
        lax.psum_scatter(
            grad_value_two.astype(jnp.bfloat16), "seq", scatter_dimension=1, tiled=True
        ).astype(jnp.float32),
    )
    text_value_low = text_value_grad.astype(jnp.bfloat16)
    text_kv_grad = jnp.concatenate([text_key_grad.astype(jnp.bfloat16), text_value_low], axis=-1)
    cross_query_term = weight_grad(hidden_two, query_two_low)
    cross_kv_term = weight_grad(text_states, text_kv_grad)
    cross_qv_term = jnp.concatenate([column_sums(query_two_low), column_sums(text_value_low)])
    text_grad = project_back(text_kv_grad, cross_back[3])
    back_two, gain_two_grad, shift_two_grad = norm_back(
        project_back(query_two_low, cross_back[2]),
        normed_two,
        inverse_two,
        cross_back[0].astype(jnp.float32),
    )
    grad_one = grad_two + back_two
    cross_grads = (
        lax.psum_scatter(gain_two_grad, ("dp", "seq"), scatter_dimension=0, tiled=True),
        lax.psum_scatter(shift_two_grad, ("dp", "seq"), scatter_dimension=0, tiled=True),
        lax.psum_scatter(cross_query_term, ("dp", "seq"), scatter_dimension=0, tiled=True),
        lax.psum_scatter(cross_kv_term, ("dp", "seq"), scatter_dimension=0, tiled=True),
        lax.psum_scatter(cross_qv_term, ("dp", "seq"), scatter_dimension=0, tiled=True),
        lax.psum_scatter(cross_out_term, ("dp", "seq"), scatter_dimension=0, tiled=True),
        lax.psum_scatter(cross_bias_term, ("dp", "seq"), scatter_dimension=0, tiled=True),
    )
    self_back = gather_self(norm1_gain, norm1_bias, self_qkv, self_bias_qv, self_out, self_out_bias)
    grad_self = grad_one.astype(jnp.bfloat16)
    self_out_term = weight_grad(attended, grad_self)
    self_bias_term = column_sums(grad_self)
    grad_att_one = project_back(grad_self, self_back[4]).astype(jnp.bfloat16)
    grad_query_one, grad_key_all, grad_value_all, delta_one = attend_back(
        query_one, key_all, value_all, grad_att_one, log_one, causal_at, self_width
    )
    grad_key_one, grad_value_one = (
        lax.psum_scatter(
            grad_key_all.astype(jnp.bfloat16), "seq", scatter_dimension=1, tiled=True
        ).astype(jnp.float32),
        lax.psum_scatter(
            grad_value_all.astype(jnp.bfloat16), "seq", scatter_dimension=1, tiled=True
        ).astype(jnp.float32),
    )
    query_one_low = grad_query_one.astype(jnp.bfloat16)
    value_one_low = grad_value_one.astype(jnp.bfloat16)
    grad_qkv = jnp.concatenate(
        [query_one_low, grad_key_one.astype(jnp.bfloat16), value_one_low], axis=-1
    )
    self_qkv_term = weight_grad(hidden_one, grad_qkv)
    self_qv_term = jnp.concatenate([column_sums(query_one_low), column_sums(value_one_low)])
    back_one, gain_one_grad, shift_one_grad = norm_back(
        project_back(grad_qkv, self_back[2]),
        normed_one,
        inverse_one,
        self_back[0].astype(jnp.float32),
    )
    image_grad = grad_one + back_one
    self_grads = (
        lax.psum_scatter(gain_one_grad, ("dp", "seq"), scatter_dimension=0, tiled=True),
        lax.psum_scatter(shift_one_grad, ("dp", "seq"), scatter_dimension=0, tiled=True),
        lax.psum_scatter(self_qkv_term, ("dp", "seq"), scatter_dimension=0, tiled=True),
        lax.psum_scatter(self_qv_term, ("dp", "seq"), scatter_dimension=0, tiled=True),
        lax.psum_scatter(self_out_term, ("dp", "seq"), scatter_dimension=0, tiled=True),
        lax.psum_scatter(self_bias_term, ("dp", "seq"), scatter_dimension=0, tiled=True),
    )
    return (
        block_output,
        image_grad,
        text_grad,
        self_grads[0],
        self_grads[1],
        self_grads[2],
        self_grads[3],
        self_grads[4],
        self_grads[5],
        cross_grads[0],
        cross_grads[1],
        cross_grads[2],
        cross_grads[3],
        cross_grads[4],
        cross_grads[5],
        cross_grads[6],
        mlp_grads[0],
        mlp_grads[1],
        mlp_grads[2],
        mlp_grads[3],
        mlp_grads[4],
        mlp_grads[5],
    )


def solution(mesh):
    placed = (
        P("dp", "seq", None),
        P("dp", "seq", None),
        P("dp"),
        P("dp", "seq", None),
        P(("dp", "seq")),
        P(("dp", "seq")),
        P(("dp", "seq"), None),
        P(("dp", "seq")),
        P(("dp", "seq"), None),
        P(("dp", "seq")),
        P(("dp", "seq")),
        P(("dp", "seq")),
        P(("dp", "seq"), None),
        P(("dp", "seq"), None),
        P(("dp", "seq")),
        P(("dp", "seq"), None),
        P(("dp", "seq")),
        P(("dp", "seq")),
        P(("dp", "seq")),
        P(("dp", "seq"), None),
        P(("dp", "seq")),
        P(("dp", "seq"), None),
        P(("dp", "seq")),
    )
    return jax.shard_map(
        per_device,
        mesh=mesh,
        in_specs=placed,
        out_specs=(
            P("dp", "seq", None),
            P("dp", "seq", None),
            P("dp", "seq", None),
            P(("dp", "seq")),
            P(("dp", "seq")),
            P(("dp", "seq"), None),
            P(("dp", "seq")),
            P(("dp", "seq"), None),
            P(("dp", "seq")),
            P(("dp", "seq")),
            P(("dp", "seq")),
            P(("dp", "seq"), None),
            P(("dp", "seq"), None),
            P(("dp", "seq")),
            P(("dp", "seq"), None),
            P(("dp", "seq")),
            P(("dp", "seq")),
            P(("dp", "seq")),
            P(("dp", "seq"), None),
            P(("dp", "seq")),
            P(("dp", "seq"), None),
            P(("dp", "seq")),
        ),
        check_vma=False,
    )
```

profile of v0, /device:TPU:0, one launch (start us, length us, event | category | flops | bytes accessed | tf_op | source)
XLA Modules:
  0.0 2874.9 jit_solution(14863094227326183235)
XLA Ops:
  8.9 66.9 %all-gather.21.cloned.1.call-done = bf16[1024,2048]{1,0:T(8,128)(2,1)} async-done(((bf16[32,2048]{1,0:T(8,128)(2,1)}), bf16[1024,2048]{1,0:T(8,128)(2,1)}) %all-gather.21.cloned.1.call-update) | async-done | bytes 4194320 | tf_op jit(solution)/shard_map/all_gather | solution.py:169
  82.2 40.1 %all-reduce.24 = (bf16[2048]{0:T(1024)(128)(2,1)S(1)}, bf16[2048]{0:T(1024)(128)(2,1)S(1)}, bf16[1024]{0:T(1024)(128)(2,1)S(1)}, bf16[1024]{0:T(1024)(128)(2,1)S...) all-reduce(bf16[2048]{0:T(1024)(128)(2,1)S(1)} %dynamic-update-slic, ...), channel_id=1, replica_groups=mesh['dp'=8,'seq'=4] {'dp','seq'}, use_global_device_ids=true, to_apply=%add.2 | all-reduce | flops 13312 | bytes 53248
  124.8 22.2 all-gather.13.cloned.1.call-done
  147.0 9.0 fusion.63
  156.1 4.5 copy-done.24
  162.4 6.8 fusion.81
  173.7 65.8 %all-gather = bf16[32,1,128]{2,1,0:T(2,128)(2,1)S(1)} all-gather(bf16[1,1,128]{2,1,0:T(2,128)(2,1)S(1)} %bitcast.324), channel_id=1, replica_groups=mesh['dp'=8,'seq'=4] {'dp','seq'}, dimensions={0}, use_global_device_ids=true | all-gather | bytes 8448 | tf_op jit(solution)/shard_map/all_gather | solution.py:181
  247.1 45.8 %all-gather.17.cloned.1.call-done = bf16[4,1024,1024]{2,1,0:T(8,128)(2,1)} async-done(((bf16[4,256,1024]{2,1,0:T(8,128)(2,1)}), bf16[4,1024,1024]{2,1,0:T(8,128)(2,1)}) %all-gather.17.cloned.1.call-update) | async-done | bytes 8388624 | tf_op jit(solution)/shard_map/all_gather | solution.py:236
  292.9 11.7 copy.129
  304.6 43.5 %while.18 = (s32[]{:T(128)}, f32[4,16,256]{2,1,0:T(8,128)S(1)}, f32[4,16,256]{2,1,0:T(8,128)S(1)}, bf16[4,1024,1024]{1,2,0:T(8,128)(2,1)}, bf16[4,256,16,64]{1,3...) while((s32[]{:T(128)}, f32[4,16,256]{2,1,0:T(8,128)S(1)}, ...), condition=%wide.region_5.6_spmd.clone, body=%wide.region_2.5_spmd.clone.sunk | while | flops 283230592 | bytes 22973616 | solution.py:81
  348.1 34.2 %all-gather.15.cloned.1.call-done = bf16[4,1024,1024]{2,1,0:T(8,128)(2,1)} async-done(((bf16[4,256,1024]{2,1,0:T(8,128)(2,1)}), bf16[4,1024,1024]{2,1,0:T(8,128)(2,1)}) %all-gather.15.cloned.1.call-update) | async-done | bytes 8388624 | tf_op jit(solution)/shard_map/all_gather | solution.py:237
  382.3 11.4 copy.128
  393.7 81.0 %while.38 = (s32[]{:T(128)}, f32[4,256,16,64]{1,3,2,0:T(8,128)}, bf16[4,1024,1024]{1,2,0:T(8,128)(2,1)}, bf16[4,1024,1024]{1,2,0:T(8,128)(2,1)}, bf16[4,256,16,6...) while((s32[]{:T(128)}, f32[4,256,16,64]{1,3,2,0:T(8,128)}, ...), condition=%wide.region_7.8_spmd.clone, body=%wide.region_6.7_spmd.clone.sunk | while | flops 547389824 | bytes 16911544 | solution.py:93
  396.5 6.1 bitcast_add_fusion.4
  405.4 7.4 bitcast_add_fusion.4
  415.5 7.4 bitcast_add_fusion.4
  425.7 7.6 bitcast_add_fusion.4
  436.2 7.4 bitcast_add_fusion.4
  446.4 7.4 bitcast_add_fusion.4
  456.6 7.4 bitcast_add_fusion.4
  466.7 7.4 bitcast_add_fusion.4
  474.7 4.6 convert_element_type.221
  479.3 5.7 fusion.130
  487.6 12.1 all-gather.25.cloned.1.call-done
  499.8 6.6 add_convert_fusion.2
  517.3 40.6 %all-gather.29.cloned.1.call-done = bf16[1024,1024]{1,0:T(8,128)(2,1)} async-done(((bf16[32,1024]{1,0:T(8,128)(2,1)}), bf16[1024,1024]{1,0:T(8,128)(2,1)}) %all-gather.29.cloned.1.call-update) | async-done | bytes 2097168 | tf_op jit(solution)/shard_map/all_gather | solution.py:171
  557.9 5.5 fusion.131
  566.0 71.1 %all-gather.31.cloned.1.call-done = bf16[1024,4096]{1,0:T(8,128)(2,1)} async-done(((bf16[32,4096]{1,0:T(8,128)(2,1)}), bf16[1024,4096]{1,0:T(8,128)(2,1)}) %all-gather.31.cloned.1.call-update) | async-done | bytes 8388624 | tf_op jit(solution)/shard_map/all_gather | solution.py:180
  637.1 16.1 fusion.56
  653.1 63.0 %all-gather.33.cloned.1.call-done = bf16[4096,1024]{1,0:T(8,128)(2,1)} async-done(((bf16[128,1024]{1,0:T(8,128)(2,1)}), bf16[4096,1024]{1,0:T(8,128)(2,1)}) %all-gather.33.cloned.1.call-update) | async-done | bytes 8388624 | tf_op jit(solution)/shard_map/all_gather | solution.py:182
  716.1 24.7 convert_reduce_fusion
  740.8 16.4 multiply_reduce_fusion.1
  767.6 6.6 convolution_convert_fusion.1
  774.2 7.3 multiply_reduce_fusion
  783.8 7.9 multiply_convert_fusion.2
  797.0 4.4 multiply_reduce_fusion.2
  815.3 52.9 %while.39 = (s32[]{:T(128)}, f32[4,16,256]{2,1,0:T(8,128)S(1)}, bf16[4,1024,1024]{1,2,0:T(8,128)(2,1)}, bf16[4,256,16,64]{1,3,2,0:T(8,128)(2,1)S(1)}, f32[4,16,2...) while((s32[]{:T(128)}, f32[4,16,256]{2,1,0:T(8,128)S(1)}, ...), condition=%wide.region_21.22_spmd.clone, body=%wide.region_19.21_spmd.clone.sunk | while | flops 547406208 | bytes 36048088 | solution.py:118
  868.3 117.0 %while.40 = (s32[]{:T(128)}, f32[4,256,16,64]{1,3,2,0:T(8,128)}, f32[8,4,128,16,64]{2,4,3,1,0:T(8,128)}, bf16[8,4,128,16,64]{2,4,3,1,0:T(8,128)(2,1)}, s32[8]{0:...) while((s32[]{:T(128)}, f32[4,256,16,64]{1,3,2,0:T(8,128)}, ...), condition=%wide.region_23.24_spmd.clone, body=%wide.region_22.23_spmd.clone.sunk | while | flops 1365279104 | bytes 108301640 | solution.py:138
  985.2 18.7 copy.176
  1004.0 22.6 reshape.449
  1026.6 10.0 fusion.49
  1036.6 19.0 copy.175
  1055.6 22.8 reshape.448
  1085.1 4.4 convert_reduce_fusion.7
  1095.5 16.2 reduce-scatter.16.cloned.1.call-done
  1114.2 86.8 %reduce-scatter.14.cloned.1.call-done = bf16[4,256,1024]{2,1,0:T(8,128)(2,1)} async-done(((bf16[4,1024,1024]{2,1,0:T(8,128)(2,1)}), bf16[4,256,1024]{2,1,0:T(8,128)(2,1)}) %reduce-scatter.14.cloned.1.call-update) | async-done | bytes 2097168 | tf_op jit(solution)/shard_map/reduce_scatter | solution.py:347
  1201.0 13.6 fusion.78
  1214.7 6.7 convolution_bitcast_fusion.4
  1222.1 7.6 convolution_bitcast_fusion.5
  1229.8 7.3 convolution_bitcast_fusion.6
  1238.2 4.6 convolution_bitcast_fusion.3
  1242.8 9.2 copy.177
  1252.7 20.2 convolution_bitcast_fusion
  1273.6 16.4 convolution_bitcast_fusion.1
  1290.6 14.4 convolution_bitcast_fusion.2
  1305.7 18.7 add_convert_fusion
  1329.5 34.5 %all-reduce.27.cloned.1.call-done = (f32[1024]{0:T(1024)}, f32[1024]{0:T(1024)}, f32[2048]{0:T(1024)}, f32[1024]{0:T(1024)}, f32[1024]{0:T(1024)}, /*index=5*/f3...) async-done(((f32[1024]{0:T(1024)}, f32[1024]{0:T(1024)}, f32[2048]{0:T(1024)}, ...) | async-done | bytes 69648
  1379.1 132.1 %reduce-scatter.28.cloned.1.call-done = f32[32,1024]{1,0:T(8,128)} async-done(((f32[1024,1024]{1,0:T(8,128)}), f32[32,1024]{1,0:T(8,128)}) %reduce-scatter.28.cloned.1.call-update) | async-done | bytes 131088 | tf_op jit(solution)/shard_map/reduce_scatter | solution.py:335
  1511.2 141.7 %reduce-scatter.26.cloned.1.call-done = f32[32,1024]{1,0:T(8,128)} async-done(((f32[1024,1024]{1,0:T(8,128)}), f32[32,1024]{1,0:T(8,128)}) %reduce-scatter.26.cloned.1.call-update) | async-done | bytes 131088 | tf_op jit(solution)/shard_map/reduce_scatter | solution.py:332
  1653.0 142.2 %reduce-scatter.24.cloned.1.call-done = f32[32,1024]{1,0:T(8,128)} async-done(((f32[1024,1024]{1,0:T(8,128)}), f32[32,1024]{1,0:T(8,128)}) %reduce-scatter.24.cloned.1.call-update) | async-done | bytes 131088 | tf_op jit(solution)/shard_map/reduce_scatter | solution.py:373
  1795.2 184.8 %reduce-scatter.34.cloned.1.call-done = f32[32,2048]{1,0:T(8,128)} async-done(((f32[1024,2048]{1,0:T(8,128)}), f32[32,2048]{1,0:T(8,128)}) %reduce-scatter.34.cloned.1.call-update) | async-done | bytes 262160
  1980.0 361.6 %reduce-scatter.32.cloned.1.call-done = f32[128,1024]{1,0:T(8,128)} async-done(((f32[4096,1024]{1,0:T(8,128)}), f32[128,1024]{1,0:T(8,128)}) %reduce-scatter.32.cloned.1.call-update) | async-done | bytes 524304 | tf_op jit(solution)/shard_map/reduce_scatter | solution.py:294
  2341.6 362.0 %reduce-scatter.30.cloned.1.call-done = f32[32,4096]{1,0:T(8,128)} async-done(((f32[1024,4096]{1,0:T(8,128)}), f32[32,4096]{1,0:T(8,128)}) %reduce-scatter.30.cloned.1.call-update) | async-done | bytes 524304 | tf_op jit(solution)/shard_map/reduce_scatter | solution.py:292
  2703.6 164.5 %reduce-scatter.22.cloned.1.call-done = f32[32,3072]{1,0:T(8,128)} async-done(((f32[1024,3072]{1,0:T(8,128)}), f32[32,3072]{1,0:T(8,128)}) %reduce-scatter.22.cloned.1.call-update) | async-done | bytes 393232 | tf_op jit(solution)/shard_map/reduce_scatter | solution.py:371
  (633 shorter events, 340.1 us)
Async XLA Ops:
  7.2 68.6 %copy-start = (bf16[4,32,1024]{2,1,0:T(8,128)(2,1)S(1)}, bf16[4,32,1024]{2,1,0:T(8,128)(2,1)}, u32[]{:S(2)}) copy-start(bf16[4,32,1024]{2,1,0:T(8,128)(2,1)} %param.32) | copy-start | bytes 786436
  7.2 72.3 %copy-start.78 = (bf16[32]{0:T(256)(128)(2,1)S(1)}, bf16[32]{0:T(256)(128)(2,1)}, u32[]{:S(2)}) copy-start(bf16[32]{0:T(256)(128)(2,1)} %param.49) | copy-start | bytes 196
  7.2 72.6 %copy-start.79 = (bf16[32]{0:T(256)(128)(2,1)S(1)}, bf16[32]{0:T(256)(128)(2,1)}, u32[]{:S(2)}) copy-start(bf16[32]{0:T(256)(128)(2,1)} %param.53) | copy-start | bytes 196
  7.2 72.8 %copy-start.80 = (bf16[32]{0:T(256)(128)(2,1)S(1)}, bf16[32]{0:T(256)(128)(2,1)}, u32[]{:S(2)}) copy-start(bf16[32]{0:T(256)(128)(2,1)} %param.41) | copy-start | bytes 196
  7.2 73.0 %copy-start.81 = (bf16[32]{0:T(256)(128)(2,1)S(1)}, bf16[32]{0:T(256)(128)(2,1)}, u32[]{:S(2)}) copy-start(bf16[32]{0:T(256)(128)(2,1)} %param.42) | copy-start | bytes 196
  7.3 73.3 %copy-start.82 = (bf16[32]{0:T(256)(128)(2,1)S(1)}, bf16[32]{0:T(256)(128)(2,1)}, u32[]{:S(2)}) copy-start(bf16[32]{0:T(256)(128)(2,1)} %param.47) | copy-start | bytes 196
  7.3 73.5 %copy-start.83 = (bf16[32]{0:T(256)(128)(2,1)S(1)}, bf16[32]{0:T(256)(128)(2,1)}, u32[]{:S(2)}) copy-start(bf16[32]{0:T(256)(128)(2,1)} %param.35) | copy-start | bytes 196
  7.3 73.7 %copy-start.84 = (bf16[32]{0:T(256)(128)(2,1)S(1)}, bf16[32]{0:T(256)(128)(2,1)}, u32[]{:S(2)}) copy-start(bf16[32]{0:T(256)(128)(2,1)} %param.36) | copy-start | bytes 196
  7.3 73.9 %copy-start.85 = (bf16[32]{0:T(256)(128)(2,1)S(1)}, bf16[32]{0:T(256)(128)(2,1)}, u32[]{:S(2)}) copy-start(bf16[32]{0:T(256)(128)(2,1)} %param.40) | copy-start | bytes 196
  7.3 74.2 %copy-start.86 = (bf16[32]{0:T(256)(128)(2,1)S(1)}, bf16[32]{0:T(256)(128)(2,1)}, u32[]{:S(2)}) copy-start(bf16[32]{0:T(256)(128)(2,1)} %param.48) | copy-start | bytes 196
  7.3 74.4 %copy-start.87 = (bf16[64]{0:T(256)(128)(2,1)S(1)}, bf16[64]{0:T(256)(128)(2,1)}, u32[]{:S(2)}) copy-start(bf16[64]{0:T(256)(128)(2,1)} %param.38) | copy-start | bytes 388
  7.3 74.6 %copy-start.88 = (bf16[64]{0:T(256)(128)(2,1)S(1)}, bf16[64]{0:T(256)(128)(2,1)}, u32[]{:S(2)}) copy-start(bf16[64]{0:T(256)(128)(2,1)} %param.45) | copy-start | bytes 388
  7.3 115.0 %copy-start.13 = (bf16[4,256,1024]{2,1,0:T(8,128)(2,1)S(1)}, bf16[4,256,1024]{2,1,0:T(8,128)(2,1)}, u32[]{:S(2)}) copy-start(bf16[4,256,1024]{2,1,0:T(8,128)(2,1)} %param.31) | copy-start | bytes 6291460
  7.3 68.5 %all-gather.21.cloned.1.call-start = ((), (), s32[]{:S(2)}) async-start(), calls=%async_computation.15 | async-start | bytes 4325376 | tf_op jit(solution)/shard_map/all_gather | solution.py:169
  8.1 139.0 %all-gather.13.cloned.1.call-start = ((), (), s32[]{:S(2)}) async-start(), calls=%async_computation.11 | async-start | bytes 6488064 | tf_op jit(solution)/shard_map/all_gather | solution.py:157
  8.8 230.7 %all-gather.27.cloned.1.call-start = ((), (), s32[]{:S(2)}) async-start(), calls=%async_computation.18 | async-start | bytes 1310720 | tf_op jit(solution)/shard_map/all_gather | solution.py:255
  79.5 162.4 %all-gather.23.cloned.1.call-start = ((), (), s32[]{:S(2)}) async-start(), calls=%async_computation.16 | async-start | bytes 1310720 | tf_op jit(solution)/shard_map/all_gather | solution.py:256
  122.6 33.4 %copy-start.38 = (f32[4,256]{1,0:T(4,128)}, f32[4,256]{1,0:T(4,128)S(1)}, u32[]{:S(2)}) copy-start(f32[4,256]{1,0:T(4,128)S(1)} %broadcast_multiply_fusion.8) | copy-start | bytes 12292
  124.7 168.2 %all-gather.17.cloned.1.call-start = ((), (), s32[]{:S(2)}) async-start(), calls=%async_computation.13 | async-start | bytes 10485760 | tf_op jit(solution)/shard_map/all_gather | solution.py:236
  124.8 31.3 %copy-start.50 = (f32[4,256]{1,0:T(4,128)}, f32[4,256]{1,0:T(4,128)S(1)}, u32[]{:S(2)}) copy-start(f32[4,256]{1,0:T(4,128)S(1)} %add_rsqrt_fusion.2) | copy-start | bytes 12292
  124.8 31.2 %copy-start.52 = (f32[1024]{0:T(1024)}, f32[1024]{0:T(1024)S(1)}, u32[]{:S(2)}) copy-start(f32[1024]{0:T(1024)S(1)} %convert_element_type.215) | copy-start | bytes 12292
  124.8 31.2 %copy-start.65 = (f32[1024]{0:T(1024)}, f32[1024]{0:T(1024)S(1)}, u32[]{:S(2)}) copy-start(f32[1024]{0:T(1024)S(1)} %convert_element_type.216) | copy-start | bytes 12292
  162.3 220.0 %all-gather.15.cloned.1.call-start = ((), (), s32[]{:S(2)}) async-start(), calls=%async_computation.12 | async-start | bytes 10485760 | tf_op jit(solution)/shard_map/all_gather | solution.py:237
  162.4 10.5 copy-start.89
  162.4 11.3 copy-start.74
  169.2 310.1 %all-gather.19.cloned.1.call-start = ((), (), s32[]{:S(2)}) async-start(), calls=%async_computation.14 | async-start | bytes 2162688 | tf_op jit(solution)/shard_map/all_gather | solution.py:159
  170.0 329.8 %all-gather.25.cloned.1.call-start = ((), (), s32[]{:S(2)}) async-start(), calls=%async_computation.17 | async-start | bytes 2162688 | tf_op jit(solution)/shard_map/all_gather | solution.py:168
  170.7 387.2 %all-gather.29.cloned.1.call-start = ((), (), s32[]{:S(2)}) async-start(), calls=%async_computation.19 | async-start | bytes 2162688 | tf_op jit(solution)/shard_map/all_gather | solution.py:171
  171.5 465.6 %all-gather.31.cloned.1.call-start = ((), (), s32[]{:S(2)}) async-start(), calls=%async_computation.20 | async-start | bytes 8650752 | tf_op jit(solution)/shard_map/all_gather | solution.py:180
  172.0 544.1 %all-gather.33.cloned.1.call-start = ((), (), s32[]{:S(2)}) async-start(), calls=%async_computation.21 | async-start | bytes 8650752 | tf_op jit(solution)/shard_map/all_gather | solution.py:182
  172.8 921.1 %reduce-scatter.20.cloned.1.call-start = ((), (), s32[]{:S(2)}) async-start(), calls=%async_computation.25 | async-start | bytes 1310720 | tf_op jit(solution)/shard_map/reduce_scatter | solution.py:312
  173.0 340.7 %copy-start.62 = (pred[4,128]{1,0:T(4,128)(4,1)}, pred[4,128]{1,0:T(4,128)(4,1)S(1)}, u32[]{:S(2)}) copy-start(pred[4,128]{1,0:T(4,128)(4,1)S(1)} %iota_compare_fusion) | copy-start | bytes 1540
  173.0 628.4 %copy-start.40 = (f32[1024]{0:T(1024)}, f32[1024]{0:T(1024)S(1)}, u32[]{:S(2)}) copy-start(f32[1024]{0:T(1024)S(1)} %convert_element_type.235) | copy-start | bytes 12292
  173.0 326.8 %copy-start.54 = (f32[1024]{0:T(1024)}, f32[1024]{0:T(1024)S(1)}, u32[]{:S(2)}) copy-start(f32[1024]{0:T(1024)S(1)} %convert_element_type.226) | copy-start | bytes 12292
  173.0 326.7 %copy-start.69 = (f32[1024]{0:T(1024)}, f32[1024]{0:T(1024)S(1)}, u32[]{:S(2)}) copy-start(f32[1024]{0:T(1024)S(1)} %convert_element_type.227) | copy-start | bytes 12292
  173.0 464.0 %copy-start.67 = (f32[1024]{0:T(1024)}, f32[1024]{0:T(1024)S(1)}, u32[]{:S(2)}) copy-start(f32[1024]{0:T(1024)S(1)} %convert_element_type.236) | copy-start | bytes 12292
  239.5 476.6 %copy-start.60 = (f32[32,1,128]{2,1,0:T(1,128)}, f32[32,1,128]{2,1,0:T(1,128)S(1)}, u32[]{:S(2)}) copy-start(f32[32,1,128]{2,1,0:T(1,128)S(1)} %convert_element_type.273) | copy-start | bytes 49156
  474.7 10.3 copy-start.1
  485.0 14.7 copy-start.72
  485.0 14.7 copy-start.46
  487.6 18.8 copy-start.57
  514.7 43.2 %copy-start.71 = (f32[1024]{0:T(1024)S(1)}, f32[1024]{0:T(1024)}, u32[]{:S(2)}) copy-start(f32[1024]{0:T(1024)} %convert_element_type.234) | copy-start | bytes 12292
  517.3 46.1 %copy-start.90 = (bf16[4,16,64,256]{3,2,1,0:T(8,128)(2,1)}, bf16[4,16,64,256]{3,2,1,0:T(8,128)(2,1)S(1)}, u32[]{:S(2)}) copy-start(bf16[4,16,64,256]{3,2,1,0:T(8,128)(2,1)S(1)} %convolution_convert_fusion) | copy-start | bytes 6291460
  563.4 238.0 %copy-start.36 = (f32[4,256]{1,0:T(4,128)}, f32[4,256]{1,0:T(4,128)S(1)}, u32[]{:S(2)}) copy-start(f32[4,256]{1,0:T(4,128)S(1)} %broadcast_multiply_fusion.6) | copy-start | bytes 12292
  566.0 235.4 %copy-start.42 = (f32[4,256]{1,0:T(4,128)}, f32[4,256]{1,0:T(4,128)S(1)}, u32[]{:S(2)}) copy-start(f32[4,256]{1,0:T(4,128)S(1)} %add_rsqrt_fusion) | copy-start | bytes 12292
  566.0 150.2 %copy-start.25 = (bf16[4,256,1024]{2,1,0:T(8,128)(2,1)S(1)}, bf16[4,256,1024]{2,1,0:T(8,128)(2,1)}, u32[]{:S(2)}) copy-start(bf16[4,256,1024]{2,1,0:T(8,128)(2,1)} %param.34) | copy-start | bytes 6291460
  740.8 16.4 copy-start.10
  783.8 327.9 %reduce-scatter.16.cloned.1.call-start = ((), (), s32[]{:S(2)}) async-start(), calls=%async_computation.23 | async-start | bytes 10485760 | tf_op jit(solution)/shard_map/reduce_scatter | solution.py:350
  1026.6 174.4 %reduce-scatter.14.cloned.1.call-start = ((), (), s32[]{:S(2)}) async-start(), calls=%async_computation.22 | async-start | bytes 10485760 | tf_op jit(solution)/shard_map/reduce_scatter | solution.py:347
  1078.4 158.8 %reduce-scatter.18.cloned.1.call-start = ((), (), s32[]{:S(2)}) async-start(), calls=%async_computation.24 | async-start | bytes 1310720 | tf_op jit(solution)/shard_map/reduce_scatter | solution.py:309
  1089.5 111.5 %copy-start.14 = (bf16[4,256,1024]{2,1,0:T(8,128)(2,1)S(1)}, bf16[4,256,1024]{2,1,0:T(8,128)(2,1)}, u32[]{:S(2)}) copy-start(bf16[4,256,1024]{2,1,0:T(8,128)(2,1)} %param.31) | copy-start | bytes 6291460
  1089.5 111.5 %copy-start.39 = (f32[4,256]{1,0:T(4,128)S(1)}, f32[4,256]{1,0:T(4,128)}, u32[]{:S(2)}) copy-start(f32[4,256]{1,0:T(4,128)} %copy-done.38) | copy-start | bytes 12292
  1089.5 111.5 %copy-start.51 = (f32[4,256]{1,0:T(4,128)S(1)}, f32[4,256]{1,0:T(4,128)}, u32[]{:S(2)}) copy-start(f32[4,256]{1,0:T(4,128)} %copy-done.50) | copy-start | bytes 12292
  1089.5 111.5 %copy-start.53 = (f32[1024]{0:T(1024)S(1)}, f32[1024]{0:T(1024)}, u32[]{:S(2)}) copy-start(f32[1024]{0:T(1024)} %copy-done.52) | copy-start | bytes 12292
  1093.8 270.2 %all-reduce.27.cloned.1.call-start = ((), (), s32[]{:S(2)}) async-start(), calls=%async_computation.33 | async-start | bytes 139264
  1214.6 296.6 %reduce-scatter.28.cloned.1.call-start = ((), (), s32[]{:S(2)}) async-start(), calls=%async_computation.29 | async-start | bytes 4325376 | tf_op jit(solution)/shard_map/reduce_scatter | solution.py:335
  1221.5 431.5 %reduce-scatter.26.cloned.1.call-start = ((), (), s32[]{:S(2)}) async-start(), calls=%async_computation.28 | async-start | bytes 4325376 | tf_op jit(solution)/shard_map/reduce_scatter | solution.py:332
  1229.7 565.5 %reduce-scatter.24.cloned.1.call-start = ((), (), s32[]{:S(2)}) async-start(), calls=%async_computation.27 | async-start | bytes 4325376 | tf_op jit(solution)/shard_map/reduce_scatter | solution.py:373
  1237.1 742.8 %reduce-scatter.34.cloned.1.call-start = ((), (), s32[]{:S(2)}) async-start(), calls=%async_computation.32 | async-start | bytes 8650752
  1252.0 1089.6 %reduce-scatter.32.cloned.1.call-start = ((), (), s32[]{:S(2)}) async-start(), calls=%async_computation.31 | async-start | bytes 17301504 | tf_op jit(solution)/shard_map/reduce_scatter | solution.py:294
  1272.9 1430.7 %reduce-scatter.30.cloned.1.call-start = ((), (), s32[]{:S(2)}) async-start(), calls=%async_computation.30 | async-start | bytes 17301504 | tf_op jit(solution)/shard_map/reduce_scatter | solution.py:292
  1290.0 1578.1 %reduce-scatter.22.cloned.1.call-start = ((), (), s32[]{:S(2)}) async-start(), calls=%async_computation.26 | async-start | bytes 12976128 | tf_op jit(solution)/shard_map/reduce_scatter | solution.py:371
  1305.7 18.7 copy-start.12
  1305.7 21.0 copy-start.28
  (78 other events, 220.9 us)
Sparse Core Ops, SparseCore 0:
  11.0 64.7 all-gather.20
  78.7 68.2 all-gather.12
  149.5 25.1 all-gather.26
  176.9 26.6 all-gather.22
  205.3 87.6 all-gather.16
  294.6 87.6 all-gather.14
  385.2 56.3 all-gather.18
  444.5 55.2 all-gather.24
  502.6 55.2 all-gather.28
  560.6 76.3 all-gather.30
  640.0 76.1 all-gather.32
  783.9 26.2 reduce-scatter.19
  1026.7 84.9 reduce-scatter.15
  1114.6 86.3 reduce-scatter.13
  1204.0 27.7 reduce-scatter.17
  1238.0 125.9 all-reduce.26
  1366.8 144.3 reduce-scatter.27
  1514.0 138.8 reduce-scatter.25
  1655.9 139.2 reduce-scatter.23
  1798.0 181.9 reduce-scatter.33
  1982.9 358.5 reduce-scatter.31
  2344.5 359.0 reduce-scatter.29
  2711.2 156.8 reduce-scatter.21
where the time goes:
time: 2890 us; the launch traced here: 2870 us
  waiting for transfers between devices  1990 us (69%)
  matrix products  428 us (15%)
  local copies, waits for them, and re-layouts  253 us (9%)
  blocking collectives  106 us (4%)
  other arithmetic  75.5 us (3%)
    reduce_scatter x1, waiting for transfers between devices, per_device(): lax.psum_scatter(w_in_grad, ('dp', 'seq'), scatter_dimension=0, tiled=True)  362 us
    reduce_scatter x1, waiting for transfers between devices, per_device(): lax.psum_scatter(w_out_grad, ('dp', 'seq'), scatter_dimension=0, tiled=True)  362 us
    unnamed x25, waiting for transfers between devices  224 us
    reduce_scatter x1, waiting for transfers between devices, per_device(): lax.psum_scatter(self_qkv_term, ('dp', 'seq'), scatter_dimension=0, tiled...  165 us
    reduce_scatter x1, waiting for transfers between devices, per_device(): lax.psum_scatter(self_out_term, ('dp', 'seq'), scatter_dimension=0, tiled...  142 us
    reduce_scatter x1, waiting for transfers between devices, per_device(): lax.psum_scatter(cross_query_term, ('dp', 'seq'), scatter_dimension=0, ti...  142 us
    reduce_scatter x1, waiting for transfers between devices, per_device(): lax.psum_scatter(cross_out_term, ('dp', 'seq'), scatter_dimension=0, tile...  132 us
    reduce_scatter x1, waiting for transfers between devices, per_device(): lax.psum_scatter(grad_key_all.astype(jnp.bfloat16), 'seq', scatter_dimens...  86.8 us
  transfers between devices with their start and end apart: 23, of which 18 were waited for; matrix products, arithmetic and copies ran while one was open for 23% of the time, Pallas kernels for 0%

commit v1 on v0

--- a/solution.py
+++ b/solution.py
@@ -1,6 +1,10 @@
+import functools
+
 import jax
 import jax.numpy as jnp
 from jax import lax
+from jax.experimental import pallas as pl
+from jax.experimental.pallas import tpu as pltpu
 from jax.sharding import PartitionSpec as P
 
 D = 1024
@@ -11,6 +15,7 @@
 EPSILON = 1e-05
 SCALING = 0.125
 NEGATIVE = -1e30
+VMEM = 48 * 1024 * 1024
 
 
 def layer_norm(values, gain, shift):
@@ -399,6 +404,425 @@
     )
 
 
+LOG2E = 1.4426950408889634
+LN2 = 0.6931471805599453
+QB = 256
+PAIR = 2 * HEAD_DIM
+NT = (((1,), (1,)), ((), ()))
+NN = (((1,), (0,)), ((), ()))
+TN = (((0,), (0,)), ((), ()))
+
+
+def mm(left, right, dims=NN):
+    return lax.dot_general(left, right, dims, preferred_element_type=jnp.float32)
+
+
+def head_lanes(rows, head):
+    lane = lax.broadcasted_iota(jnp.int32, rows.shape, 1)
+    keep = (lane < HEAD_DIM) if head == 0 else (lane >= HEAD_DIM)
+    return jnp.where(keep, rows, jnp.zeros_like(rows))
+
+
+def attend_kernel(causal, len_ref, q_ref, k_ref, v_ref, o_ref, lse_ref, vx_ref):
+    keys = k_ref.shape[0]
+    length = q_ref.shape[0]
+    block = min(QB, length)
+    vx_ref[:, :PAIR] = v_ref[...]
+    vx_ref[:, PAIR:] = jnp.ones((keys, PAIR), jnp.bfloat16)
+    for start in range(0, length, block):
+        limit = start + block if causal else keys
+        rows = q_ref[start : start + block, :]
+        both = []
+        for head in range(2):
+            scores = mm(head_lanes(rows, head), k_ref[:limit, :], NT)
+            col = lax.broadcasted_iota(jnp.int32, scores.shape, 1)
+            if causal:
+                row = lax.broadcasted_iota(jnp.int32, scores.shape, 0) + start
+                scores = jnp.where(col <= row, scores, NEGATIVE)
+            else:
+                scores = jnp.where(col < len_ref[0], scores, NEGATIVE)
+            top = jnp.max(scores, axis=1, keepdims=True)
+            weights = jnp.exp2(scores - top).astype(jnp.bfloat16)
+            total = mm(weights, vx_ref[:limit, :])
+            both.append(total[:, :PAIR] / total[:, PAIR:])
+            stat = (top + jnp.log2(total[:, PAIR:])).T
+            lse_ref[0, head : head + 1, start : start + block] = stat[:1, :]
+        lane = lax.broadcasted_iota(jnp.int32, both[0].shape, 1)
+        merged = jnp.where(lane < HEAD_DIM, both[0], both[1])
+        o_ref[start : start + block, :] = merged.astype(jnp.bfloat16)
+
+
+def attend_back_kernel(
+    causal, len_ref, q_ref, k_ref, v_ref, o_ref, do_ref, lse_ref, dq_ref, dk_ref, dv_ref, acc_ref
+):
+    keys = k_ref.shape[0]
+    length = q_ref.shape[0]
+    block = min(QB, keys)
+    product = (do_ref[...].astype(jnp.float32) * o_ref[...].astype(jnp.float32)).T
+    acc_ref[...] = jnp.zeros_like(acc_ref)
+    delta = [
+        jnp.sum(product[head * HEAD_DIM : (head + 1) * HEAD_DIM, :], axis=0, keepdims=True)
+        for head in range(2)
+    ]
+    for start in range(0, keys, block):
+        first = start if causal else 0
+        key_rows = k_ref[start : start + block, :]
+        value_rows = v_ref[start : start + block, :]
+        grad_keys = grad_values = None
+        for head in range(2):
+            queries = head_lanes(q_ref[first:, :], head)
+            grads = head_lanes(do_ref[first:, :], head)
+            scores = mm(key_rows, queries, NT)
+            probs = jnp.exp2(scores - lse_ref[0, head : head + 1, first:])
+            row = lax.broadcasted_iota(jnp.int32, scores.shape, 0)
+            if causal:
+                col = lax.broadcasted_iota(jnp.int32, scores.shape, 1)
+                probs = jnp.where(row <= col, probs, 0.0)
+            else:
+                probs = jnp.where(row + start < len_ref[0], probs, 0.0)
+            back = mm(value_rows, grads, NT)
+            scored = (probs * (back - delta[head][:, first:])).astype(jnp.bfloat16)
+            term_v = mm(probs.astype(jnp.bfloat16), grads)
+            term_k = mm(scored, queries)
+            grad_values = term_v if grad_values is None else grad_values + term_v
+            grad_keys = term_k if grad_keys is None else grad_keys + term_k
+            acc_ref[first:, :] += mm(scored, head_lanes(key_rows, head), TN)
+        dk_ref[start : start + block, :] = (grad_keys * LN2).astype(jnp.bfloat16)
+        dv_ref[start : start + block, :] = grad_values.astype(jnp.bfloat16)
+    dq_ref[...] = (acc_ref[...] * SCALING).astype(jnp.bfloat16)
+
+
+def flash(lengths, query, keys, values, offsets, causal):
+    length, count = (query.shape[0], keys.shape[0])
+    pairs = HEADS // 2
+
+    def columns(rows, offset):
+        return pl.BlockSpec((rows, PAIR), lambda i, *_: (0, i + offset))
+
+    area = length * count * HEADS // (2 if causal else 1)
+    return pl.pallas_call(
+        functools.partial(attend_kernel, causal),
+        grid_spec=pltpu.PrefetchScalarGridSpec(
+            num_scalar_prefetch=1,
+            grid=(pairs,),
+            in_specs=[
+                columns(length, offsets[0]),
+                columns(count, offsets[1]),
+                columns(count, offsets[2]),
+            ],
+            out_specs=[
+                columns(length, 0),
+                pl.BlockSpec((1, 2, length), lambda i, *_: (i, 0, 0)),
+            ],
+            scratch_shapes=[pltpu.VMEM((count, 2 * PAIR), jnp.bfloat16)],
+        ),
+        out_shape=[
+            jax.ShapeDtypeStruct((length, D), jnp.bfloat16),
+            jax.ShapeDtypeStruct((pairs, 2, length), jnp.float32),
+        ],
+        compiler_params=pltpu.CompilerParams(vmem_limit_bytes=VMEM),
+        cost_estimate=pl.CostEstimate(
+            flops=area * 1024, bytes_accessed=8 * length * D, transcendentals=area
+        ),
+        name="attend",
+    )(lengths, query, keys, values)
+
+
+def flash_back(lengths, query, keys, values, offsets, out, grad, lse, causal):
+    length, count = (query.shape[0], keys.shape[0])
+    pairs = HEADS // 2
+
+    def columns(rows, offset):
+        return pl.BlockSpec((rows, PAIR), lambda i, *_: (0, i + offset))
+
+    area = length * count * HEADS // (2 if causal else 1)
+    return pl.pallas_call(
+        functools.partial(attend_back_kernel, causal),
+        grid_spec=pltpu.PrefetchScalarGridSpec(
+            num_scalar_prefetch=1,
+            grid=(pairs,),
+            in_specs=[
+                columns(length, offsets[0]),
+                columns(count, offsets[1]),
+                columns(count, offsets[2]),
+                columns(length, 0),
+                columns(length, 0),
+                pl.BlockSpec((1, 2, length), lambda i, *_: (i, 0, 0)),
+            ],
+            out_specs=[columns(length, 0), columns(count, 0), columns(count, 0)],
+            scratch_shapes=[pltpu.VMEM((length, PAIR), jnp.float32)],
+        ),
+        out_shape=[
+            jax.ShapeDtypeStruct((length, D), jnp.bfloat16),
+            jax.ShapeDtypeStruct((count, D), jnp.bfloat16),
+            jax.ShapeDtypeStruct((count, D), jnp.bfloat16),
+        ],
+        compiler_params=pltpu.CompilerParams(vmem_limit_bytes=VMEM),
+        cost_estimate=pl.CostEstimate(
+            flops=area * 2560, bytes_accessed=14 * length * D, transcendentals=area
+        ),
+        name="attend_back",
+    )(lengths, query, keys, values, out, grad, lse)
+
+
+def gelu_pair(values):
+    root = 0.7978845608028654
+    square = values * values
+    bend = jnp.tanh(root * values * (1.0 + 0.044715 * square))
+    half = 0.5 * (1.0 + bend)
+    slope = half + 0.5 * values * (1.0 - bend * bend) * root * (1.0 + 0.134145 * square)
+    return (values * half, slope)
+
+
+def norm_rows(rows, gain, shift):
+    center = rows - jnp.mean(rows, axis=-1, keepdims=True)
+    inverse = lax.rsqrt(jnp.mean(center * center, axis=-1, keepdims=True) + EPSILON)
+    normed = center * inverse
+    return ((normed * gain + shift).astype(jnp.bfloat16), normed, inverse)
+
+
+def norm_rows_back(grad_rows, normed, inverse, gain):
+    scaled = grad_rows * gain
+    back = inverse * (
+        scaled
+        - jnp.mean(scaled, axis=-1, keepdims=True)
+        - normed * jnp.mean(scaled * normed, axis=-1, keepdims=True)
+    )
+    return (back, jnp.sum(grad_rows * normed, axis=0), jnp.sum(grad_rows, axis=0))
+
+
+def total_of(*terms):
+    total = terms[0].astype(jnp.float32)
+    for term in terms[1:]:
+        total = total + term.astype(jnp.float32)
+    return total
+
+
+def pick(array, index, axis):
+    return lax.dynamic_index_in_dim(array, index, axis, keepdims=False)
+
+
+class Ring:
+    def __init__(self, n_dp, n_seq):
+        dp, seq = (lax.axis_index("dp"), lax.axis_index("seq"))
+        self.count = n_dp * n_seq
+        self.seq = seq
+        self.index = dp * n_seq + seq
+        self.x, self.y, self.c, self.z = (seq % 2, seq // 2, dp % 2, dp // 2)
+
+    def swap(self, array, bits):
+        return lax.ppermute(array, ("dp", "seq"), [(i, i ^ bits) for i in range(self.count)])
+
+    def spread_sum(self, grads):
+        widths = [grad.shape[-1] for grad in grads]
+        per = grads[0].shape[0] // self.count
+        views = [grad.reshape(4, 2, 2, 2, per, grad.shape[-1]) for grad in grads]
+
+        def joined(parts):
+            return parts[0] if len(parts) == 1 else jnp.concatenate(parts, axis=-1)
+
+        sent = joined([pick(view, 1 - self.c, 1).astype(jnp.bfloat16) for view in views])
+        kept = joined([pick(view, self.c, 1).astype(jnp.bfloat16) for view in views])
+        got = self.swap(sent, 4)
+        half = sum(widths) // 2
+        halves = []
+        for side, (axis, bit, other_bit) in enumerate(((1, 2, 1), (2, 1, 2))):
+            cut = slice(side * half, (side + 1) * half)
+            here, there = (self.y, self.x) if side == 0 else (self.x, self.y)
+            mine, came = (kept[..., cut], got[..., cut])
+            out = total_of(pick(mine, 1 - here, axis), pick(came, 1 - here, axis))
+            back = self.swap(out.astype(jnp.bfloat16), bit)
+            mine, came = (pick(mine, here, axis), pick(came, here, axis))
+            out = total_of(*(pick(part, 1 - there, 1) for part in (mine, came, back)))
+            last = self.swap(out.astype(jnp.bfloat16), other_bit)
+            halves.append(
+                [*(pick(part, there, 1) for part in (mine, came, back)), last]
+            )
+        result = [total_of(*(pick(part, self.z, 0) for part in parts)) for parts in halves]
+        result = jnp.concatenate(result, axis=-1)
+        for step in (1, 2, 3):
+            out = jnp.concatenate(
+                [total_of(*(pick(p, self.z ^ step, 0) for p in parts)).astype(jnp.bfloat16) for parts in halves],
+                axis=-1,
+            )
+            result = result + self.swap(out, 8 * step).astype(jnp.float32)
+        ends = [sum(widths[: i + 1]) for i in range(len(widths))]
+        return [result[:, end - width : end] for end, width in zip(ends, widths)]
+
+
+def whole_images(n_dp, n_seq, *args):
+    (
+        image_tokens,
+        text_states,
+        text_lengths,
+        out_grad,
+        norm1_gain,
+        norm1_bias,
+        self_qkv,
+        self_bias_qv,
+        self_out,
+        self_out_bias,
+        norm2_gain,
+        norm2_bias,
+        cross_query,
+        cross_kv,
+        cross_bias_qv,
+        cross_out,
+        cross_out_bias,
+        norm3_gain,
+        norm3_bias,
+        mlp_in,
+        mlp_in_bias,
+        mlp_out,
+        mlp_out_bias,
+    ) = args
+    f32, bf16 = (jnp.float32, jnp.bfloat16)
+    axes = ("dp", "seq")
+    ring = Ring(n_dp, n_seq)
+    images, part, _ = image_tokens.shape
+    text_part = text_states.shape[1]
+    rows = norm1_gain.shape[0]
+    length, prompt = (part * n_seq, text_part * n_seq)
+
+    def gather(shard):
+        return lax.all_gather(shard, axes, axis=0, tiled=True)
+
+    vectors = [
+        norm1_gain, norm1_bias, self_out_bias, norm2_gain, norm2_bias, cross_out_bias,
+        norm3_gain, norm3_bias, mlp_out_bias, self_bias_qv, cross_bias_qv, mlp_in_bias,
+    ]
+    strip = jnp.concatenate([v.reshape(-1, rows) for v in vectors], axis=0).T
+    strip = jnp.pad(strip, ((0, 0), (0, 128 - strip.shape[1])))
+    moved = lax.all_to_all(
+        jnp.concatenate([image_tokens, text_states], axis=1), "seq", 0, 0, tiled=True
+    )
+    first = gather(jnp.concatenate([self_qkv, strip], axis=1))
+    second = gather(jnp.concatenate([self_out, cross_query, cross_kv, cross_out], axis=1))
+    w_in, w_out = (gather(mlp_in), gather(mlp_out))
+    grad_rows = lax.all_to_all(out_grad, "seq", 0, 0, tiled=True).reshape(length, D)
+
+    table = first[:, 3 * D :].T.astype(f32)
+    full, at = ([], 0)
+    for v in vectors:
+        wide = v.shape[0] // rows
+        full.append(
+            table[at : at + wide].reshape(wide, -1, rows).transpose(1, 0, 2).reshape(-1)
+        )
+        at += wide
+    (g1, b1, bias_out, g2, b2, bias_cross, g3, b3, bias_last, bias_qv, bias_qv2, bias_in) = full
+    w_qkv = first[:, : 3 * D]
+    w_self, w_query, w_kv, w_cross = (
+        second[:, :D],
+        second[:, D : 2 * D],
+        second[:, 2 * D : 4 * D],
+        second[:, 4 * D :],
+    )
+
+    tokens = moved[:, :part].reshape(length, D)
+    texts = moved[:, part:].reshape(prompt, D)
+    prompt_length = lax.dynamic_slice_in_dim(text_lengths, ring.seq, 1, 0)
+
+    residual = tokens.astype(f32)
+    h1, n1, r1 = norm_rows(residual, g1, b1)
+    scale = jnp.concatenate([jnp.full((D,), SCALING * LOG2E, f32), jnp.ones((2 * D,), f32)])
+    shift = jnp.concatenate([bias_qv[:D], jnp.zeros((D,), f32), bias_qv[D:]])
+    qkv = ((mm(h1, w_qkv) + shift) * scale).astype(bf16)
+    o1, lse1 = flash(prompt_length, qkv, qkv, qkv, (0, 8, 16), True)
+    x1 = residual + mm(o1, w_self) + bias_out
+    h2, n2, r2 = norm_rows(x1, g2, b2)
+    q2 = ((mm(h2, w_query) + bias_qv2[:D]) * (SCALING * LOG2E)).astype(bf16)
+    shift2 = jnp.concatenate([jnp.zeros((D,), f32), bias_qv2[D:]])
+    kv2 = (mm(texts, w_kv) + shift2).astype(bf16)
+    o2, lse2 = flash(prompt_length, q2, kv2, kv2, (0, 0, 8), False)
+    x2 = x1 + mm(o2, w_cross) + bias_cross
+    h3, n3, r3 = norm_rows(x2, g3, b3)
+    act, slope = gelu_pair(mm(h3, w_in) + bias_in)
+    act, slope = (act.astype(bf16), slope.astype(bf16))
+    out = (x2 + mm(act, w_out) + bias_last).astype(bf16)
+    block_output = lax.all_to_all(out.reshape(n_seq, part, D), "seq", 0, 0, tiled=True)
+
+    w_out_grad = mm(act, grad_rows, TN)
+    du = (mm(grad_rows, w_out, NT) * slope.astype(f32)).astype(bf16)
+    (mlp_out_grad,) = ring.spread_sum([w_out_grad])
+    (mlp_in_grad,) = ring.spread_sum([mm(h3, du, TN)])
+    top = grad_rows.astype(f32)
+    back3, g3_grad, b3_grad = norm_rows_back(mm(du, w_in, NT), n3, r3, g3)
+    dx2 = top + back3
+    dc = dx2.astype(bf16)
+    do2 = mm(dc, w_cross, NT).astype(bf16)
+    dq2, dk2, dv2 = flash_back(prompt_length, q2, kv2, kv2, (0, 0, 8), o2, do2, lse2, False)
+    dkv2 = jnp.concatenate([dk2, dv2], axis=1)
+    text_grad = mm(dkv2, w_kv, NT)
+    back2, g2_grad, b2_grad = norm_rows_back(mm(dq2, w_query, NT), n2, r2, g2)
+    dx1 = dx2 + back2
+    da = dx1.astype(bf16)
+    do1 = mm(da, w_self, NT).astype(bf16)
+    cross_out_grad, cross_query_grad, cross_kv_grad, self_out_grad = ring.spread_sum(
+        [mm(o2, dc, TN), mm(h2, dq2, TN), mm(texts, dkv2, TN), mm(o1, da, TN)]
+    )
+    dq1, dk1, dv1 = flash_back(prompt_length, qkv, qkv, qkv, (0, 8, 16), o1, do1, lse1, True)
+    dqkv = jnp.concatenate([dq1, dk1, dv1], axis=1)
+    (self_qkv_grad,) = ring.spread_sum([mm(h1, dqkv, TN)])
+    back1, g1_grad, b1_grad = norm_rows_back(mm(dqkv, w_qkv, NT), n1, r1, g1)
+    image_grad = (dx1 + back1).astype(bf16)
+    leaving = jnp.concatenate(
+        [image_grad.reshape(n_seq, part, D), text_grad.astype(bf16).reshape(n_seq, text_part, D)],
+        axis=1,
+    )
+    leaving = lax.all_to_all(leaving, "seq", 0, 0, tiled=True).astype(f32)
+
+    def columns(array):
+        return jnp.sum(array.astype(f32), axis=0)
+
+    small = [
+        g1_grad, b1_grad, columns(da), g2_grad, b2_grad, columns(dc), g3_grad, b3_grad,
+        columns(grad_rows), jnp.concatenate([columns(dq1), columns(dv1)]),
+        jnp.concatenate([columns(dq2), columns(dv2)]), columns(du),
+    ]
+    sums = lax.psum(jnp.concatenate(small), axes)
+    mine, at = ([], 0)
+    for v in small:
+        wide = v.shape[0] // ring.count
+        mine.append(lax.dynamic_slice_in_dim(sums, at + ring.index * wide, wide, 0))
+        at += v.shape[0]
+    return (
+        block_output,
+        leaving[:, :part],
+        leaving[:, part:],
+        mine[0],
+        mine[1],
+        self_qkv_grad,
+        mine[9],
+        self_out_grad,
+        mine[2],
+        mine[3],
+        mine[4],
+        cross_query_grad,
+        cross_kv_grad,
+        mine[10],
+        cross_out_grad,
+        mine[5],
+        mine[6],
+        mine[7],
+        mlp_in_grad,
+        mine[11],
+        mlp_out_grad,
+        mine[8],
+    )
+
+
+def plan_of(mesh):
+    n_dp, n_seq = (mesh.shape["dp"], mesh.shape["seq"])
+
+    def layer(*args):
+        images = args[0].shape[0]
+        if images == n_seq and (n_dp, n_seq) == (8, 4):
+            return whole_images(n_dp, n_seq, *args)
+        return per_device(*args)
+
+    return layer
+
+
 def solution(mesh):
     placed = (
         P("dp", "seq", None),
@@ -426,7 +850,7 @@
         P(("dp", "seq")),
     )
     return jax.shard_map(
-        per_device,
+        plan_of(mesh),
         mesh=mesh,
         in_specs=placed,
         out_specs=(

time: 2890 us -> 877 us (0.30)
  waiting for transfers between devices: 1990 us -> 369 us
  matrix products: 428 us -> 189 us
  local copies, waits for them, and re-layouts: 253 us -> 91.2 us
  blocking collectives: 106 us -> 0 us
  Pallas kernels: 0 us -> 86 us
  starting transfers between devices: 1.51 us -> 58.6 us
    reduce_scatter x10 -> x0, waiting for transfers between devices: 1410 us -> none  [the longest x1 362 us: per_device(): lax.psum_scatter(w_in_grad, ('dp', 'seq'), scatter_dimension=0, tiled=True)]
    dot_general x99 -> x21, matrix products: 428 us -> 189 us  [mm(): lax.dot_general(left, right, dims, preferred_element_type=jnp.float32)]
    unnamed x25 -> x5, waiting for transfers between devices: 224 us -> 1.25 us
    all_gather x11 -> x4, waiting for transfers between devices: 356 us -> 155 us  [gather(): return lax.all_gather(shard, axes, axis=0, tiled=True)]
    ppermute x0 -> x32, waiting for transfers between devices: none -> 119 us  [swap(): lax.ppermute(array, ('dp', 'seq'), [(i, i ^ bits) for i in range(self.cou...]
    convert_element_type x11 -> x7, local copies, waits for them, and re-layouts: 104 us -> 14.8 us  [the longest x5 14.1 us: spread_sum(): pick(view, self.c, 1).astype(jnp.bfloat16)]
    pallas_call x0 -> x4, Pallas kernels: none -> 86 us  [the longest x2 49.3 us: flash_back(): pl.pallas_call(functools.partial(attend_back_kernel, causal), grid_spec=p...]
    all_gather x1 -> x0, blocking collectives: 65.8 us -> none  [gather_mlp(): lax.all_gather(bias_in, ('dp', 'seq'), axis=0, tiled=True)]
  transfers between devices with their start and end apart: 23 -> 41, of which waited for: 18 -> 20; matrix products, arithmetic and copies ran while one was open for 23% -> 24% of each run, Pallas kernels for 0% -> 4%
where the time goes in v1:
time: 877 us; the launch traced here: 866 us
  waiting for transfers between devices  369 us (42%)
  matrix products  189 us (22%)
  local copies, waits for them, and re-layouts  91.2 us (10%)
  Pallas kernels  86 us (10%)
  starting transfers between devices  58.6 us (7%)
  other arithmetic  57.4 us (7%)
  between operations  15.4 us (2%)
    dot_general x21, matrix products, mm(): lax.dot_general(left, right, dims, preferred_element_type=jnp.float32)  189 us
    all_gather x4, waiting for transfers between devices, gather(): return lax.all_gather(shard, axes, axis=0, tiled=True)  155 us
    ppermute x32, waiting for transfers between devices, swap(): lax.ppermute(array, ('dp', 'seq'), [(i, i ^ bits) for i in range(self.cou...  119 us
    pallas_call x2, Pallas kernels, flash_back(): pl.pallas_call(functools.partial(attend_back_kernel, causal), grid_spec=p...  49.3 us
    ppermute x32, starting transfers between devices, swap(): lax.ppermute(array, ('dp', 'seq'), [(i, i ^ bits) for i in range(self.cou...  40.4 us
    all_to_all x1, waiting for transfers between devices, whole_images(): lax.all_to_all(jnp.concatenate([image_tokens, text_states], axis=1), 'seq...  37.8 us
    pallas_call x2, Pallas kernels, flash(): pl.pallas_call(functools.partial(attend_kernel, causal), grid_spec=pltpu....  36.7 us
    psum x1, waiting for transfers between devices, whole_images(): sums = lax.psum(jnp.concatenate(small), axes)  32.4 us
  transfers between devices with their start and end apart: 41, of which 20 were waited for; matrix products, arithmetic and copies ran while one was open for 24% of the time, Pallas kernels for 4%

profile of v1, /device:TPU:0, one launch (start us, length us, event | category | flops | bytes accessed | tf_op | source)
XLA Modules:
  0.0 866.2 jit_solution(4630563530683018573)
XLA Ops:
  15.9 5.2 all-to-all-start.2
  21.1 3.2 pad_maximum_fusion.3
  24.3 23.1 %all-to-all-done.2 = bf16[4,256,1024]{2,1,0:T(8,128)(2,1)S(1)} async-done(((bf16[4,256,1024]{2,1,0:T(8,128)(2,1)}), bf16[4,256,1024]{2,1,0:T(8,128)(2,1)S(1)}, u32[]{:S(2)}, u32[]{:S(2)}) %all-to-all-start.2) | async-done | bytes 2097184 | tf_op jit(solution)/shard_map/all_to_all | solution.py:702
  48.7 3.6 all-to-all-start
  55.6 37.8 %all-to-all-done = bf16[4,288,1024]{2,1,0:T(8,128)(2,1)S(1)} async-done(((bf16[4,288,1024]{2,1,0:T(8,128)(2,1)}), bf16[4,288,1024]{2,1,0:T(8,128)(2,1)S(1)}, u32[]{:S(2)}, u32[]{:S(2)}) %all-to-all-start) | async-done | bytes 2359328 | tf_op jit(solution)/shard_map/all_to_all | solution.py:696
  96.9 10.1 %all-gather.5.cloned.1.call-done = bf16[1024,3200]{1,0:T(8,128)(2,1)} async-done(((bf16[32,3200]{1,0:T(8,128)(2,1)}), bf16[1024,3200]{1,0:T(8,128)(2,1)}) %all-gather.5.cloned.1.call-update) | async-done | bytes 6553616 | tf_op jit(solution)/shard_map/all_gather | solution.py:688
  117.5 4.1 copy.70
  121.6 11.4 %multiply_convert_fusion.2.q_ref.k_ref.v_ref = bf16[1024,3072]{1,0:T(8,128)(2,1)} fusion(f32[3072]{0:T(1024)S(1)} %copy-done.67, f32[3072]{0:T(1024)S(1)} %pad_maximum_fusion.18, bf16[1024,1024]{1,0:T(8,128)(2,1)S(1)} %copy-done.28, bf16[1024,3200]{1,0:T(8,128)(2,1)} %all-gather.5.cloned.1.call-done), kind=kOutput, calls=%fused_computation.16 | convolution fusion | flops 6451888128 | bytes 14704640 | tf_op jit(solution)/shard_map/dot_general | solution.py:417
  133.0 24.0 %attend.2 = (bf16[1024,1024]{1,0:T(8,128)(2,1)S(1)}, f32[8,2,1024]{2,1,0:T(2,128)S(1)}) custom-call(s32[1]{0:T(128)} %dynamic_slice.646.len_ref, bf16[1024,3072]{1,0:T(8,128)(2,1)} %multiply_convert_fusion.2.q_ref.k_ref.v_ref, bf16[1024,3072]{1,0:T(8,128)(2,1)} %multiply_convert_fusion.2.q_ref.k_ref.v_ref, ...), custom_call_target="tpu_custom_call" | custom-call | flops 8589934592 | bytes 8388608 | tf_op jit(solution)/shard_map/attend/pallas_call | solution.py:503
  157.0 39.0 %all-gather.7.cloned.1.call-done = bf16[1024,5120]{1,0:T(8,128)(2,1)} async-done(((bf16[32,5120]{1,0:T(8,128)(2,1)}), bf16[1024,5120]{1,0:T(8,128)(2,1)}) %all-gather.7.cloned.1.call-update) | async-done | bytes 10485776 | tf_op jit(solution)/shard_map/all_gather | solution.py:688
  196.0 4.9 fusion.148
  202.9 2.9 multiply_convert_fusion.4.q_ref
  205.8 12.7 %attend.3 = (bf16[1024,1024]{1,0:T(8,128)(2,1)S(1)}, f32[8,2,1024]{2,1,0:T(2,128)S(1)}) custom-call(s32[1]{0:T(128)} %dynamic_slice.646.len_ref, bf16[1024,1024]{1,0:T(8,128)(2,1)S(1)} %multiply_convert_fusion.4.q_ref, bf16[128,2048]{1,0:T(8,128)(2,1)S(1)} %fusion.42.k_ref.v_ref, bf16[128,2048]{1,0:T(8,128)(2,1)S(1)} %fusion.42.k_ref.v_ref), custom_call_target="tpu_custom_call" | custom-call | flops 2147483648 | bytes 8388608 | tf_op jit(solution)/shard_map/attend/pallas_call | solution.py:503
  218.6 4.8 fusion.149
  225.9 49.1 %all-gather.9.cloned.1.call-done = bf16[1024,4096]{1,0:T(8,128)(2,1)} async-done(((bf16[32,4096]{1,0:T(8,128)(2,1)}), bf16[1024,4096]{1,0:T(8,128)(2,1)}) %all-gather.9.cloned.1.call-update) | async-done | bytes 8388624 | tf_op jit(solution)/shard_map/all_gather | solution.py:688
  275.0 21.8 %fusion.6 = (bf16[4096,1024]{0,1:T(8,128)(2,1)}, f32[1024,4096]{1,0:T(8,128)}) fusion(f32[4096]{0:T(1024)S(1)} %add.1666, bf16[1024,4096]{1,0:T(8,128)(2,1)} %all-gather.9.cloned.1.call-done, f32[1024,1024]{1,0:T(8,128)} %copy-done.20, f32[1024]{0:T(1024)S(1)} %get-tuple-element.56, f32[1024]{0:T(1024)S(1)} %get-tuple-element.54, ...), kind=kOutput, calls=%fused_computation.9 | convolution fusion | flops 8637120512 | bytes 37781504 | tf_op jit(solution)/shard_map/dot_general | solution.py:417
  296.8 57.1 %all-gather.11.cloned.1.call-done = bf16[4096,1024]{1,0:T(8,128)(2,1)} async-done(((bf16[128,1024]{1,0:T(8,128)(2,1)}), bf16[4096,1024]{1,0:T(8,128)(2,1)}) %all-gather.11.cloned.1.call-update) | async-done | bytes 8388624 | tf_op jit(solution)/shard_map/all_gather | solution.py:688
  353.9 23.1 %convert_reduce_fusion = (f32[4096]{0:T(1024)}, bf16[1024,4096]{1,0:T(8,128)(2,1)}) fusion(f32[1024,4096]{1,0:T(8,128)} %get-tuple-element.158, f32[4096]{0:T(1024)S(1)} %add.1666, bf16[1024,1024]{1,0:T(8,128)(2,1)S(1)} %bitcast.530, bf16[4096,1024]{1,0:T(8,128)(2,1)} %all-gather.11.cloned.1.call-done), kind=kOutput, calls=%fused_computation.10 | convolution fusion | flops 8686399488 | bytes 35684352 | tf_op jit(solution)/shard_map/dot_general | solution.py:417
  377.0 15.8 %multiply_reduce_fusion = (f32[1024]{0:T(1024)S(1)}, f32[1024]{0:T(1024)S(1)}, f32[1024]{0:T(1024)S(1)}, f32[1024]{0:T(1024)S(1)}, f32[1024,1024]{1,0:T(8,128)S(1)}) fusion(f32[1024,1024]{1,0:T(8,128)} %copy-done.20, f32[1024]{0:T(1024)S(1)} %add_rsqrt_fusion, f32[1024]{0:T(1024)S(1)} %broadcast_multiply_fusion.6, f32[1024]{0:T(1024)S(1)} %get-tuple-element.54, ...), kind=kOutput, calls=%fused_computation.66 | convolution fusion | flops 8599367680 | bytes 25194496 | tf_op jit(solution)/shard_map/dot_general | solution.py:417
  394.9 6.8 convolution_convert_fusion.1.do_ref
  401.7 12.9 %attend_back.2 = (bf16[1024,1024]{1,0:T(8,128)(2,1)S(1)}, bf16[128,1024]{1,0:T(8,128)(2,1)S(1)}, bf16[128,1024]{1,0:T(8,128)(2,1)S(1)}) custom-call(s32[1]{0:T(128)} %dynamic_slice.646.len_ref, bf16[1024,1024]{1,0:T(8,128)(2,1)S(1)} %copy-done.3, bf16[128,2048]{1,0:T(8,128)(2,1)S(1)} %fusion.42.k_ref.v_ref, bf16[128,2048]{1,0:T(8,128)(2,1)S(1)} %fusion.42.k_ref.v_ref, ...), custom_call_target="tpu_custom_call" | custom-call | flops 5368709120 | bytes 14680064 | tf_op jit(solution)/shard_map/attend_back/pallas_call | solution.py:539
  414.7 4.7 multiply_reduce_fusion.1
  421.3 6.8 convolution_convert_fusion.do_ref
  428.1 36.4 %attend_back.3 = (bf16[1024,1024]{1,0:T(8,128)(2,1)S(1)}, bf16[1024,1024]{1,0:T(8,128)(2,1)S(1)}, bf16[1024,1024]{1,0:T(8,128)(2,1)}) custom-call(s32[1]{0:T(128)} %dynamic_slice.646.len_ref, bf16[1024,3072]{1,0:T(8,128)(2,1)} %multiply_convert_fusion.2.q_ref.k_ref.v_ref, bf16[1024,3072]{1,0:T(8,128)(2,1)} %multiply_convert_fusion.2.q_ref.k_ref.v_ref, ...), custom_call_target="tpu_custom_call" | custom-call | flops 21474836480 | bytes 14680064 | tf_op jit(solution)/shard_map/attend_back/pallas_call | solution.py:539
  466.9 3.7 fusion.121
  470.7 4.0 fusion.134
  474.7 3.8 fusion.124
  478.5 15.1 %fusion.132 = bf16[1024,4096]{1,0:T(8,128)(2,1)} fusion(bf16[1024,4096]{1,0:T(8,128)(2,1)} %get-tuple-element.156, f32[1024,1024]{1,0:T(8,128)S(1)} %copy-done.22, f32[1024]{0:T(1024)S(1)} %get-tuple-element.56, f32[1024]{0:T(1024)S(1)} %get-tuple-element.54, f32[1024]{0:T(1024)S(1)} %add_rsqrt_fusion, f32[1024]{0:T(1024)S(1)} %broadcast_multiply_fusion.6), kind=kOutput, calls=%fused_computation.338 | convolution fusion | flops 8595177472 | bytes 20987904 | tf_op jit(solution)/shard_map/dot_general | solution.py:417
  493.6 17.6 %add_convert_fusion.1 = bf16[1024,1024]{1,0:T(8,128)(2,1)} fusion(f32[1024,1024]{1,0:T(8,128)S(1)} %copy-done.22, f32[1024]{0:T(1024)S(1)} %copy-done.63, bf16[4096,1024]{1,0:T(8,128)(2,1)} %all-gather.11.cloned.1.call-done, f32[1024,4096]{1,0:T(8,128)} %get-tuple-element.158, f32[4096]{0:T(1024)S(1)} %add.1666), kind=kOutput, calls=%fused_computation.74 | convolution fusion | flops 8635023360 | bytes 31477760 | tf_op jit(solution)/shard_map/dot_general | solution.py:417
  511.2 4.4 all-to-all-start.1
  521.9 13.1 %fusion.31 = (f32[1024]{0:T(1024)S(1)}, f32[1024]{0:T(1024)S(1)}, f32[1024]{0:T(1024)S(1)}, f32[1024]{0:T(1024)S(1)}, f32[1024,1024]{1,0:T(8,128)}) fusion(f32[1024]{0:T(1024)S(1)} %bitcast.553, f32[1024]{0:T(1024)S(1)} %bitcast.556, bf16[4,288,1024]{2,1,0:T(8,128)(2,1)S(1)} %copy-done.7, f32[1024]{0:T(1024)S(1)} %copy-done.60, ...), kind=kOutput, calls=%fused_computation.59 | convolution fusion | flops 6452932608 | bytes 18903040 | tf_op jit(solution)/shard_map/dot_general | solution.py:417
  535.8 9.7 %fusion.8 = bf16[4,2,2,2,32,3072]{5,4,3,2,1,0:T(8,128)(2,1)S(1)} fusion(bf16[4,2,2,2,32,1024]{5,4,3,2,1,0:T(8,128)(2,1)S(1)} %bitcast.540, bf16[1024,3072]{1,0:T(8,128)(2,1)} %constant_dynamic-update-slice_fusion), kind=kOutput, calls=%fused_computation.23 | convolution fusion | flops 6442450944 | bytes 14680064 | tf_op jit(solution)/shard_map/dot_general | solution.py:417
  545.5 3.3 fusion.38
  555.1 6.3 pad_maximum_fusion
  561.6 3.9 fusion.14
  565.7 12.0 %copy.95 = bf16[4096,1024]{1,0:T(8,128)(2,1)} copy(bf16[4096,1024]{0,1:T(8,128)(2,1)} %get-tuple-element.157) | data formatting | bytes 16777216 | tf_op jit(solution)/shard_map/dot_general | solution.py:417
  577.7 13.2 %fusion.150 = bf16[4,2,2,2,128,1024]{5,4,3,2,1,0:T(8,128)(2,1)S(1)} fusion(bf16[4,2,2,2,128,1024]{5,4,3,2,1,0:T(8,128)(2,1)} %bitcast.534, bf16[1024,1024,1,1,1,1]{1,0,5,4,3,2:T(8,128)(2,1)} %bitcast.529), kind=kOutput, calls=%fused_computation.356 | convolution fusion | flops 8589934592 | bytes 18874368 | tf_op jit(solution)/shard_map/dot_general | solution.py:417
  590.9 4.6 fusion.16
  595.8 3.9 fusion.59
  602.1 3.2 fusion.30
  610.9 4.7 all-to-all-start.3
  615.6 3.3 pad_maximum_fusion.1
  629.4 32.4 %all-reduce.4.cloned.1.call-done = f32[17408]{0:T(1024)} async-done(((f32[17408]{0:T(1024)}), f32[17408]{0:T(1024)}) %all-reduce.4.cloned.1.call-update) | async-done | bytes 69648 | tf_op jit(solution)/shard_map/psum | solution.py:782
  665.6 4.2 slice.223
  676.9 2.7 fusion.139
  681.8 2.9 fusion.137
  689.9 4.5 collective-permute-start.7
  696.6 3.7 collective-permute-done.7
  700.8 8.6 collective-permute-done.6
  712.2 2.9 fusion.135
  719.0 7.7 collective-permute-done.17
  728.3 7.4 collective-permute-done.27
  736.6 12.5 %collective-permute-done.25 = bf16[4,2,128,512]{3,2,1,0:T(8,128)(2,1)S(1)} collective-permute-done((bf16[4,2,128,512]{3,2,1,0:T(8,128)(2,1)}, bf16[4,2,128,512]{3,2,1,0:T(8,128)(2,1)S(1)}, u32[]{:S(2)}, u32[]{:S(2)}) %collective-permute-start.25) | collective-permute-done | bytes 1048608 | tf_op jit(solution)/shard_map/ppermute | solution.py:614
  749.8 10.6 %collective-permute-done.20 = bf16[4,32,2048]{2,1,0:T(8,128)(2,1)S(1)} collective-permute-done((bf16[4,32,2048]{2,1,0:T(8,128)(2,1)S(1)}, bf16[4,32,2048]{2,1,0:T(8,128)(2,1)S(1)}, u32[]{:S(2)}, u32[]{:S(2)}) %collective-permute-start.20) | collective-permute-done | bytes 524320 | tf_op jit(solution)/shard_map/ppermute | solution.py:614
  762.7 12.3 %collective-permute-done.18 = bf16[4,32,2048]{2,1,0:T(8,128)(2,1)S(1)} collective-permute-done((bf16[4,32,2048]{2,1,0:T(8,128)(2,1)S(1)}, bf16[4,32,2048]{2,1,0:T(8,128)(2,1)S(1)}, u32[]{:S(2)}, u32[]{:S(2)}) %collective-permute-start.18) | collective-permute-done | bytes 524320 | tf_op jit(solution)/shard_map/ppermute | solution.py:614
  778.0 17.9 %collective-permute-done.28 = bf16[4,128,512]{2,1,0:T(8,128)(2,1)S(1)} collective-permute-done((bf16[4,128,512]{2,1,0:T(8,128)(2,1)S(1)}, bf16[4,128,512]{2,1,0:T(8,128)(2,1)S(1)}, u32[]{:S(2)}, u32[]{:S(2)}) %collective-permute-start.28) | collective-permute-done | bytes 524320 | tf_op jit(solution)/shard_map/ppermute | solution.py:614
  795.9 4.6 collective-permute-start.22
  806.5 13.5 %collective-permute-done.22 = bf16[32,4096]{1,0:T(8,128)(2,1)S(1)} collective-permute-done((bf16[32,4096]{1,0:T(8,128)(2,1)S(1)}, bf16[32,4096]{1,0:T(8,128)(2,1)S(1)}, u32[]{:S(2)}, u32[]{:S(2)}) %collective-permute-start.22) | collective-permute-done | bytes 262176 | tf_op jit(solution)/shard_map/ppermute | solution.py:614
  823.9 3.8 collective-permute-done.30
  828.7 3.3 collective-permute-done.10
  832.8 4.4 collective-permute-start.13
  837.4 5.0 collective-permute-done.15
  842.4 12.4 %collective-permute-done.14 = bf16[32,5120]{1,0:T(8,128)(2,1)S(1)} collective-permute-done((bf16[32,5120]{1,0:T(8,128)(2,1)S(1)}, bf16[32,5120]{1,0:T(8,128)(2,1)S(1)}, u32[]{:S(2)}, u32[]{:S(2)}) %collective-permute-start.14) | collective-permute-done | bytes 327712 | tf_op jit(solution)/shard_map/ppermute | solution.py:614
  856.4 3.1 copy.136
  (338 shorter events, 119.3 us)
Async XLA Ops:
  7.2 13.9 %copy-start.53 = (bf16[4,32,1024]{2,1,0:T(8,128)(2,1)S(1)}, bf16[4,32,1024]{2,1,0:T(8,128)(2,1)}, u32[]{:S(2)}) copy-start(bf16[4,32,1024]{2,1,0:T(8,128)(2,1)} %param.24) | copy-start | bytes 786436
  7.2 99.8 %all-gather.5.cloned.1.call-start = ((), (), s32[]{:S(2)}) async-start(), calls=%async_computation.4 | async-start | bytes 6758400 | tf_op jit(solution)/shard_map/all_gather | solution.py:688
  12.8 183.2 %all-gather.7.cloned.1.call-start = ((), (), s32[]{:S(2)}) async-start(), calls=%async_computation.5 | async-start | bytes 10813440 | tf_op jit(solution)/shard_map/all_gather | solution.py:688
  14.6 260.4 %all-gather.9.cloned.1.call-start = ((), (), s32[]{:S(2)}) async-start(), calls=%async_computation.6 | async-start | bytes 8650752 | tf_op jit(solution)/shard_map/all_gather | solution.py:688
  15.3 338.6 %all-gather.11.cloned.1.call-start = ((), (), s32[]{:S(2)}) async-start(), calls=%async_computation.7 | async-start | bytes 8650752 | tf_op jit(solution)/shard_map/all_gather | solution.py:688
  15.9 31.5 %all-to-all-start.2 = ((bf16[4,256,1024]{2,1,0:T(8,128)(2,1)}), bf16[4,256,1024]{2,1,0:T(8,128)(2,1)S(1)}, u32[]{:S(2)}, u32[]{:S(2)}) async-start(bf16[4,256,1024]{2,1,0:T(8,128)(2,1)} %param.26), calls=%async_computation.2 | async-start | bytes 4194304 | tf_op jit(solution)/shard_map/all_to_all | solution.py:702
  21.1 31.4 %copy-start.66 = (s32[4]{0:T(128)S(1)}, s32[4]{0:T(128)}, u32[]{:S(2)}) copy-start(s32[4]{0:T(128)} %param.25) | copy-start | bytes 52
  48.7 44.7 %all-to-all-start = ((bf16[4,288,1024]{2,1,0:T(8,128)(2,1)}), bf16[4,288,1024]{2,1,0:T(8,128)(2,1)S(1)}, u32[]{:S(2)}, u32[]{:S(2)}) async-start(bf16[4,288,1024]{2,1,0:T(8,128)(2,1)} %pad_maximum_fusion.3), calls=%async_computation | async-start | bytes 4718592 | tf_op jit(solution)/shard_map/all_to_all | solution.py:696
  93.4 21.9 %copy-start.6 = (bf16[4,288,1024]{2,1,0:T(8,128)(2,1)}, bf16[4,288,1024]{2,1,0:T(8,128)(2,1)S(1)}, u32[]{:S(2)}) copy-start(bf16[4,288,1024]{2,1,0:T(8,128)(2,1)S(1)} %all-to-all-done) | copy-start | bytes 7077892
  94.5 20.8 %copy-start.55 = (f32[1,2,4,128]{3,1,2,0:T(2,128)}, f32[1,2,4,128]{3,1,2,0:T(2,128)S(1)}, u32[]{:S(2)}) copy-start(f32[1,2,4,128]{3,1,2,0:T(2,128)S(1)} %copy.117) | copy-start | bytes 12292
  94.5 20.8 %copy-start.57 = (f32[1,2,4,128]{3,1,2,0:T(2,128)}, f32[1,2,4,128]{3,1,2,0:T(2,128)S(1)}, u32[]{:S(2)}) copy-start(f32[1,2,4,128]{3,1,2,0:T(2,128)S(1)} %copy.116) | copy-start | bytes 12292
  115.3 87.6 %copy-start.64 = (f32[1024]{0:T(1024)}, f32[1024]{0:T(1024)S(1)}, u32[]{:S(2)}) copy-start(f32[1024]{0:T(1024)S(1)} %get-tuple-element.58) | copy-start | bytes 12292
  157.0 43.9 %copy-start.4 = (bf16[1024,1024]{1,0:T(8,128)(2,1)}, bf16[1024,1024]{1,0:T(8,128)(2,1)S(1)}, u32[]{:S(2)}) copy-start(bf16[1024,1024]{1,0:T(8,128)(2,1)S(1)} %get-tuple-element.32.o_ref) | copy-start | bytes 6291460
  200.9 17.6 %copy-start.13 = (f32[1024,1024]{1,0:T(8,128)}, f32[1024,1024]{1,0:T(8,128)S(1)}, u32[]{:S(2)}) copy-start(f32[1024,1024]{1,0:T(8,128)S(1)} %get-tuple-element.149) | copy-start | bytes 12582916
  205.8 17.5 %copy-start.2 = (bf16[1024,1024]{1,0:T(8,128)(2,1)}, bf16[1024,1024]{1,0:T(8,128)(2,1)S(1)}, u32[]{:S(2)}) copy-start(bf16[1024,1024]{1,0:T(8,128)(2,1)S(1)} %multiply_convert_fusion.4.q_ref) | copy-start | bytes 6291460
  275.0 78.9 %copy-start.10 = (bf16[4,256,1024]{2,1,0:T(8,128)(2,1)S(1)}, bf16[4,256,1024]{2,1,0:T(8,128)(2,1)}, u32[]{:S(2)}) copy-start(bf16[4,256,1024]{2,1,0:T(8,128)(2,1)} %copy-done.9) | copy-start | bytes 6291460
  377.0 15.8 %copy-start.21 = (f32[1024,1024]{1,0:T(8,128)S(1)}, f32[1024,1024]{1,0:T(8,128)}, u32[]{:S(2)}) copy-start(f32[1024,1024]{1,0:T(8,128)} %copy-done.20) | copy-start | bytes 12582916
  401.7 12.9 %copy-start.14 = (f32[1024,1024]{1,0:T(8,128)S(1)}, f32[1024,1024]{1,0:T(8,128)}, u32[]{:S(2)}) copy-start(f32[1024,1024]{1,0:T(8,128)} %copy-done.13) | copy-start | bytes 12582916
  421.3 45.6 %copy-start.11 = (f32[1024,1024]{1,0:T(8,128)}, f32[1024,1024]{1,0:T(8,128)S(1)}, u32[]{:S(2)}) copy-start(f32[1024,1024]{1,0:T(8,128)S(1)} %get-tuple-element.66) | copy-start | bytes 12582916
  478.5 15.1 %copy-start.63 = (f32[1024]{0:T(1024)S(1)}, f32[1024]{0:T(1024)}, u32[]{:S(2)}) copy-start(f32[1024]{0:T(1024)} %get-tuple-element.55) | copy-start | bytes 12292
  511.2 99.7 %all-to-all-start.1 = ((bf16[4,256,1024]{2,1,0:T(8,128)(2,1)}), bf16[4,256,1024]{2,1,0:T(8,128)(2,1)}, u32[]{:S(2)}, u32[]{:S(2)}) async-start(bf16[4,256,1024]{2,1,0:T(8,128)(2,1)} %bitcast.541), calls=%async_computation.1 | async-start | bytes 4194304 | tf_op jit(solution)/shard_map/all_to_all | solution.py:742
  515.7 146.1 %all-reduce.4.cloned.1.call-start = ((), (), s32[]{:S(2)}) async-start(), calls=%async_computation.8 | async-start | bytes 139264 | tf_op jit(solution)/shard_map/psum | solution.py:782
  521.8 13.2 %copy-start.61 = (f32[1024]{0:T(1024)S(1)}, f32[1024]{0:T(1024)}, u32[]{:S(2)}) copy-start(f32[1024]{0:T(1024)} %convert_reduce_fusion.5) | copy-start | bytes 12292
  521.8 13.3 %copy-start.62 = (f32[4096]{0:T(1024)S(1)}, f32[4096]{0:T(1024)}, u32[]{:S(2)}) copy-start(f32[4096]{0:T(1024)} %get-tuple-element.155) | copy-start | bytes 49156
  521.9 14.0 %copy-start.44 = (bf16[1024,1024]{1,0:T(8,128)(2,1)S(1)}, bf16[1024,1024]{1,0:T(8,128)(2,1)}, u32[]{:S(2)}) copy-start(bf16[1024,1024]{1,0:T(8,128)(2,1)} %copy.70) | copy-start | bytes 6291460
  548.8 70.1 %collective-permute-start = (bf16[4,2,2,32,3072]{4,3,2,1,0:T(8,128)(2,1)}, bf16[4,2,2,32,3072]{4,3,2,1,0:T(8,128)(2,1)}, u32[]{:S(2)}, u32[]{:S(2)}) collective-permute-start(bf16[4,2,2,32,3072]{4,3,2,1,0:T(8,128)(2,1)} %get-tuple-element.79), channel_id=1, source_target_pairs={{0,4},{1,5},{2,6},{3,7},{4,0},{5,1},{6,2},{7,3},{8,12},{9,13},{10,... | collective-permute-start | bytes 9437192 | tf_op jit(solution)/shard_map/ppermute | solution.py:614
  552.6 9.0 %slice-start = ((s8[8388608]{0:T(1024)(128)(4,1)}), s8[4194304]{0:T(1024)(128)(4,1)S(1)}, s32[]{:S(2)}) async-start(s8[8388608]{0:T(1024)(128)(4,1)} %bitcast.531), calls=%async_computation.9 | async-start | bytes 8388608
  561.3 150.8 %collective-permute-start.8 = (bf16[4,2,2,32,5120]{4,3,2,1,0:T(8,128)(2,1)}, bf16[4,2,2,32,5120]{4,3,2,1,0:T(8,128)(2,1)}, u32[]{:S(2)}, u32[]{:S(2)}) collective-permute-start(bf16[4,2,2,32,5120]{4,3,2,1,0:T(8,128)(2,1)} %pad_maximum_fusion), channel_id=1, source_target_pairs={{0,4},{1,5},{2,6},{3,7},{4,0},{5,1},{6,2},{7,3},{8,12},{9,13},{10,... | collective-permute-start | bytes 15728648 | tf_op jit(solution)/shard_map/ppermute | solution.py:614
  565.5 111.4 %collective-permute-start.16 = (bf16[4,2,2,32,4096]{4,3,2,1,0:T(8,128)(2,1)}, bf16[4,2,2,32,4096]{4,3,2,1,0:T(8,128)(2,1)}, u32[]{:S(2)}, u32[]{:S(2)}) collective-permute-start(bf16[4,2,2,32,4096]{4,3,2,1,0:T(8,128)(2,1)} %get-tuple-element.70), channel_id=1, source_target_pairs={{0,4},{1,5},{2,6},{3,7},{4,0},{5,1},{6,2},{7,3},{8,12},{9,13},{10,... | collective-permute-start | bytes 12582920 | tf_op jit(solution)/shard_map/ppermute | solution.py:614
  595.5 86.3 %collective-permute-start.24 = (bf16[4,2,2,128,1024]{4,3,2,1,0:T(8,128)(2,1)}, bf16[4,2,2,128,1024]{4,3,2,1,0:T(8,128)(2,1)}, u32[]{:S(2)}, u32[]{:S(2)}) collective-permute-start(bf16[4,2,2,128,1024]{4,3,2,1,0:T(8,128)(2,1)} %get-tuple-element.68), channel_id=1, source_target_pairs={{0,4},{1,5},{2,6},{3,7},{4,0},{5,1},{6,2},{7,3},{8,12},{9,13},{10,... | collective-permute-start | bytes 12582920 | tf_op jit(solution)/shard_map/ppermute | solution.py:614
  610.9 54.7 %all-to-all-start.3 = ((bf16[4,288,1024]{2,1,0:T(8,128)(2,1)}), bf16[4,288,1024]{2,1,0:T(8,128)(2,1)}, u32[]{:S(2)}, u32[]{:S(2)}) async-start(bf16[4,288,1024]{2,1,0:T(8,128)(2,1)} %pad_maximum_fusion.4), calls=%async_computation.3 | async-start | bytes 4718592 | tf_op jit(solution)/shard_map/all_to_all | solution.py:772
  622.3 49.3 %collective-permute-start.3 = (bf16[4,2,32,1536]{3,2,1,0:T(8,128)(2,1)}, bf16[4,2,32,1536]{3,2,1,0:T(8,128)(2,1)}, u32[]{:S(2)}, u32[]{:S(2)}) collective-permute-start(bf16[4,2,32,1536]{3,2,1,0:T(8,128)(2,1)} %fusion.77), channel_id=1, source_target_pairs={{0,1},{1,0},{2,3},{3,2},{4,5},{5,4},{6,7},{7,6},{8,9},{9,8},{10,11... | collective-permute-start | bytes 2359304 | tf_op jit(solution)/shard_map/ppermute | solution.py:614
  625.4 49.0 %collective-permute-start.1 = (bf16[4,2,32,1536]{3,2,1,0:T(8,128)(2,1)}, bf16[4,2,32,1536]{3,2,1,0:T(8,128)(2,1)}, u32[]{:S(2)}, u32[]{:S(2)}) collective-permute-start(bf16[4,2,32,1536]{3,2,1,0:T(8,128)(2,1)} %fusion.76), channel_id=1, source_target_pairs={{0,2},{1,3},{2,0},{3,1},{4,6},{5,7},{6,4},{7,5},{8,10},{9,11},{10,... | collective-permute-start | bytes 2359304 | tf_op jit(solution)/shard_map/ppermute | solution.py:614
  665.6 8.8 %copy-start.34 = (bf16[4,2,2,32,1536]{4,3,2,1,0:T(8,128)(2,1)S(1)}, bf16[4,2,2,32,1536]{4,3,2,1,0:T(8,128)(2,1)}, u32[]{:S(2)}) copy-start(bf16[4,2,2,32,1536]{4,3,2,1,0:T(8,128)(2,1)} %get-tuple-element.116) | copy-start | bytes 4718596
  665.6 8.8 %copy-start.38 = (bf16[4,2,2,32,1536]{4,3,2,1,0:T(8,128)(2,1)S(1)}, bf16[4,2,2,32,1536]{4,3,2,1,0:T(8,128)(2,1)}, u32[]{:S(2)}) copy-start(bf16[4,2,2,32,1536]{4,3,2,1,0:T(8,128)(2,1)} %copy-done.37) | copy-start | bytes 4718596
  672.9 14.5 %collective-permute-start.4 = (bf16[4,32,1536]{2,1,0:T(8,128)(2,1)S(1)}, bf16[4,32,1536]{2,1,0:T(8,128)(2,1)S(1)}, u32[]{:S(2)}, u32[]{:S(2)}) collective-permute-start(bf16[4,32,1536]{2,1,0:T(8,128)(2,1)S(1)} %fusion.78), channel_id=1, source_target_pairs={{0,2},{1,3},{2,0},{3,1},{4,6},{5,7},{6,4},{7,5},{8,10},{9,11},{10,... | collective-permute-start | bytes 1179656 | tf_op jit(solution)/shard_map/ppermute | solution.py:614
  675.6 13.1 %collective-permute-start.2 = (bf16[4,32,1536]{2,1,0:T(8,128)(2,1)S(1)}, bf16[4,32,1536]{2,1,0:T(8,128)(2,1)S(1)}, u32[]{:S(2)}, u32[]{:S(2)}) collective-permute-start(bf16[4,32,1536]{2,1,0:T(8,128)(2,1)S(1)} %fusion.79), channel_id=1, source_target_pairs={{0,1},{1,0},{2,3},{3,2},{4,5},{5,4},{6,7},{7,6},{8,9},{9,8},{10,11... | collective-permute-start | bytes 1179656 | tf_op jit(solution)/shard_map/ppermute | solution.py:614
  681.0 35.2 %collective-permute-start.19 = (bf16[4,2,32,2048]{3,2,1,0:T(8,128)(2,1)}, bf16[4,2,32,2048]{3,2,1,0:T(8,128)(2,1)}, u32[]{:S(2)}, u32[]{:S(2)}) collective-permute-start(bf16[4,2,32,2048]{3,2,1,0:T(8,128)(2,1)} %fusion.63), channel_id=1, source_target_pairs={{0,1},{1,0},{2,3},{3,2},{4,5},{5,4},{6,7},{7,6},{8,9},{9,8},{10,11... | collective-permute-start | bytes 3145736 | tf_op jit(solution)/shard_map/ppermute | solution.py:614
  686.1 9.2 %copy-start.30 = (bf16[4,2,2,32,2048]{4,3,2,1,0:T(8,128)(2,1)S(1)}, bf16[4,2,2,32,2048]{4,3,2,1,0:T(8,128)(2,1)}, u32[]{:S(2)}) copy-start(bf16[4,2,2,32,2048]{4,3,2,1,0:T(8,128)(2,1)} %get-tuple-element.110) | copy-start | bytes 6291460
  689.9 10.4 %collective-permute-start.7 = (bf16[32,3072]{1,0:T(8,128)(2,1)S(1)}, bf16[32,3072]{1,0:T(8,128)(2,1)S(1)}, u32[]{:S(2)}, u32[]{:S(2)}) collective-permute-start(bf16[32,3072]{1,0:T(8,128)(2,1)S(1)} %pad_maximum_fusion.17), channel_id=1, source_target_pairs={{0,24},{1,25},{2,26},{3,27},{4,28},{5,29},{6,30},{7,31},{8,16},{9,... | collective-permute-start | bytes 589832 | tf_op jit(solution)/shard_map/ppermute | solution.py:614
  694.4 15.0 %collective-permute-start.6 = (bf16[32,3072]{1,0:T(8,128)(2,1)S(1)}, bf16[32,3072]{1,0:T(8,128)(2,1)S(1)}, u32[]{:S(2)}, u32[]{:S(2)}) collective-permute-start(bf16[32,3072]{1,0:T(8,128)(2,1)S(1)} %pad_maximum_fusion.16), channel_id=1, source_target_pairs={{0,16},{1,17},{2,18},{3,19},{4,20},{5,21},{6,22},{7,23},{8,24},{9,... | collective-permute-start | bytes 589832 | tf_op jit(solution)/shard_map/ppermute | solution.py:614
  695.1 15.0 %collective-permute-start.5 = (bf16[32,3072]{1,0:T(8,128)(2,1)S(1)}, bf16[32,3072]{1,0:T(8,128)(2,1)S(1)}, u32[]{:S(2)}, u32[]{:S(2)}) collective-permute-start(bf16[32,3072]{1,0:T(8,128)(2,1)S(1)} %pad_maximum_fusion.15), channel_id=1, source_target_pairs={{0,8},{1,9},{2,10},{3,11},{4,12},{5,13},{6,14},{7,15},{8,0},{9,1},... | collective-permute-start | bytes 589832 | tf_op jit(solution)/shard_map/ppermute | solution.py:614
  700.3 26.3 %collective-permute-start.17 = (bf16[4,2,32,2048]{3,2,1,0:T(8,128)(2,1)}, bf16[4,2,32,2048]{3,2,1,0:T(8,128)(2,1)S(1)}, u32[]{:S(2)}, u32[]{:S(2)}) collective-permute-start(bf16[4,2,32,2048]{3,2,1,0:T(8,128)(2,1)} %fusion.62), channel_id=1, source_target_pairs={{0,2},{1,3},{2,0},{3,1},{4,6},{5,7},{6,4},{7,5},{8,10},{9,11},{10,... | collective-permute-start | bytes 3145736 | tf_op jit(solution)/shard_map/ppermute | solution.py:614
  709.4 26.3 %collective-permute-start.27 = (bf16[4,2,128,512]{3,2,1,0:T(8,128)(2,1)}, bf16[4,2,128,512]{3,2,1,0:T(8,128)(2,1)S(1)}, u32[]{:S(2)}, u32[]{:S(2)}) collective-permute-start(bf16[4,2,128,512]{3,2,1,0:T(8,128)(2,1)} %fusion.65), channel_id=1, source_target_pairs={{0,1},{1,0},{2,3},{3,2},{4,5},{5,4},{6,7},{7,6},{8,9},{9,8},{10,11... | collective-permute-start | bytes 3145736 | tf_op jit(solution)/shard_map/ppermute | solution.py:614
  710.1 39.0 %collective-permute-start.25 = (bf16[4,2,128,512]{3,2,1,0:T(8,128)(2,1)}, bf16[4,2,128,512]{3,2,1,0:T(8,128)(2,1)S(1)}, u32[]{:S(2)}, u32[]{:S(2)}) collective-permute-start(bf16[4,2,128,512]{3,2,1,0:T(8,128)(2,1)} %fusion.64), channel_id=1, source_target_pairs={{0,2},{1,3},{2,0},{3,1},{4,6},{5,7},{6,4},{7,5},{8,10},{9,11},{10,... | collective-permute-start | bytes 3145736 | tf_op jit(solution)/shard_map/ppermute | solution.py:614
  715.0 12.9 %copy-start.26 = (bf16[4,2,2,32,2560]{4,3,2,1,0:T(8,128)(2,1)S(1)}, bf16[4,2,2,32,2560]{4,3,2,1,0:T(8,128)(2,1)}, u32[]{:S(2)}) copy-start(bf16[4,2,2,32,2560]{4,3,2,1,0:T(8,128)(2,1)} %pad_maximum_fusion.1) | copy-start | bytes 7864324
  715.4 85.9 %collective-permute-start.11 = (bf16[4,2,32,2560]{3,2,1,0:T(8,128)(2,1)S(1)}, bf16[4,2,32,2560]{3,2,1,0:T(8,128)(2,1)S(1)}, u32[]{:S(2)}, u32[]{:S(2)}) collective-permute-start(bf16[4,2,32,2560]{3,2,1,0:T(8,128)(2,1)S(1)} %fusion.56), channel_id=1, source_target_pairs={{0,1},{1,0},{2,3},{3,2},{4,5},{5,4},{6,7},{7,6},{8,9},{9,8},{10,11... | collective-permute-start | bytes 3932168 | tf_op jit(solution)/shard_map/ppermute | solution.py:614
  717.5 42.8 %collective-permute-start.20 = (bf16[4,32,2048]{2,1,0:T(8,128)(2,1)S(1)}, bf16[4,32,2048]{2,1,0:T(8,128)(2,1)S(1)}, u32[]{:S(2)}, u32[]{:S(2)}) collective-permute-start(bf16[4,32,2048]{2,1,0:T(8,128)(2,1)S(1)} %fusion.74), channel_id=1, source_target_pairs={{0,2},{1,3},{2,0},{3,1},{4,6},{5,7},{6,4},{7,5},{8,10},{9,11},{10,... | collective-permute-start | bytes 1572872 | tf_op jit(solution)/shard_map/ppermute | solution.py:614
  726.9 48.1 %collective-permute-start.18 = (bf16[4,32,2048]{2,1,0:T(8,128)(2,1)S(1)}, bf16[4,32,2048]{2,1,0:T(8,128)(2,1)S(1)}, u32[]{:S(2)}, u32[]{:S(2)}) collective-permute-start(bf16[4,32,2048]{2,1,0:T(8,128)(2,1)S(1)} %fusion.75), channel_id=1, source_target_pairs={{0,1},{1,0},{2,3},{3,2},{4,5},{5,4},{6,7},{7,6},{8,9},{9,8},{10,11... | collective-permute-start | bytes 1572872 | tf_op jit(solution)/shard_map/ppermute | solution.py:614
  728.3 46.8 %copy-start.50 = (bf16[4,2,32,2048]{3,2,1,0:T(8,128)(2,1)S(1)}, bf16[4,2,32,2048]{3,2,1,0:T(8,128)(2,1)}, u32[]{:S(2)}) copy-start(bf16[4,2,32,2048]{3,2,1,0:T(8,128)(2,1)} %copy-done.49) | copy-start | bytes 3145732
  735.7 67.4 %collective-permute-start.9 = (bf16[4,2,32,2560]{3,2,1,0:T(8,128)(2,1)S(1)}, bf16[4,2,32,2560]{3,2,1,0:T(8,128)(2,1)S(1)}, u32[]{:S(2)}, u32[]{:S(2)}) collective-permute-start(bf16[4,2,32,2560]{3,2,1,0:T(8,128)(2,1)S(1)} %fusion.55), channel_id=1, source_target_pairs={{0,2},{1,3},{2,0},{3,1},{4,6},{5,7},{6,4},{7,5},{8,10},{9,11},{10,... | collective-permute-start | bytes 3932168 | tf_op jit(solution)/shard_map/ppermute | solution.py:614
  749.1 46.8 %collective-permute-start.28 = (bf16[4,128,512]{2,1,0:T(8,128)(2,1)S(1)}, bf16[4,128,512]{2,1,0:T(8,128)(2,1)S(1)}, u32[]{:S(2)}, u32[]{:S(2)}) collective-permute-start(bf16[4,128,512]{2,1,0:T(8,128)(2,1)S(1)} %fusion.72), channel_id=1, source_target_pairs={{0,2},{1,3},{2,0},{3,1},{4,6},{5,7},{6,4},{7,5},{8,10},{9,11},{10,... | collective-permute-start | bytes 1572872 | tf_op jit(solution)/shard_map/ppermute | solution.py:614
  760.3 40.5 %collective-permute-start.26 = (bf16[4,128,512]{2,1,0:T(8,128)(2,1)S(1)}, bf16[4,128,512]{2,1,0:T(8,128)(2,1)S(1)}, u32[]{:S(2)}, u32[]{:S(2)}) collective-permute-start(bf16[4,128,512]{2,1,0:T(8,128)(2,1)S(1)} %fusion.73), channel_id=1, source_target_pairs={{0,1},{1,0},{2,3},{3,2},{4,5},{5,4},{6,7},{7,6},{8,9},{9,8},{10,11... | collective-permute-start | bytes 1572872 | tf_op jit(solution)/shard_map/ppermute | solution.py:614
  775.4 30.1 %collective-permute-start.23 = (bf16[32,4096]{1,0:T(8,128)(2,1)S(1)}, bf16[32,4096]{1,0:T(8,128)(2,1)S(1)}, u32[]{:S(2)}, u32[]{:S(2)}) collective-permute-start(bf16[32,4096]{1,0:T(8,128)(2,1)S(1)} %pad_maximum_fusion.11), channel_id=1, source_target_pairs={{0,24},{1,25},{2,26},{3,27},{4,28},{5,29},{6,30},{7,31},{8,16},{9,... | collective-permute-start | bytes 786440 | tf_op jit(solution)/shard_map/ppermute | solution.py:614
  795.9 24.1 %collective-permute-start.22 = (bf16[32,4096]{1,0:T(8,128)(2,1)S(1)}, bf16[32,4096]{1,0:T(8,128)(2,1)S(1)}, u32[]{:S(2)}, u32[]{:S(2)}) collective-permute-start(bf16[32,4096]{1,0:T(8,128)(2,1)S(1)} %pad_maximum_fusion.10), channel_id=1, source_target_pairs={{0,16},{1,17},{2,18},{3,19},{4,20},{5,21},{6,22},{7,23},{8,24},{9,... | collective-permute-start | bytes 786440 | tf_op jit(solution)/shard_map/ppermute | solution.py:614
  800.8 20.5 %collective-permute-start.21 = (bf16[32,4096]{1,0:T(8,128)(2,1)S(1)}, bf16[32,4096]{1,0:T(8,128)(2,1)S(1)}, u32[]{:S(2)}, u32[]{:S(2)}) collective-permute-start(bf16[32,4096]{1,0:T(8,128)(2,1)S(1)} %pad_maximum_fusion.9), channel_id=1, source_target_pairs={{0,8},{1,9},{2,10},{3,11},{4,12},{5,13},{6,14},{7,15},{8,0},{9,1},... | collective-permute-start | bytes 786440 | tf_op jit(solution)/shard_map/ppermute | solution.py:614
  801.3 22.6 %collective-permute-start.31 = (bf16[128,1024]{1,0:T(8,128)(2,1)S(1)}, bf16[128,1024]{1,0:T(8,128)(2,1)S(1)}, u32[]{:S(2)}, u32[]{:S(2)}) collective-permute-start(bf16[128,1024]{1,0:T(8,128)(2,1)S(1)} %pad_maximum_fusion.14), channel_id=1, source_target_pairs={{0,24},{1,25},{2,26},{3,27},{4,28},{5,29},{6,30},{7,31},{8,16},{9,... | collective-permute-start | bytes 786440 | tf_op jit(solution)/shard_map/ppermute | solution.py:614
  803.1 24.6 %collective-permute-start.30 = (bf16[128,1024]{1,0:T(8,128)(2,1)S(1)}, bf16[128,1024]{1,0:T(8,128)(2,1)S(1)}, u32[]{:S(2)}, u32[]{:S(2)}) collective-permute-start(bf16[128,1024]{1,0:T(8,128)(2,1)S(1)} %pad_maximum_fusion.13), channel_id=1, source_target_pairs={{0,16},{1,17},{2,18},{3,19},{4,20},{5,21},{6,22},{7,23},{8,24},{9,... | collective-permute-start | bytes 786440 | tf_op jit(solution)/shard_map/ppermute | solution.py:614
  805.5 22.2 %collective-permute-start.29 = (bf16[128,1024]{1,0:T(8,128)(2,1)S(1)}, bf16[128,1024]{1,0:T(8,128)(2,1)S(1)}, u32[]{:S(2)}, u32[]{:S(2)}) collective-permute-start(bf16[128,1024]{1,0:T(8,128)(2,1)S(1)} %pad_maximum_fusion.12), channel_id=1, source_target_pairs={{0,8},{1,9},{2,10},{3,11},{4,12},{5,13},{6,14},{7,15},{8,0},{9,1},... | collective-permute-start | bytes 786440 | tf_op jit(solution)/shard_map/ppermute | solution.py:614
  819.9 12.3 %collective-permute-start.12 = (bf16[4,32,2560]{2,1,0:T(8,128)(2,1)S(1)}, bf16[4,32,2560]{2,1,0:T(8,128)(2,1)S(1)}, u32[]{:S(2)}, u32[]{:S(2)}) collective-permute-start(bf16[4,32,2560]{2,1,0:T(8,128)(2,1)S(1)} %fusion.57), channel_id=1, source_target_pairs={{0,2},{1,3},{2,0},{3,1},{4,6},{5,7},{6,4},{7,5},{8,10},{9,11},{10,... | collective-permute-start | bytes 1966088 | tf_op jit(solution)/shard_map/ppermute | solution.py:614
  821.3 10.6 %collective-permute-start.10 = (bf16[4,32,2560]{2,1,0:T(8,128)(2,1)S(1)}, bf16[4,32,2560]{2,1,0:T(8,128)(2,1)S(1)}, u32[]{:S(2)}, u32[]{:S(2)}) collective-permute-start(bf16[4,32,2560]{2,1,0:T(8,128)(2,1)S(1)} %fusion.58), channel_id=1, source_target_pairs={{0,1},{1,0},{2,3},{3,2},{4,5},{5,4},{6,7},{7,6},{8,9},{9,8},{10,11... | collective-permute-start | bytes 1966088 | tf_op jit(solution)/shard_map/ppermute | solution.py:614
  832.6 9.8 %collective-permute-start.15 = (bf16[32,5120]{1,0:T(8,128)(2,1)S(1)}, bf16[32,5120]{1,0:T(8,128)(2,1)S(1)}, u32[]{:S(2)}, u32[]{:S(2)}) collective-permute-start(bf16[32,5120]{1,0:T(8,128)(2,1)S(1)} %pad_maximum_fusion.8), channel_id=1, source_target_pairs={{0,24},{1,25},{2,26},{3,27},{4,28},{5,29},{6,30},{7,31},{8,16},{9,... | collective-permute-start | bytes 983048 | tf_op jit(solution)/shard_map/ppermute | solution.py:614
  832.7 22.0 %collective-permute-start.14 = (bf16[32,5120]{1,0:T(8,128)(2,1)S(1)}, bf16[32,5120]{1,0:T(8,128)(2,1)S(1)}, u32[]{:S(2)}, u32[]{:S(2)}) collective-permute-start(bf16[32,5120]{1,0:T(8,128)(2,1)S(1)} %pad_maximum_fusion.7), channel_id=1, source_target_pairs={{0,16},{1,17},{2,18},{3,19},{4,20},{5,21},{6,22},{7,23},{8,24},{9,... | collective-permute-start | bytes 983048 | tf_op jit(solution)/shard_map/ppermute | solution.py:614
  832.8 21.9 %collective-permute-start.13 = (bf16[32,5120]{1,0:T(8,128)(2,1)S(1)}, bf16[32,5120]{1,0:T(8,128)(2,1)S(1)}, u32[]{:S(2)}, u32[]{:S(2)}) collective-permute-start(bf16[32,5120]{1,0:T(8,128)(2,1)S(1)} %pad_maximum_fusion.6), channel_id=1, source_target_pairs={{0,8},{1,9},{2,10},{3,11},{4,12},{5,13},{6,14},{7,15},{8,0},{9,1},... | collective-permute-start | bytes 983048 | tf_op jit(solution)/shard_map/ppermute | solution.py:614
  (50 other events, 203.5 us)
Sparse Core Ops, SparseCore 0:
  12.9 94.0 all-gather.4
  110.5 85.4 all-gather.6
  198.9 76.0 all-gather.8
  277.7 76.1 all-gather.10
  535.9 125.7 all-reduce.3

commit v2 on v0

--- a/solution.py
+++ b/solution.py
@@ -1,6 +1,12 @@
+import functools
+import itertools
+
 import jax
 import jax.numpy as jnp
 from jax import lax
+from jax.experimental import pallas as pl
+from jax.experimental.pallas import tpu as pltpu
+from jax.sharding import Mesh
 from jax.sharding import PartitionSpec as P
 
 D = 1024
@@ -11,6 +17,7 @@
 EPSILON = 1e-05
 SCALING = 0.125
 NEGATIVE = -1e30
+VMEM = 56 * 1024 * 1024
 
 
 def layer_norm(values, gain, shift):
@@ -63,7 +70,7 @@
     return (jnp.where(mask_at(start, width), scores, NEGATIVE), key_block)
 
 
-def attend(query_rows, key_rows, value_rows, mask_at, width):
+def spread_attend(query_rows, key_rows, value_rows, mask_at, width):
     queries = split_heads(query_rows)
     batch_size, length = (query_rows.shape[0], query_rows.shape[1])
     blocks = key_rows.shape[1] // width
@@ -96,7 +103,7 @@
     return (total.reshape(batch_size, length, HEADS * HEAD_DIM).astype(jnp.bfloat16), log_total)
 
 
-def attend_back(query_rows, key_rows, value_rows, grad_rows, log_total, mask_at, width):
+def spread_attend_back(query_rows, key_rows, value_rows, grad_rows, log_total, mask_at, width):
     queries = split_heads(query_rows)
     grad_heads = split_heads(grad_rows)
     batch_size, length = (query_rows.shape[0], query_rows.shape[1])
@@ -237,7 +244,7 @@
         lax.all_gather(value_one, "seq", axis=1, tiled=True),
     )
     self_width = min(128, key_all.shape[1])
-    attended, log_one = attend(query_one, key_all, value_all, causal_at, self_width)
+    attended, log_one = spread_attend(query_one, key_all, value_all, causal_at, self_width)
     after_self = residual + project(attended, self_full[4]) + self_full[5].astype(jnp.float32)
     cross_full = gather_cross(
         norm2_gain, norm2_bias, cross_query, cross_kv, cross_bias_qv, cross_out, cross_out_bias
@@ -256,7 +263,7 @@
         lax.all_gather(text_value, "seq", axis=1, tiled=True),
     )
     text_width = key_two.shape[1]
-    attended_two, log_two = attend(query_two, key_two, value_two, padded_at, text_width)
+    attended_two, log_two = spread_attend(query_two, key_two, value_two, padded_at, text_width)
     after_cross = (
         after_self + project(attended_two, cross_full[5]) + cross_full[6].astype(jnp.float32)
     )
@@ -301,7 +308,7 @@
     cross_out_term = weight_grad(attended_two, grad_cross)
     cross_bias_term = column_sums(grad_cross)
     grad_att_two = project_back(grad_cross, cross_back[5]).astype(jnp.bfloat16)
-    grad_query_two, grad_key_two, grad_value_two, delta_two = attend_back(
+    grad_query_two, grad_key_two, grad_value_two, delta_two = spread_attend_back(
         query_two, key_two, value_two, grad_att_two, log_two, padded_at, text_width
     )
     query_two_low = grad_query_two.astype(jnp.bfloat16)
@@ -340,7 +347,7 @@
     self_out_term = weight_grad(attended, grad_self)
     self_bias_term = column_sums(grad_self)
     grad_att_one = project_back(grad_self, self_back[4]).astype(jnp.bfloat16)
-    grad_query_one, grad_key_all, grad_value_all, delta_one = attend_back(
+    grad_query_one, grad_key_all, grad_value_all, delta_one = spread_attend_back(
         query_one, key_all, value_all, grad_att_one, log_one, causal_at, self_width
     )
     grad_key_one, grad_value_one = (
@@ -399,59 +406,980 @@
     )
 
 
+LOG2E = 1.4426950408889634
+LN2 = 0.6931471805599453
+QB = 256
+PAIR = 2 * HEAD_DIM
+NT = (((1,), (1,)), ((), ()))
+NN = (((1,), (0,)), ((), ()))
+TN = (((0,), (0,)), ((), ()))
+BF16 = jnp.bfloat16
+F32 = jnp.float32
+
+
+def mm(left, right, dims=NN):
+    return lax.dot_general(left, right, dims, preferred_element_type=F32)
+
+
+def head_lanes(rows, head):
+    lane = lax.broadcasted_iota(jnp.int32, rows.shape, 1)
+    keep = (lane < HEAD_DIM) if head == 0 else (lane >= HEAD_DIM)
+    return jnp.where(keep, rows, jnp.zeros_like(rows))
+
+
+def whole(shape, index=None, single=True):
+    where = index or (0,) * len(shape)
+    mode = {"pipeline_mode": pl.Buffered(1)} if single else {}
+    return pl.BlockSpec(shape, lambda *_: where, **mode)
+
+
+def kernel_call(body, name, grid, ins, outs, shapes, args, scratch=(), flops=0, prefetch=0, moved=0, exps=0):
+    return pl.pallas_call(
+        body,
+        grid_spec=pltpu.PrefetchScalarGridSpec(
+            num_scalar_prefetch=prefetch,
+            grid=grid,
+            in_specs=ins,
+            out_specs=outs,
+            scratch_shapes=list(scratch),
+        ),
+        out_shape=[jax.ShapeDtypeStruct(s, d) for s, d in shapes],
+        compiler_params=pltpu.CompilerParams(vmem_limit_bytes=VMEM),
+        cost_estimate=pl.CostEstimate(flops=flops // 32, bytes_accessed=moved // 32, transcendentals=exps // 32),
+        name=name,
+    )(*args)
+
+
+def attend_kernel(q_ref, k_ref, v_ref, o_ref, lse_ref, vx_ref):
+    keys = k_ref.shape[0]
+    length = q_ref.shape[0]
+    block = min(QB, length)
+    vx_ref[:, :PAIR] = v_ref[...]
+    vx_ref[:, PAIR:] = jnp.ones((keys, PAIR), BF16)
+    for start in range(0, length, block):
+        limit = start + block
+        rows = q_ref[start:limit, :]
+        both = []
+        for head in range(2):
+            scores = mm(head_lanes(rows, head), k_ref[:limit, :], NT)
+            last = scores[:, start:]
+            col = lax.broadcasted_iota(jnp.int32, last.shape, 1)
+            row = lax.broadcasted_iota(jnp.int32, last.shape, 0)
+            last = jnp.where(col <= row, last, NEGATIVE)
+            if start:
+                scores = jnp.concatenate([scores[:, :start], last], axis=1)
+            else:
+                scores = last
+            top = jnp.max(scores, axis=1, keepdims=True)
+            weights = jnp.exp2(scores - top).astype(BF16)
+            total = mm(weights, vx_ref[:limit, :])
+            both.append(total[:, :PAIR] / total[:, PAIR:])
+            stat = (top + jnp.log2(total[:, PAIR:])).T
+            lse_ref[0, head : head + 1, start:limit] = stat[:1, :]
+        lane = lax.broadcasted_iota(jnp.int32, both[0].shape, 1)
+        o_ref[start:limit, :] = jnp.where(lane < HEAD_DIM, both[0], both[1]).astype(BF16)
+
+
+def attend_back_kernel(
+    q_ref, k_ref, v_ref, o_ref, do_ref, lse_ref, dq_ref, dk_ref, dv_ref, acc_ref
+):
+    keys = k_ref.shape[0]
+    block = min(QB, keys)
+    product = (do_ref[...].astype(F32) * o_ref[...].astype(F32)).T
+    acc_ref[...] = jnp.zeros_like(acc_ref)
+    delta = [
+        jnp.sum(product[head * HEAD_DIM : (head + 1) * HEAD_DIM, :], axis=0, keepdims=True)
+        for head in range(2)
+    ]
+    for start in range(0, keys, block):
+        key_rows = k_ref[start : start + block, :]
+        value_rows = v_ref[start : start + block, :]
+        grad_keys = grad_values = None
+        for head in range(2):
+            queries = head_lanes(q_ref[start:, :], head)
+            grads = head_lanes(do_ref[start:, :], head)
+            scores = mm(key_rows, queries, NT)
+            probs = jnp.exp2(scores - lse_ref[0, head : head + 1, start:])
+            edge = probs[:, :block]
+            row = lax.broadcasted_iota(jnp.int32, edge.shape, 0)
+            col = lax.broadcasted_iota(jnp.int32, edge.shape, 1)
+            edge = jnp.where(row <= col, edge, 0.0)
+            if start + block < keys:
+                probs = jnp.concatenate([edge, probs[:, block:]], axis=1)
+            else:
+                probs = edge
+            back = mm(value_rows, grads, NT)
+            scored = (probs * (back - delta[head][:, start:])).astype(BF16)
+            term_v = mm(probs.astype(BF16), grads)
+            term_k = mm(scored, queries)
+            grad_values = term_v if grad_values is None else grad_values + term_v
+            grad_keys = term_k if grad_keys is None else grad_keys + term_k
+            acc_ref[start:, :] += mm(scored, head_lanes(key_rows, head), TN)
+        dk_ref[start : start + block, :] = (grad_keys * LN2).astype(BF16)
+        dv_ref[start : start + block, :] = grad_values.astype(BF16)
+    dq_ref[...] = (acc_ref[...] * SCALING).astype(BF16)
+
+
+def column_pair(rows, offset):
+    return pl.BlockSpec((rows, PAIR), lambda i, *_: (0, i + offset))
+
+
+def attend(qkv):
+    length = qkv.shape[0]
+    pairs = HEADS // 2
+    return kernel_call(
+        attend_kernel,
+        "attend",
+        (pairs,),
+        [column_pair(length, pairs * i) for i in range(3)],
+        [column_pair(length, 0), pl.BlockSpec((1, 2, length), lambda i, *_: (i, 0, 0))],
+        [((length, D), BF16), ((pairs, 2, length), F32)],
+        (qkv, qkv, qkv),
+        scratch=[pltpu.VMEM((length, 2 * PAIR), BF16)],
+        flops=length * length * HEADS * 512,
+        moved=8 * length * D,
+        exps=length * length * HEADS // 2,
+    )
+
+
+def attend_back(qkv, out, grad, lse, first, count):
+    length = qkv.shape[0]
+    pairs = HEADS // 2
+    return kernel_call(
+        attend_back_kernel,
+        "attend_back",
+        (count,),
+        [column_pair(length, pairs * i + first) for i in range(3)]
+        + [column_pair(length, first)] * 2
+        + [pl.BlockSpec((1, 2, length), lambda i, *_: (i + first, 0, 0))],
+        [column_pair(length, 0)] * 3,
+        [((length, count * PAIR), BF16)] * 3,
+        (qkv, qkv, qkv, out, grad, lse),
+        scratch=[pltpu.VMEM((length, PAIR), F32)],
+        flops=length * length * count * 2560,
+        moved=2 * 8 * length * count * PAIR,
+        exps=length * length * count,
+    )
+
+
+def normed_of(rows):
+    center = rows - jnp.mean(rows, axis=1, keepdims=True)
+    inverse = lax.rsqrt(jnp.mean(center * center, axis=1, keepdims=True) + EPSILON)
+    return (center * inverse, inverse)
+
+
+def norm_input_grad(grads, normed, inverse, gain):
+    scaled = grads * gain
+    return inverse * (
+        scaled
+        - jnp.mean(scaled, axis=1, keepdims=True)
+        - normed * jnp.mean(scaled * normed, axis=1, keepdims=True)
+    )
+
+
+def sums(rows):
+    return jnp.sum(rows, axis=0, keepdims=True)
+
+
+def add_row(ref, at, value, first):
+    @pl.when(first)
+    def _():
+        ref[at : at + 1, :] = value
+
+    @pl.when(jnp.logical_not(first))
+    def _():
+        ref[at : at + 1, :] += value
+
+
+def gelu_pair(values):
+    root = 0.7978845608028654
+    square = values * values
+    bend = jnp.tanh(values * (root + (0.044715 * root) * square))
+    half = 0.5 + 0.5 * bend
+    slope = half + values * (0.5 - 0.5 * bend * bend) * (root + (0.134145 * root) * square)
+    return (values * half, slope)
+
+
+def qkv_kernel(x_ref, w_ref, vec_ref, h_ref, qkv_ref):
+    normed, _ = normed_of(x_ref[...].astype(F32))
+    low = (normed * vec_ref[0:1, :] + vec_ref[1:2, :]).astype(BF16)
+    h_ref[...] = low
+    for part in range(3):
+        mixed = mm(low, w_ref[:, part * D : (part + 1) * D]) + vec_ref[2 + part : 3 + part, :]
+        if part == 0:
+            mixed = mixed * (SCALING * LOG2E)
+        qkv_ref[:, part * D : (part + 1) * D] = mixed.astype(BF16)
+
+
+def pair_keys(kv_ref, at, keys):
+    block = kv_ref[:, at : at + PAIR]
+    return jnp.concatenate([head_lanes(block, 0), head_lanes(block, 1)], axis=0)
+
+
+def cross_kernel(
+    len_ref, x_ref, o_ref, ws_ref, wq_ref, wc_ref, kv_ref, vec_ref,
+    x1_ref, h2_ref, q2_ref, o2_ref, x2_ref, h3_ref, lse_ref,
+):
+    keys = kv_ref.shape[0]
+    after = x_ref[...].astype(F32) + mm(o_ref[...], ws_ref[...]) + vec_ref[0:1, :]
+    x1_ref[...] = after
+    normed, _ = normed_of(after)
+    low = (normed * vec_ref[1:2, :] + vec_ref[2:3, :]).astype(BF16)
+    h2_ref[...] = low
+    q2_ref[...] = ((mm(low, wq_ref[...]) + vec_ref[3:4, :]) * (SCALING * LOG2E)).astype(BF16)
+    ones = jnp.ones((keys, PAIR), BF16)
+    for pair in range(HEADS // 2):
+        at = pair * PAIR
+        scores = mm(q2_ref[:, at : at + PAIR], pair_keys(kv_ref, at, keys), NT)
+        col = lax.broadcasted_iota(jnp.int32, (scores.shape[0], keys), 1)
+        inside = col < len_ref[0]
+        halves, tops = ([], [])
+        for head in range(2):
+            part = jnp.where(inside, scores[:, head * keys : (head + 1) * keys], NEGATIVE)
+            top = jnp.max(part, axis=1, keepdims=True)
+            halves.append(jnp.exp2(part - top).astype(BF16))
+            tops.append(top)
+        values = kv_ref[:, D + at : D + at + PAIR]
+        right = jnp.concatenate(
+            [
+                jnp.concatenate([head_lanes(values, h), head_lanes(ones, h)], axis=1)
+                for h in range(2)
+            ],
+            axis=0,
+        )
+        total = mm(jnp.concatenate(halves, axis=1), right)
+        o2_ref[:, at : at + PAIR] = (total[:, :PAIR] / total[:, PAIR:]).astype(BF16)
+        lane = lax.broadcasted_iota(jnp.int32, (scores.shape[0], PAIR), 1)
+        stat = (jnp.where(lane < HEAD_DIM, tops[0], tops[1]) + jnp.log2(total[:, PAIR:])).T
+        lse_ref[2 * pair : 2 * pair + 1, :] = stat[:1, :]
+        lse_ref[2 * pair + 1 : 2 * pair + 2, :] = stat[HEAD_DIM : HEAD_DIM + 1, :]
+    after = after + mm(o2_ref[...], wc_ref[...]) + vec_ref[4:5, :]
+    x2_ref[...] = after
+    normed, _ = normed_of(after)
+    h3_ref[...] = (normed * vec_ref[5:6, :] + vec_ref[6:7, :]).astype(BF16)
+
+
+def mlp_kernel(h_ref, wi_ref, wo_ref, bias_ref, x2_ref, last_ref, act_ref, slope_ref, out_ref, acc_ref):
+    step = pl.program_id(0)
+    length = h_ref.shape[0]
+    for start in range(0, length, QB):
+        rows = slice(start, start + QB)
+        act, slope = gelu_pair(mm(h_ref[rows, :], wi_ref[...]) + bias_ref[0])
+        act = act.astype(BF16)
+        act_ref[rows, :] = act
+        slope_ref[rows, :] = slope.astype(BF16)
+        term = mm(act, wo_ref[...])
+
+        @pl.when(step == 0)
+        def _():
+            acc_ref[rows, :] = x2_ref[rows, :] + last_ref[...] + term
+
+        @pl.when(step > 0)
+        def _():
+            acc_ref[rows, :] += term
+
+        @pl.when(step == pl.num_programs(0) - 1)
+        def _():
+            out_ref[rows, :] = acc_ref[rows, :].astype(BF16)
+
+
+def du_kernel(g_ref, wo_ref, slope_ref, du_ref, sum_ref):
+    length = g_ref.shape[0]
+    total = None
+    for start in range(0, length, QB):
+        rows = slice(start, start + QB)
+        grad = mm(g_ref[rows, :], wo_ref[...], NT) * slope_ref[rows, :].astype(F32)
+        low = grad.astype(BF16)
+        du_ref[rows, :] = low
+        part = sums(low.astype(F32))
+        total = part if total is None else total + part
+    sum_ref[0] = total
+
+
+def norm3_kernel(du_ref, wi_ref, g_ref, x2_ref, gain_ref, wc_ref, dx_ref, dc_ref, do_ref, vec_ref):
+    first = pl.program_id(0) == 0
+    grads = None
+    for step in range(wi_ref.shape[1] // D):
+        cols = slice(step * D, (step + 1) * D)
+        term = mm(du_ref[:, cols], wi_ref[:, cols], NT)
+        grads = term if grads is None else grads + term
+    normed, inverse = normed_of(x2_ref[...])
+    out = g_ref[...].astype(F32) + norm_input_grad(grads, normed, inverse, gain_ref[...])
+    dx_ref[...] = out
+    low = out.astype(BF16)
+    dc_ref[...] = low
+    do_ref[...] = mm(low, wc_ref[...], NT).astype(BF16)
+    add_row(vec_ref, 0, sums(grads * normed), first)
+    add_row(vec_ref, 1, sums(grads), first)
+    add_row(vec_ref, 2, sums(low.astype(F32)), first)
+    add_row(vec_ref, 3, sums(g_ref[...].astype(F32)), first)
+
+
+def cross_back_kernel(
+    len_ref, q_ref, kv_ref, o_ref, do_ref, lse_ref, wq_ref, ws_ref, x1_ref, dx2_ref, gain_ref,
+    dq_ref, dkv_ref, dx_ref, da_ref, do1_ref, vec_ref, acc_ref,
+):
+    step = pl.program_id(0)
+    first = step == 0
+    keys = kv_ref.shape[0]
+
+    @pl.when(first)
+    def _():
+        acc_ref[...] = jnp.zeros_like(acc_ref)
+
+    lane = lax.broadcasted_iota(jnp.int32, (keys, PAIR), 1)
+    for pair in range(HEADS // 2):
+        at = pair * PAIR
+        queries = q_ref[:, at : at + PAIR]
+        grads = do_ref[:, at : at + PAIR]
+        product = (grads.astype(F32) * o_ref[:, at : at + PAIR].astype(F32)).T
+        both_keys = pair_keys(kv_ref, at, keys)
+        scores = mm(both_keys, queries, NT)
+        back = mm(pair_keys(kv_ref, D + at, keys), grads, NT)
+        row = lax.broadcasted_iota(jnp.int32, (keys, scores.shape[1]), 0)
+        inside = row < len_ref[0]
+        probs, scored = ([], [])
+        for head in range(2):
+            span = slice(head * keys, (head + 1) * keys)
+            at_head = 2 * pair + head
+            prob = jnp.exp2(scores[span, :] - lse_ref[at_head : at_head + 1, :])
+            prob = jnp.where(inside, prob, 0.0)
+            delta = sums(product[head * HEAD_DIM : (head + 1) * HEAD_DIM, :])
+            probs.append(prob.astype(BF16))
+            scored.append((prob * (back[span, :] - delta)).astype(BF16))
+        probs, scored = (jnp.concatenate(probs, axis=0), jnp.concatenate(scored, axis=0))
+        for base, left, right in ((0, scored, queries), (D, probs, grads)):
+            both = mm(left, right)
+            acc_ref[:, base + at : base + at + PAIR] += jnp.where(
+                lane < HEAD_DIM, both[:keys, :], both[keys:, :]
+            )
+        dq_ref[:, at : at + PAIR] = (mm(scored, both_keys, TN) * SCALING).astype(BF16)
+
+    @pl.when(step == pl.num_programs(0) - 1)
+    def _():
+        dkv_ref[:, :D] = (acc_ref[:, :D] * LN2).astype(BF16)
+        dkv_ref[:, D:] = acc_ref[:, D:].astype(BF16)
+
+    grads = mm(dq_ref[...], wq_ref[...], NT)
+    normed, inverse = normed_of(x1_ref[...])
+    out = dx2_ref[...] + norm_input_grad(grads, normed, inverse, gain_ref[...])
+    dx_ref[...] = out
+    low = out.astype(BF16)
+    da_ref[...] = low
+    do1_ref[...] = mm(low, ws_ref[...], NT).astype(BF16)
+    add_row(vec_ref, 0, sums(grads * normed), first)
+    add_row(vec_ref, 1, sums(grads), first)
+    add_row(vec_ref, 2, sums(low.astype(F32)), first)
+    add_row(vec_ref, 3, sums(dq_ref[...].astype(F32)), first)
+
+
+def norm1_kernel(*refs):
+    *grad_refs, w_ref, x_ref, dx1_ref, gain_ref, out_ref, vec_ref = refs
+    first = pl.program_id(0) == 0
+    grads, at = (None, 0)
+    groups = len(grad_refs) // 3
+    rows_q, rows_v = ([], [])
+    for group in range(groups):
+        for part in range(3):
+            ref = grad_refs[3 * group + part]
+            wide = ref.shape[1]
+            base = part * D + group * wide
+            term = mm(ref[...], w_ref[:, base : base + wide], NT)
+            grads = term if grads is None else grads + term
+        rows_q.append(sums(grad_refs[3 * group][...].astype(F32)))
+        rows_v.append(sums(grad_refs[3 * group + 2][...].astype(F32)))
+    normed, inverse = normed_of(x_ref[...].astype(F32))
+    back = norm_input_grad(grads, normed, inverse, gain_ref[...])
+    out_ref[...] = (dx1_ref[...] + back).astype(BF16)
+    add_row(vec_ref, 0, sums(grads * normed), first)
+    add_row(vec_ref, 1, sums(grads), first)
+    add_row(vec_ref, 2, jnp.concatenate(rows_q, axis=1), first)
+    add_row(vec_ref, 3, jnp.concatenate(rows_v, axis=1), first)
+
+
+def weight_grad_kernel(units, count, scattered, place_ref, *refs):
+    operands, (sent_ref, kept_ref, acc_ref) = (refs[:count], refs[count:])
+    step = pl.program_id(0)
+    block = acc_ref.shape[0] // 32
+    known = sorted(set(units))
+    for left, right in known:
+        steps = [t for t, unit in enumerate(units) if unit == (left, right)]
+        hit = step == steps[0]
+        for t in steps[1:]:
+            hit = jnp.logical_or(hit, step == t)
+
+        @pl.when(hit)
+        def _():
+            acc_ref[...] = mm(operands[left][...], operands[right][...], TN)
+
+    halves = ((sent_ref, 1 - place_ref[1]), (kept_ref, place_ref[1]))
+    if not scattered:
+        wide = 4 * block
+        for z, (ref, core) in itertools.product(range(4), halves):
+            row = pl.multiple_of((2 * z + core) * wide, wide)
+            ref[z * wide : (z + 1) * wide, :] = acc_ref[pl.ds(row, wide), :].astype(BF16)
+        return
+    for order, far, near, low in itertools.product(range(2), repeat=4):
+        z = place_ref[0] ^ (2 * order + low)
+        y, x = (near, far) if order else (far, near)
+        inner = (place_ref[2] ^ y) * 2 + (place_ref[3] ^ x)
+        at = (((order * 2 + far) * 2 + near) * 2 + low) * block
+        for ref, core in halves:
+            row = pl.multiple_of(((z * 2 + core) * 4 + inner) * block, block)
+            ref[at : at + block, :] = acc_ref[pl.ds(row, block), :].astype(BF16)
+
+
+def weight_grads(places, operands, specs, units, width, name, scattered=True):
+    steps = len(units)
+    tokens = operands[0].shape[0]
+    return kernel_call(
+        functools.partial(weight_grad_kernel, tuple(units), len(operands), scattered),
+        name,
+        (steps,),
+        specs,
+        [pl.BlockSpec((D // 2, width), lambda t, *_: (0, t))] * 2,
+        [((D // 2, steps * width), BF16)] * 2,
+        (places, *operands),
+        scratch=[pltpu.VMEM((D, width), F32)],
+        flops=2 * tokens * D * width * steps,
+        moved=2 * D * width * steps + 2 * tokens * D,
+        prefetch=1,
+    )
+
+
+def place_kernel(per, place_ref, *refs):
+    pieces, out_ref = (refs[:8], refs[8])
+    for index, piece in enumerate(pieces):
+        far_core, far_side, second = (index // 4, index % 2, (index // 2) % 2)
+        for near in range(2):
+            for low in range(2):
+                z = 2 * second + low
+                y, x = (near, far_side) if second else (far_side, near)
+                row = (place_ref[0] ^ z) * 2 + (place_ref[1] ^ far_core)
+                row = (row * 2 + (place_ref[2] ^ y)) * 2 + (place_ref[3] ^ x)
+                row = pl.multiple_of(row * per, per)
+                out_ref[pl.ds(row, per), :] = piece[near, low]
+
+
+def put_in_order(places, pieces):
+    near, low, per, width = pieces[0].shape
+    wide = width // 5
+    (out,) = kernel_call(
+        functools.partial(place_kernel, per),
+        "put_in_order",
+        (5,),
+        [pl.BlockSpec((near, low, per, wide), lambda t, *_: (0, 0, 0, t))] * 8,
+        [pl.BlockSpec((per * 32, wide), lambda t, *_: (0, t))],
+        [((per * 32, width), BF16)],
+        (places, *pieces),
+        moved=4 * per * 32 * width,
+        prefetch=1,
+    )
+    return out
+
+
+def total_of(*terms):
+    total = terms[0].astype(F32)
+    for term in terms[1:]:
+        total = total + term.astype(F32)
+    return total
+
+
+AXES = ("z", "core", "seq")
+
+
+class Ring:
+    def __init__(self, mesh):
+        self.count = mesh.size
+        self.seq, self.z, self.c = (lax.axis_index(a) for a in ("seq", "z", "core"))
+        self.x, self.y = (self.seq % 2, self.seq // 2)
+
+    def swap(self, array, bits):
+        return lax.ppermute(array, AXES, [(i, i ^ bits) for i in range(self.count)])
+
+
+class Gather:
+    def __init__(self, ring, shard):
+        self.ring = ring
+        self.hold = [shard] * 3
+        self.own = shard
+        self.bits = (8, 16, 24)
+
+    def launch(self):
+        self.hold = [self.ring.swap(array, bits) for array, bits in zip(self.hold, self.bits)]
+
+    def near(self):
+        self.pair = [jnp.stack([self.own, self.hold[0]]), jnp.stack(self.hold[1:])]
+        self.hold, self.bits = (list(self.pair), (1, 2))
+
+    def far(self):
+        self.pair = [jnp.stack([mine, came]) for mine, came in zip(self.pair, self.hold)]
+        self.hold, self.bits = (list(self.pair), (2, 1))
+
+    def core(self):
+        self.quad = [self.pair[0], self.hold[0], self.pair[1], self.hold[1]]
+        self.hold, self.bits = (list(self.quad), (4,) * 4)
+
+    def done(self, places):
+        return put_in_order(places, self.quad + self.hold)
+
+
+class Steps:
+    def __init__(self, ring, halves):
+        self.ring = ring
+        shape = (2, 2, 2, 2, halves[0].shape[0] // 16, halves[0].shape[1])
+        sent, self.kept = (half.reshape(shape) for half in halves)
+        self.hold, self.bits = ([sent], (4,))
+
+    def launch(self):
+        self.hold = [self.ring.swap(array, bits) for array, bits in zip(self.hold, self.bits)]
+
+    def near(self):
+        (self.got,) = self.hold
+        self.bits = (2, 1)
+        self.hold = [total_of(self.kept[i, 1], self.got[i, 1]).astype(BF16) for i in range(2)]
+
+    def far(self):
+        parts = [(self.kept[i, 0], self.got[i, 0], self.hold[i]) for i in range(2)]
+        self.bits = (1, 2)
+        self.hold = [total_of(*(p[1] for p in parts[i])).astype(BF16) for i in range(2)]
+        self.parts = [total_of(*(p[0] for p in parts[i])).astype(BF16) for i in range(2)]
+
+    def deep(self):
+        parts = [(self.parts[i], self.hold[i]) for i in range(2)]
+        self.result = total_of(*(p[0] for p in parts[0]))
+        self.bits = (8, 16, 24)
+        self.hold = [
+            total_of(*(p[step % 2] for p in parts[step // 2])).astype(BF16) for step in (1, 2, 3)
+        ]
+
+    def scatter(self):
+        parts = [total_of(self.parts[i], self.hold[i]).astype(BF16) for i in range(2)]
+        self.hold = [jnp.concatenate(parts).reshape(-1, self.kept.shape[-1])]
+
+    def launch_scatter(self):
+        self.result = lax.psum_scatter(self.hold[0], "z", scatter_dimension=0, tiled=True)
+        self.hold = []
+
+    def done(self):
+        return total_of(self.result, *self.hold)
+
+
+def at_once(*groups):
+    arrays = [group if isinstance(group, list) else group.hold for group in groups]
+    arrays = lax.optimization_barrier(arrays)
+    for group, values in zip(groups, arrays):
+        if isinstance(group, list):
+            group[:] = values
+        else:
+            group.hold = list(values)
+
+
+def whole_images(mesh, *args):
+    (
+        image_tokens, text_states, text_lengths, out_grad, norm1_gain, norm1_bias, self_qkv,
+        self_bias_qv, self_out, self_out_bias, norm2_gain, norm2_bias, cross_query, cross_kv,
+        cross_bias_qv, cross_out, cross_out_bias, norm3_gain, norm3_bias, mlp_in, mlp_in_bias,
+        mlp_out, mlp_out_bias,
+    ) = args
+    n_seq = mesh.shape["seq"]
+    ring = Ring(mesh)
+    part, text_part = (image_tokens.shape[1], text_states.shape[1])
+    rows = norm1_gain.shape[0]
+    fours = mlp_out.shape[0] // rows
+    length, prompt = (part * n_seq, text_part * n_seq)
+    places = jnp.stack([ring.z, ring.c, ring.y, ring.x]).astype(jnp.int32)
+    flat_places = places * jnp.array([0, 1, 1, 1], jnp.int32)
+
+    def gather(shard):
+        return lax.all_gather(shard, AXES, axis=0, tiled=True)
+
+    def across(vectors):
+        return jnp.concatenate([v.reshape(ring.count, -1) for v in vectors], axis=1)
+
+    def line(*vectors):
+        table = jnp.stack(vectors)
+        return jnp.pad(table, ((0, -len(vectors) % 8), (0, 0)))
+
+    in_shard = mlp_in.reshape(rows, ring.count, fours, rows).transpose(0, 2, 1, 3).reshape(rows, -1)
+    out_shard = mlp_out.reshape(fours, rows, D).transpose(1, 0, 2).reshape(rows, -1)
+    mlp = gather(jnp.concatenate([in_shard, out_shard], axis=1))
+    vectors = [
+        norm1_gain, norm1_bias, self_out_bias, norm2_gain, norm2_bias, cross_out_bias,
+        norm3_gain, norm3_bias, mlp_out_bias, self_bias_qv, cross_bias_qv, mlp_in_bias,
+    ]
+    strip = jnp.concatenate(vectors).reshape(-1, rows)
+    strip = jnp.pad(strip, ((0, 128 - strip.shape[0]), (0, 0))).T
+    w_first = Gather(ring, jnp.concatenate([self_qkv, strip], axis=1))
+    w_second = Gather(
+        ring, jnp.concatenate([self_out, cross_query, cross_kv, cross_out], axis=1)
+    )
+    w_first.launch()
+    now = [
+        lax.all_to_all(
+            jnp.concatenate([image_tokens, text_states], axis=1), "seq", 0, 0, tiled=True
+        )
+    ]
+    at_once(now, w_first)
+    (moved,) = now
+    w_first.near()
+    at_once(w_first, w_second)
+    w_first.launch()
+    w_second.launch()
+    at_once(w_first)
+    w_first.far()
+    w_first.launch()
+    at_once(w_first, w_second)
+    w_first.core()
+    w_second.near()
+    at_once(w_first, w_second)
+    w_first.launch()
+    w_second.launch()
+    at_once(w_first)
+    first = w_first.done(places)
+
+    tokens = moved[:, :part].reshape(length, D)
+    texts = moved[:, part:].reshape(prompt, D)
+    prompt_length = lax.dynamic_slice_in_dim(text_lengths, ring.seq, 1, 0)
+
+    table = lax.optimization_barrier(first[:, 3 * D :]).T.astype(F32)
+    full, at = ([], 0)
+    for v in vectors[:-1]:
+        wide = v.shape[0] // rows
+        full.append(table[at : at + wide].reshape(wide, -1, rows).transpose(1, 0, 2).reshape(-1))
+        at += wide
+    bias_in = table[at : at + fours].reshape(fours, 1, D)
+    (g1, b1, bias_out, g2, b2, bias_cross, g3, b3, bias_last, bias_qv, bias_qv2) = full
+    zero = jnp.zeros((D,), F32)
+
+    tile = min(QB, length)
+    grid = (length // tile,)
+    row_tile = pl.BlockSpec((tile, D), lambda i, *_: (i, 0))
+    vec8, vec1 = (whole((8, D)), whole((1, D)))
+    sum8 = pl.BlockSpec((8, D), lambda *_: (0, 0))
+    square = (D, D)
+    flat = (length, D)
+
+    def weight_block(index):
+        return whole(square, (0, index))
+
+    def streamed(offset):
+        return pl.BlockSpec(square, lambda t, *_: (0, t + offset))
+
+    def columns(width):
+        return pl.BlockSpec((tile, width), lambda i, *_: (i, 0))
+
+    stat_tile = pl.BlockSpec((HEADS, tile), lambda i, *_: (0, i))
+    unit = 2 * length * D * D
+
+    h1, qkv = kernel_call(
+        qkv_kernel, "qkv", grid,
+        [row_tile, whole((D, 3 * D)), vec8],
+        [row_tile, columns(3 * D)],
+        [(flat, BF16), ((length, 3 * D), BF16)],
+        (tokens, first, line(g1, b1, bias_qv[:D], zero, bias_qv[D:])),
+        flops=3 * unit, moved=16 * length * D,
+    )
+    now = [qkv, h1]
+    at_once(now, w_second)
+    w_second.far()
+    at_once(now, w_second)
+    qkv, h1 = now
+    w_second.launch()
+    o1, lse1 = attend(qkv)
+    now = [o1]
+    at_once(now, w_second)
+    w_second.core()
+    w_second.launch()
+    at_once(now, w_second)
+    (o1,) = now
+    second = w_second.done(places)
+    kv2 = (mm(texts, second[:, 2 * D : 4 * D]) + jnp.concatenate([zero, bias_qv2[D:]])).astype(BF16)
+    x1, h2, q2, o2, x2, h3, lse2 = kernel_call(
+        cross_kernel, "cross", grid,
+        [row_tile, row_tile, weight_block(0), weight_block(1), weight_block(4),
+         whole((prompt, 2 * D)), vec8],
+        [row_tile] * 6 + [stat_tile],
+        [(flat, F32), (flat, BF16), (flat, BF16), (flat, BF16), (flat, F32), (flat, BF16),
+         ((HEADS, length), F32)],
+        (prompt_length, tokens, o1, second, second, second, kv2,
+         line(bias_out, g2, b2, bias_qv2[:D], bias_cross, g3, b3)),
+        flops=5 * unit, moved=30 * length * D, prefetch=1,
+    )
+    out_grad, h3 = lax.optimization_barrier((out_grad, h3))
+    grad_rows = lax.all_to_all(out_grad, "seq", 0, 0, tiled=True).reshape(flat)
+    hidden = (length, fours * D)
+    by_unit = pl.BlockSpec((length, D), lambda t, *_: (0, t))
+    act, slope, out = kernel_call(
+        mlp_kernel, "mlp", (fours,),
+        [whole(flat), streamed(0), streamed(fours),
+         pl.BlockSpec((1, 1, D), lambda t, *_: (t, 0, 0)), whole(flat), vec1],
+        [by_unit, by_unit, whole(flat, single=False)],
+        [(hidden, BF16), (hidden, BF16), (flat, BF16)],
+        (h3, mlp, mlp, bias_in, x2, bias_last.reshape(1, D)),
+        scratch=[pltpu.VMEM(flat, F32)],
+        flops=2 * fours * unit, moved=40 * length * D,
+    )
+
+    now = [out, act, slope, grad_rows]
+    at_once(now)
+    out, act, slope, grad_rows = now
+    leaving_out = [lax.all_to_all(out.reshape(n_seq, part, D), "seq", 0, 0, tiled=True)]
+    full_flat = whole(flat)
+    du, du_sum = kernel_call(
+        du_kernel, "du", (fours,),
+        [full_flat, streamed(fours), by_unit],
+        [by_unit, pl.BlockSpec((1, 1, D), lambda t, *_: (t, 0, 0))],
+        [(hidden, BF16), ((fours, 1, D), F32)],
+        (grad_rows, mlp, slope),
+        flops=fours * unit, moved=26 * length * D,
+    )
+    last = fours - 1
+    r_mlp = Steps(
+        ring,
+        weight_grads(
+            flat_places,
+            (act, grad_rows, h3, du),
+            [
+                pl.BlockSpec((length, D), lambda t, *_: (0, jnp.minimum(t, last))),
+                full_flat,
+                full_flat,
+                pl.BlockSpec((length, D), lambda t, *_: (0, jnp.maximum(t - fours, 0))),
+            ],
+            [(0, 1)] * fours + [(2, 3)] * fours,
+            D,
+            "d_mlp",
+        ),
+    )
+    now = [du]
+    at_once(now, leaving_out, r_mlp)
+    (du,) = now
+    (block_output,) = leaving_out
+    r_mlp.launch()
+    dx2, dc, do2, sums3 = kernel_call(
+        norm3_kernel, "norm3_back", grid,
+        [columns(fours * D), whole((D, fours * D)), row_tile, row_tile, vec1, weight_block(4)],
+        [row_tile] * 3 + [sum8],
+        [(flat, F32), (flat, BF16), (flat, BF16), ((8, D), F32)],
+        (du, mlp, grad_rows, x2, g3.reshape(1, D), second),
+        flops=(fours + 1) * unit, moved=32 * length * D,
+    )
+    now = [dx2, dc, do2]
+    at_once(now, r_mlp)
+    r_mlp.near()
+    at_once(now, r_mlp)
+    r_mlp.launch()
+    dx2, dc, do2 = now
+    dq2, dkv2, dx1, da, do1, sums2 = kernel_call(
+        cross_back_kernel, "cross_back", grid,
+        [row_tile, whole((prompt, 2 * D)), row_tile, row_tile, stat_tile,
+         weight_block(1), weight_block(0), row_tile, row_tile, vec1],
+        [row_tile, whole((prompt, 2 * D), single=False), row_tile, row_tile, row_tile, sum8],
+        [(flat, BF16), ((prompt, 2 * D), BF16), (flat, F32), (flat, BF16), (flat, BF16), ((8, D), F32)],
+        (prompt_length, q2, kv2, o2, do2, lse2, second, second, x1, dx2, g2.reshape(1, D)),
+        scratch=[pltpu.VMEM((prompt, 2 * D), F32)],
+        flops=5 * unit, moved=34 * length * D, prefetch=1,
+    )
+    text_block = [whole((prompt, D), (0, i)) for i in range(2)]
+    r_mid = Steps(
+        ring,
+        weight_grads(
+            flat_places,
+            (o1, da, o2, dc, h2, dq2, texts, dkv2, dkv2),
+            [full_flat] * 6 + [whole((prompt, D))] + text_block,
+            [(0, 1), (2, 3), (4, 5), (6, 7), (6, 8)],
+            D,
+            "d_mid",
+        ),
+    )
+    now = [do1, dx1, dkv2]
+    at_once(now, r_mid, r_mlp)
+    r_mlp.far()
+    at_once(now, r_mid, r_mlp)
+    do1, dx1, dkv2 = now
+    r_mid.launch()
+    r_mlp.launch()
+    count = HEADS // 4
+    back_a = list(attend_back(qkv, o1, do1, lse1, 0, count))
+    now = [do1]
+    at_once(now, back_a, r_mid, r_mlp)
+    r_mid.near()
+    r_mlp.scatter()
+    at_once(now, back_a, r_mid, r_mlp)
+    (do1,) = now
+    r_mid.launch()
+    r_mlp.launch_scatter()
+    narrow = [full_flat] + [whole((length, count * PAIR))] * 3
+    units = [(0, 1), (0, 2), (0, 3)]
+    r_a = Steps(ring, weight_grads(places, (h1, *back_a), narrow, units, count * PAIR, "d_qkv_a"))
+    now = [do1]
+    at_once(now, r_a)
+    r_a.launch()
+    back_b = list(attend_back(qkv, o1, now[0], lse1, count, count))
+    at_once(back_b, r_a, r_mid)
+    r_mid.far()
+    r_a.near()
+    at_once(back_b, r_a, r_mid)
+    r_mid.launch()
+    r_a.launch()
+    r_b = Steps(ring, weight_grads(places, (h1, *back_b), narrow, units, count * PAIR, "d_qkv_b"))
+    at_once(back_b, r_a, r_b, r_mid)
+    r_mid.scatter()
+    r_a.far()
+    dv2_sum = jnp.sum(dkv2[:, D:].astype(F32), axis=0)
+    early = [
+        sums2[2], sums2[0], sums2[1], sums3[2], sums3[0], sums3[1], sums3[3],
+        jnp.concatenate([sums2[3], dv2_sum]),
+        du_sum.reshape(fours, ring.count, rows).transpose(1, 0, 2).reshape(-1),
+    ]
+    early = [across(early)]
+    text_grad = mm(dkv2, second[:, 2 * D : 4 * D], NT).astype(BF16)
+    at_once(back_b, r_a, r_b, r_mid, early)
+    r_b.launch()
+    r_a.launch()
+    r_mid.launch_scatter()
+    early = [lax.all_to_all(early[0], AXES, 0, 0, tiled=True)]
+    image_grad, sums1 = kernel_call(
+        norm1_kernel, "norm1_back", grid,
+        [columns(count * PAIR)] * 6 + [whole((D, 3 * D)), row_tile, row_tile, vec1],
+        [row_tile, sum8],
+        [(flat, BF16), ((8, D), F32)],
+        (*back_a, *back_b, first, tokens, dx1, g1.reshape(1, D)),
+        flops=3 * unit, moved=18 * length * D,
+    )
+    now = [image_grad, text_grad, sums1]
+    at_once(now, r_a, r_b, early)
+    image_grad, text_grad, sums1 = now
+    r_b.near()
+    leaving = jnp.concatenate(
+        [image_grad.reshape(n_seq, part, D), text_grad.reshape(n_seq, text_part, D)], axis=1
+    )
+    now = [leaving]
+    at_once(now, r_b)
+    r_b.launch()
+    (leaving,) = now
+    leaving = [lax.all_to_all(leaving, "seq", 0, 0, tiled=True)]
+    at_once(r_b, r_a)
+    r_a.deep()
+    r_b.far()
+    late = [across([sums1[0], sums1[1], jnp.concatenate([sums1[2], sums1[3]])])]
+    at_once(r_a, r_b, late)
+    r_b.launch()
+    r_a.launch()
+    at_once(r_b, leaving, late)
+    late = lax.all_to_all(late[0], AXES, 0, 0, tiled=True)
+    r_b.deep()
+    r_b.launch()
+    leaving = leaving[0].astype(F32)
+    mlp_grad = r_mlp.done()
+    mlp_out_grad = mlp_grad[:, : fours * D].reshape(rows, fours, D).transpose(1, 0, 2).reshape(-1, D)
+    mlp_in_grad = mlp_grad[:, fours * D :].reshape(rows, fours, ring.count, rows)
+    mlp_in_grad = mlp_in_grad.transpose(0, 2, 1, 3).reshape(rows, -1)
+    mid, last_a, last_b = (r_mid.done(), r_a.done(), r_b.done())
+    wide = count * PAIR
+    self_qkv_grad = jnp.concatenate(
+        [half[:, i * wide : (i + 1) * wide] for i in range(3) for half in (last_a, last_b)], axis=1
+    )
+
+    small = jnp.concatenate([jnp.sum(early[0], axis=0), jnp.sum(late, axis=0)])
+
+    def mine(total, at, wide):
+        return total[at * rows : at * rows + wide]
+
+    two = 2 * rows
+    return (
+        block_output,
+        leaving[:, :part],
+        leaving[:, part:],
+        mine(small, 9 + fours, rows),
+        mine(small, 10 + fours, rows),
+        self_qkv_grad,
+        mine(small, 11 + fours, two),
+        mid[:, :D],
+        mine(small, 0, rows),
+        mine(small, 1, rows),
+        mine(small, 2, rows),
+        mid[:, 2 * D : 3 * D],
+        mid[:, 3 * D :],
+        mine(small, 7, two),
+        mid[:, D : 2 * D],
+        mine(small, 3, rows),
+        mine(small, 4, rows),
+        mine(small, 5, rows),
+        mlp_in_grad,
+        mine(small, 9, fours * rows),
+        mlp_out_grad,
+        mine(small, 6, rows),
+    )
+
+
+def places_of(images, rows):
+    ins = (
+        P(images, "seq", None),
+        P(images, "seq", None),
+        P(images),
+        P(images, "seq", None),
+        P(rows),
+        P(rows),
+        P(rows, None),
+        P(rows),
+        P(rows, None),
+        P(rows),
+        P(rows),
+        P(rows),
+        P(rows, None),
+        P(rows, None),
+        P(rows),
+        P(rows, None),
+        P(rows),
+        P(rows),
+        P(rows),
+        P(rows, None),
+        P(rows),
+        P(rows, None),
+        P(rows),
+    )
+    outs = (
+            P(images, "seq", None),
+            P(images, "seq", None),
+            P(images, "seq", None),
+            P(rows),
+            P(rows),
+            P(rows, None),
+            P(rows),
+            P(rows, None),
+            P(rows),
+            P(rows),
+            P(rows),
+            P(rows, None),
+            P(rows, None),
+            P(rows),
+            P(rows, None),
+            P(rows),
+            P(rows),
+            P(rows),
+            P(rows, None),
+            P(rows),
+            P(rows, None),
+            P(rows),
+        )
+    return (ins, outs)
+
+
 def solution(mesh):
-    placed = (
-        P("dp", "seq", None),
-        P("dp", "seq", None),
-        P("dp"),
-        P("dp", "seq", None),
-        P(("dp", "seq")),
-        P(("dp", "seq")),
-        P(("dp", "seq"), None),
-        P(("dp", "seq")),
-        P(("dp", "seq"), None),
-        P(("dp", "seq")),
-        P(("dp", "seq")),
-        P(("dp", "seq")),
-        P(("dp", "seq"), None),
-        P(("dp", "seq"), None),
-        P(("dp", "seq")),
-        P(("dp", "seq"), None),
-        P(("dp", "seq")),
-        P(("dp", "seq")),
-        P(("dp", "seq")),
-        P(("dp", "seq"), None),
-        P(("dp", "seq")),
-        P(("dp", "seq"), None),
-        P(("dp", "seq")),
-    )
-    return jax.shard_map(
-        per_device,
-        mesh=mesh,
-        in_specs=placed,
-        out_specs=(
-            P("dp", "seq", None),
-            P("dp", "seq", None),
-            P("dp", "seq", None),
-            P(("dp", "seq")),
-            P(("dp", "seq")),
-            P(("dp", "seq"), None),
-            P(("dp", "seq")),
-            P(("dp", "seq"), None),
-            P(("dp", "seq")),
-            P(("dp", "seq")),
-            P(("dp", "seq")),
-            P(("dp", "seq"), None),
-            P(("dp", "seq"), None),
-            P(("dp", "seq")),
-            P(("dp", "seq"), None),
-            P(("dp", "seq")),
-            P(("dp", "seq")),
-            P(("dp", "seq")),
-            P(("dp", "seq"), None),
-            P(("dp", "seq")),
-            P(("dp", "seq"), None),
-            P(("dp", "seq")),
-        ),
-        check_vma=False,
-    )
+    n_dp, n_seq = (mesh.shape["dp"], mesh.shape["seq"])
+    spread = places_of("dp", ("dp", "seq"))
+    single = places_of(("z", "core"), AXES)
+
+    def layer(*args):
+        images = args[0].shape[0] // n_dp
+        if images == n_seq and (n_dp, n_seq) == (8, 4):
+            fine = Mesh(mesh.devices.reshape(n_dp // 2, 2, n_seq), AXES)
+            plan, place, grid = (functools.partial(whole_images, fine), single, fine)
+        else:
+            plan, place, grid = (per_device, spread, mesh)
+        return jax.shard_map(
+            plan, mesh=grid, in_specs=place[0], out_specs=place[1], check_vma=False
+        )(*args)
+
+    return layer

time: 2890 us -> 635 us (0.22)
  waiting for transfers between devices: 1990 us -> 127 us
  matrix products: 428 us -> 7.4 us
  Pallas kernels: 0 us -> 285 us
  local copies, waits for them, and re-layouts: 253 us -> 58.5 us
  blocking collectives: 106 us -> 0 us
  starting transfers between devices: 1.51 us -> 76.7 us
    reduce_scatter x10 -> x2, waiting for transfers between devices: 1410 us -> 0.01 us  [launch_scatter(): lax.psum_scatter(self.hold[0], 'z', scatter_dimension=0, tiled=True)]
    dot_general x99 -> x2, matrix products: 428 us -> 7.4 us  [mm(): return lax.dot_general(left, right, dims, preferred_element_type=F32)]
    all_gather x11 -> x1, waiting for transfers between devices: 356 us -> 0.01 us  [gather(): return lax.all_gather(shard, AXES, axis=0, tiled=True)]
    pallas_call x0 -> x16, Pallas kernels: none -> 285 us  [kernel_call(): pl.pallas_call(body, grid_spec=pltpu.PrefetchScalarGridSpec(num_scalar_pr...]
    unnamed x25 -> x3, waiting for transfers between devices: 224 us -> 0.05 us
    ppermute x0 -> x48, waiting for transfers between devices: none -> 122 us  [swap(): return lax.ppermute(array, AXES, [(i, i ^ bits) for i in range(self.count)])]
    convert_element_type x11 -> x0, local copies, waits for them, and re-layouts: 104 us -> none  [the longest x2 41.8 us: per_device(): grad_key_all.astype(jnp.bfloat16)]
    all_gather x1 -> x0, blocking collectives: 65.8 us -> none  [gather_mlp(): lax.all_gather(bias_in, ('dp', 'seq'), axis=0, tiled=True)]
  transfers between devices with their start and end apart: 23 -> 57, of which waited for: 18 -> 24; matrix products, arithmetic and copies ran while one was open for 23% -> 13% of each run, Pallas kernels for 0% -> 44%
where the time goes in v2:
time: 635 us; the launch traced here: 630 us
  Pallas kernels  285 us (45%)
  waiting for transfers between devices  127 us (20%)
  starting transfers between devices  76.7 us (12%)
  other arithmetic  61.8 us (10%)
  local copies, waits for them, and re-layouts  58.5 us (9%)
  between operations  14.7 us (2%)
  matrix products  7.4 us (1%)
    pallas_call x16, Pallas kernels, kernel_call(): pl.pallas_call(body, grid_spec=pltpu.PrefetchScalarGridSpec(num_scalar_pr...  285 us
    ppermute x48, waiting for transfers between devices, swap(): return lax.ppermute(array, AXES, [(i, i ^ bits) for i in range(self.count)])  122 us
    ppermute x48, starting transfers between devices, swap(): return lax.ppermute(array, AXES, [(i, i ^ bits) for i in range(self.count)])  49.1 us
  transfers between devices with their start and end apart: 57, of which 24 were waited for; matrix products, arithmetic and copies ran while one was open for 13% of the time, Pallas kernels for 44%

profile of v2, /device:TPU:0, one launch (start us, length us, event | category | flops | bytes accessed | tf_op | source)
XLA Modules:
  0.0 630.2 jit_solution(1105297556960232114)
XLA Ops:
  14.1 2.6 pad_maximum_fusion
  16.8 5.5 all-to-all-start
  22.7 3.7 collective-permute-start.2
  30.6 4.6 collective-permute-done.2
  35.2 15.5 %collective-permute-done.1 = bf16[32,3200]{1,0:T(8,128)(2,1)S(1)} collective-permute-done((bf16[32,3200]{1,0:T(8,128)(2,1)S(1)}, bf16[32,3200]{1,0:T(8,128)(2,1)S(1)}, u32[]{:S(2)}, u32[]{:S(2)}) %collective-permute-start.1) | collective-permute-done | bytes 204832 | tf_op jit(solution)/shard_map/ppermute | solution.py:898
  50.8 2.9 all-to-all-done
  54.8 3.7 collective-permute-start.3
  60.0 15.3 %collective-permute-done.3 = bf16[2,32,3200]{2,1,0:T(8,128)(2,1)S(1)} collective-permute-done((bf16[2,32,3200]{2,1,0:T(8,128)(2,1)S(1)}, bf16[2,32,3200]{2,1,0:T(8,128)(2,1)S(1)}, u32[]{:S(2)}, u32[]{:S(2)}) %collective-permute-start.3) | collective-permute-done | bytes 409632 | tf_op jit(solution)/shard_map/ppermute | solution.py:898
  79.7 3.1 collective-permute-start.8
  84.1 19.2 %collective-permute-done.7 = bf16[32,5120]{1,0:T(8,128)(2,1)S(1)} collective-permute-done((bf16[32,5120]{1,0:T(8,128)(2,1)S(1)}, bf16[32,5120]{1,0:T(8,128)(2,1)S(1)}, u32[]{:S(2)}, u32[]{:S(2)}) %collective-permute-start.7) | collective-permute-done | bytes 327712 | tf_op jit(solution)/shard_map/ppermute | solution.py:898
  103.3 9.5 %collective-permute-done.8 = bf16[32,5120]{1,0:T(8,128)(2,1)S(1)} collective-permute-done((bf16[32,5120]{1,0:T(8,128)(2,1)S(1)}, bf16[32,5120]{1,0:T(8,128)(2,1)S(1)}, u32[]{:S(2)}, u32[]{:S(2)}) %collective-permute-start.8) | collective-permute-done | bytes 327712 | tf_op jit(solution)/shard_map/ppermute | solution.py:898
  122.5 8.1 %put_in_order.2.w_ref.refs_6_ = bf16[1024,3200]{1,0:T(8,128)(2,1)} custom-call(s32[4]{0:T(128)} %get-tuple-element.401.place_ref, bf16[2,2,32,3200]{3,2,1,0:T(8,128)(2,1)} %pad_maximum_fusion.6.refs_0_, bf16[2,2,32,3200]{3,2,1,0:T(8,128)(2,1)} %collective-permute-done.5.refs_1_, bf16[2,2,32,3200]{3,2,1,0:T(8,128)(2,1)} %copy-done.1, ...), custom_call_target="tpu_custom_call" | custom-call | bytes 409600 | tf_op jit(solution)/shard_map/put_in_order/pallas_call | solution.py:437
  132.9 12.5 %qkv.1 = (bf16[1024,1024]{1,0:T(8,128)(2,1)}, bf16[1024,3072]{1,0:T(8,128)(2,1)}) custom-call(bf16[1024,1024]{1,0:T(8,128)(2,1)} %bitcast.202, bf16[1024,3200]{1,0:T(8,128)(2,1)} %put_in_order.2.w_ref.refs_6_, f32[8,1024]{1,0:T(8,128)} %pad.14.vec_ref), custom_call_target="tpu_custom_call" | custom-call | flops 201326592 | bytes 524288 | tf_op jit(solution)/shard_map/qkv/pallas_call | solution.py:437
  145.4 4.3 collective-permute-done.14
  151.3 2.3 pad_maximum_fusion.3.refs_0_
  153.5 2.4 pad_maximum_fusion.4.refs_2_
  158.3 23.3 %attend.1 = (bf16[1024,1024]{1,0:T(8,128)(2,1)}, f32[8,2,1024]{2,1,0:T(2,128)}) custom-call(bf16[1024,3072]{1,0:T(8,128)(2,1)} %get-tuple-element.237.q_ref.k_ref.v_ref, bf16[1024,3072]{1,0:T(8,128)(2,1)} %get-tuple-element.237.q_ref.k_ref.v_ref, bf16[1024,3072]{1,0:T(8,128)(2,1)} %get-tuple-element.237.q_ref.k_ref.v_ref), custom_call_target="tpu_custom_call" | custom-call | flops 268435456 | bytes 262144 | tf_op jit(solution)/shard_map/attend/pallas_call | solution.py:437
  181.6 11.1 %collective-permute-done.16.refs_1_ = bf16[2,2,32,5120]{3,2,1,0:T(8,128)(2,1)} collective-permute-done((bf16[2,2,32,5120]{3,2,1,0:T(8,128)(2,1)}, bf16[2,2,32,5120]{3,2,1,0:T(8,128)(2,1)}, u32[]{:S(2)}, u32[]{:S(2)}) %collective-permute-start.16) | collective-permute-done | bytes 1310752 | tf_op jit(solution)/shard_map/ppermute | solution.py:898
  196.2 1.9 collective-permute-done.21.refs_7_
  198.0 10.4 %put_in_order.3.ws_ref.wq_ref.wc_ref = bf16[1024,5120]{1,0:T(8,128)(2,1)} custom-call(s32[4]{0:T(128)} %get-tuple-element.401.place_ref, bf16[2,2,32,5120]{3,2,1,0:T(8,128)(2,1)} %pad_maximum_fusion.3.refs_0_, bf16[2,2,32,5120]{3,2,1,0:T(8,128)(2,1)} %collective-permute-done.16.refs_1_, bf16[2,2,32,5120]{3,2,1,0:T(8,128)(2,1)} %pad_maximum_fusion.4.refs_2_, ...), custom_call_target="tpu_custom_call" | custom-call | bytes 655360 | tf_op jit(solution)/shard_map/put_in_order/pallas_call | solution.py:437
  208.4 3.7 fusion.7.kv_ref
  212.1 18.4 %cross.1 = (f32[1024,1024]{1,0:T(8,128)}, bf16[1024,1024]{1,0:T(8,128)(2,1)}, bf16[1024,1024]{1,0:T(8,128)(2,1)}, bf16[1024,1024]{1,0:T(8,128)(2,1)}, f32[1024,1...) custom-call(s32[1]{0:T(128)} %dynamic_slice.3.len_ref, bf16[1024,1024]{1,0:T(8,128)(2,1)} %bitcast.203, ...), custom_call_target="tpu_custom_call" | custom-call | flops 335544320 | bytes 983040 | tf_op jit(solution)/shard_map/cross/pallas_call | solution.py:437
  230.5 3.8 all-to-all-start.1
  235.6 37.7 %mlp.1 = (bf16[1024,4096]{1,0:T(8,128)(2,1)}, bf16[1024,4096]{1,0:T(8,128)(2,1)}, bf16[1024,1024]{1,0:T(8,128)(2,1)}) custom-call(bf16[1024,1024]{1,0:T(8,128)(2,1)} %get-tuple-element.250.h_ref.refs_2_, bf16[1024,8192]{1,0:T(8,128)(2,1)} %all-gather.2.cloned.1.call-done.wi_ref.wo_ref, bf16[1024,8192]{1,0:T(8,128)(2,1)} %all-gather.2.cloned.1.call-done.wi_ref.wo_ref, ...), custom_call_target="tpu_custom_call" | custom-call | flops 536870912 | bytes 1310720 | tf_op jit(solution)/shard_map/mlp/pallas_call | solution.py:437
  274.6 4.5 all-to-all-start.2
  279.6 15.2 %du.1 = (bf16[1024,4096]{1,0:T(8,128)(2,1)}, f32[4,1,1024]{2,1,0:T(1,128)}) custom-call(bf16[1024,1024]{1,0:T(8,128)(2,1)} %bitcast.205, bf16[1024,8192]{1,0:T(8,128)(2,1)} %all-gather.2.cloned.1.call-done.wi_ref.wo_ref, bf16[1024,4096]{1,0:T(8,128)(2,1)} %get-tuple-element.257.slope_ref), custom_call_target="tpu_custom_call" | custom-call | flops 268435456 | bytes 851968 | tf_op jit(solution)/shard_map/du/pallas_call | solution.py:437
  294.8 26.6 %d_mlp.1 = (bf16[512,8192]{1,0:T(8,128)(2,1)}, bf16[512,8192]{1,0:T(8,128)(2,1)}) custom-call(s32[4]{0:T(128)} %get-tuple-element.400.place_ref, bf16[1024,4096]{1,0:T(8,128)(2,1)} %get-tuple-element.260.refs_0_, bf16[1024,1024]{1,0:T(8,128)(2,1)} %bitcast.206, bf16[1024,1024]{1,0:T(8,128)(2,1)} %get-tuple-element.250.h_ref.refs_2_, ...), custom_call_target="tpu_custom_call" | custom-call | flops 536870912 | bytes 589824 | tf_op jit(solution)/shard_map/d_mlp/pallas_call | solution.py:437
  321.5 21.2 %norm3_back.1 = (f32[1024,1024]{1,0:T(8,128)}, bf16[1024,1024]{1,0:T(8,128)(2,1)}, bf16[1024,1024]{1,0:T(8,128)(2,1)}, f32[8,1024]{1,0:T(8,128)}) custom-call(bf16[1024,4096]{1,0:T(8,128)(2,1)} %get-tuple-element.266.refs_3_.du_ref, bf16[1024,8192]{1,0:T(8,128)(2,1)} %all-gather.2.cloned.1.call-done.wi_ref.wo_ref, bf16[1024,1024]{1,0:T(8,128)(2,1)} %bitcast.207, ...), custom_call_target="tpu_custom_call" | custom-call | flops 335544320 | bytes 1048576 | tf_op jit(solution)/shard_map/norm3_back/pallas_call | solution.py:437
  342.7 4.9 fusion.11
  347.7 1.9 collective-permute-start.23
  351.0 24.8 %cross_back.1 = (bf16[1024,1024]{1,0:T(8,128)(2,1)}, bf16[128,2048]{1,0:T(8,128)(2,1)}, f32[1024,1024]{1,0:T(8,128)}, bf16[1024,1024]{1,0:T(8,128)(2,1)}, bf16[1024,1024]{1,0:T(8,128)(2,1)}, /*index=5*/f32[8,1024]{1,0:T(8,128)}) custom-call(s32[1]{0:T(128)} %dynamic_slice.3.len_ref, bf16[1024,1024]{1,0:T(8,128)(2,1)} %get-tuple-element.264.q_ref, ...), custom_call_target="tpu_custom_call" | custom-call | flops 335544320 | bytes 1114112 | tf_op jit(solution)/shard_map/cross_back/pallas_call | solution.py:437
  375.8 17.1 %d_mid.1 = (bf16[512,5120]{1,0:T(8,128)(2,1)}, bf16[512,5120]{1,0:T(8,128)(2,1)}) custom-call(s32[4]{0:T(128)} %get-tuple-element.400.place_ref, bf16[1024,1024]{1,0:T(8,128)(2,1)} %get-tuple-element.244.o_ref.refs_0_, bf16[1024,1024]{1,0:T(8,128)(2,1)} %get-tuple-element.283.refs_1_, bf16[1024,1024]{1,0:T(8,128)(2,1)} %get-tuple-element.265.o_ref.refs_2_, ...), custom_call_target="tpu_custom_call" | custom-call | flops 335544320 | bytes 393216 | tf_op jit(solution)/shard_map/d_mid/pallas_call | solution.py:437
  392.9 3.1 collective-permute-done.23
  398.6 4.9 fusion.14
  405.5 18.6 %attend_back.2 = (bf16[1024,512]{1,0:T(8,128)(2,1)}, bf16[1024,512]{1,0:T(8,128)(2,1)}, bf16[1024,512]{1,0:T(8,128)(2,1)}) custom-call(bf16[1024,3072]{1,0:T(8,128)(2,1)} %get-tuple-element.237.q_ref.k_ref.v_ref, bf16[1024,3072]{1,0:T(8,128)(2,1)} %get-tuple-element.237.q_ref.k_ref.v_ref, bf16[1024,3072]{1,0:T(8,128)(2,1)} %get-tuple-element.237.q_ref.k_ref.v_ref, ...), custom_call_target="tpu_custom_call" | custom-call | flops 335544320 | bytes 262144 | tf_op jit(solution)/shard_map/attend_back/pallas_call | solution.py:437
  424.1 5.3 collective-permute-done.26
  430.6 4.4 add_convert_fusion.5
  436.5 4.2 fusion.17
  440.7 8.6 %d_qkv_a.1 = (bf16[512,1536]{1,0:T(8,128)(2,1)}, bf16[512,1536]{1,0:T(8,128)(2,1)}) custom-call(s32[4]{0:T(128)} %get-tuple-element.401.place_ref, bf16[1024,1024]{1,0:T(8,128)(2,1)} %get-tuple-element.263.refs_0_, bf16[1024,512]{1,0:T(8,128)(2,1)} %get-tuple-element.312.refs_1_.refs_0_, bf16[1024,512]{1,0:T(8,128)(2,1)} %get-tuple-element.313.refs_2_.refs_1_, ...), custom_call_target="tpu_custom_call" | custom-call | flops 100663296 | bytes 163840 | tf_op jit(solution)/shard_map/d_qkv_a/pallas_call | solution.py:437
  450.4 18.7 %attend_back.3 = (bf16[1024,512]{1,0:T(8,128)(2,1)}, bf16[1024,512]{1,0:T(8,128)(2,1)}, bf16[1024,512]{1,0:T(8,128)(2,1)}) custom-call(bf16[1024,3072]{1,0:T(8,128)(2,1)} %get-tuple-element.237.q_ref.k_ref.v_ref, bf16[1024,3072]{1,0:T(8,128)(2,1)} %get-tuple-element.237.q_ref.k_ref.v_ref, bf16[1024,3072]{1,0:T(8,128)(2,1)} %get-tuple-element.237.q_ref.k_ref.v_ref, ...), custom_call_target="tpu_custom_call" | custom-call | flops 335544320 | bytes 262144 | tf_op jit(solution)/shard_map/attend_back/pallas_call | solution.py:437
  469.1 11.6 %collective-permute-done.29 = bf16[2,2,32,5120]{3,2,1,0:T(8,128)(2,1)S(1)} collective-permute-done((bf16[2,2,32,5120]{3,2,1,0:T(8,128)(2,1)}, bf16[2,2,32,5120]{3,2,1,0:T(8,128)(2,1)S(1)}, u32[]{:S(2)}, u32[]{:S(2)}) %collective-permute-start.29) | collective-permute-done | bytes 1310752 | tf_op jit(solution)/shard_map/ppermute | solution.py:898
  482.0 3.4 fusion.20
  495.8 8.9 %d_qkv_b.1 = (bf16[512,1536]{1,0:T(8,128)(2,1)}, bf16[512,1536]{1,0:T(8,128)(2,1)}) custom-call(s32[4]{0:T(128)} %get-tuple-element.401.place_ref, bf16[1024,1024]{1,0:T(8,128)(2,1)} %get-tuple-element.263.refs_0_, bf16[1024,512]{1,0:T(8,128)(2,1)} %get-tuple-element.351.refs_1_.refs_3_, bf16[1024,512]{1,0:T(8,128)(2,1)} %get-tuple-element.352.refs_2_.refs_4_, ...), custom_call_target="tpu_custom_call" | custom-call | flops 100663296 | bytes 163840 | tf_op jit(solution)/shard_map/d_qkv_b/pallas_call | solution.py:437
  504.7 6.1 collective-permute-done.31
  510.8 2.3 fusion.33
  513.1 2.9 add_convert_fusion.7
  517.9 5.3 all-to-all-start.3
  523.3 1.8 collective-permute-start.35
  526.6 3.7 fusion.22
  530.3 14.4 %norm1_back.1 = (bf16[1024,1024]{1,0:T(8,128)(2,1)}, f32[8,1024]{1,0:T(8,128)}) custom-call(bf16[1024,512]{1,0:T(8,128)(2,1)} %get-tuple-element.312.refs_1_.refs_0_, bf16[1024,512]{1,0:T(8,128)(2,1)} %get-tuple-element.313.refs_2_.refs_1_, bf16[1024,512]{1,0:T(8,128)(2,1)} %get-tuple-element.314.refs_3_.refs_2_, ...), custom_call_target="tpu_custom_call" | custom-call | flops 201326592 | bytes 589824 | tf_op jit(solution)/shard_map/norm1_back/pallas_call | solution.py:437
  544.8 3.9 pad_maximum_fusion.1
  554.1 3.9 all-to-all-start.4
  565.5 2.5 fusion.30
  569.2 2.3 collective-permute-start.43
  572.5 1.9 fusion.53
  576.8 2.0 reshape.385
  578.8 4.7 copy.83
  583.6 4.5 reshape.386
  596.1 2.5 slice.682
  598.6 4.0 all-to-all-start.5
  603.6 1.8 collective-permute-start.45
  605.5 2.5 collective-permute-start.46
  611.1 5.2 collective-permute-done.46
  620.4 3.1 copy.105
  (292 shorter events, 101.0 us)
Async XLA Ops:
  7.2 228.4 %all-gather.2.cloned.1.call-start = ((), (), s32[]{:S(2)}) async-start(), calls=%async_computation.8 | async-start | bytes 17301504 | tf_op jit(solution)/shard_map/all_gather | solution.py:995
  16.8 36.9 %all-to-all-start = ((bf16[4,288,1024]{2,1,0:T(8,128)(2,1)}), bf16[4,288,1024]{2,1,0:T(8,128)(2,1)S(1)}, u32[]{:S(2)}, u32[]{:S(2)}) async-start(bf16[4,288,1024]{2,1,0:T(8,128)(2,1)} %pad_maximum_fusion), calls=%async_computation | async-start | bytes 4718592 | tf_op jit(solution)/shard_map/all_to_all | solution.py:1019
  22.7 12.5 %collective-permute-start.2 = (bf16[32,3200]{1,0:T(8,128)(2,1)S(1)}, bf16[32,3200]{1,0:T(8,128)(2,1)S(1)}, u32[]{:S(2)}, u32[]{:S(2)}) collective-permute-start(bf16[32,3200]{1,0:T(8,128)(2,1)S(1)} %get-tuple-element.457), channel_id=1, source_target_pairs={{0,24},{1,25},{2,26},{3,27},{4,28},{5,29},{6,30},{7,31},{8,16},{9,... | collective-permute-start | bytes 614408 | tf_op jit(solution)/shard_map/ppermute | solution.py:898
  26.4 24.4 %collective-permute-start.1 = (bf16[32,3200]{1,0:T(8,128)(2,1)S(1)}, bf16[32,3200]{1,0:T(8,128)(2,1)S(1)}, u32[]{:S(2)}, u32[]{:S(2)}) collective-permute-start(bf16[32,3200]{1,0:T(8,128)(2,1)S(1)} %get-tuple-element.457), channel_id=1, source_target_pairs={{0,16},{1,17},{2,18},{3,19},{4,20},{5,21},{6,22},{7,23},{8,24},{9,... | collective-permute-start | bytes 614408 | tf_op jit(solution)/shard_map/ppermute | solution.py:898
  26.4 24.4 %collective-permute-start = (bf16[32,3200]{1,0:T(8,128)(2,1)S(1)}, bf16[32,3200]{1,0:T(8,128)(2,1)S(1)}, u32[]{:S(2)}, u32[]{:S(2)}) collective-permute-start(bf16[32,3200]{1,0:T(8,128)(2,1)S(1)} %get-tuple-element.457), channel_id=1, source_target_pairs={{0,8},{1,9},{2,10},{3,11},{4,12},{5,13},{6,14},{7,15},{8,0},{9,1},... | collective-permute-start | bytes 614408 | tf_op jit(solution)/shard_map/ppermute | solution.py:898
  54.8 20.5 %collective-permute-start.3 = (bf16[2,32,3200]{2,1,0:T(8,128)(2,1)S(1)}, bf16[2,32,3200]{2,1,0:T(8,128)(2,1)S(1)}, u32[]{:S(2)}, u32[]{:S(2)}) collective-permute-start(bf16[2,32,3200]{2,1,0:T(8,128)(2,1)S(1)} %get-tuple-element.209), channel_id=1, source_target_pairs={{0,1},{1,0},{2,3},{3,2},{4,5},{5,4},{6,7},{7,6},{8,9},{9,8},{10,11... | collective-permute-start | bytes 1228808 | tf_op jit(solution)/shard_map/ppermute | solution.py:898
  58.5 17.7 %collective-permute-start.4 = (bf16[2,32,3200]{2,1,0:T(8,128)(2,1)S(1)}, bf16[2,32,3200]{2,1,0:T(8,128)(2,1)S(1)}, u32[]{:S(2)}, u32[]{:S(2)}) collective-permute-start(bf16[2,32,3200]{2,1,0:T(8,128)(2,1)S(1)} %get-tuple-element.210), channel_id=1, source_target_pairs={{0,2},{1,3},{2,0},{3,1},{4,6},{5,7},{6,4},{7,5},{8,10},{9,11},{10,... | collective-permute-start | bytes 1228808 | tf_op jit(solution)/shard_map/ppermute | solution.py:898
  76.3 39.4 %copy-start.1 = (bf16[2,2,32,3200]{3,2,1,0:T(8,128)(2,1)}, bf16[2,2,32,3200]{3,2,1,0:T(8,128)(2,1)S(1)}, u32[]{:S(2)}) copy-start(bf16[2,2,32,3200]{3,2,1,0:T(8,128)(2,1)S(1)} %pad_maximum_fusion.7.refs_2_) | copy-start | bytes 2457604
  76.3 36.4 %collective-permute-start.6 = (bf16[2,2,32,3200]{3,2,1,0:T(8,128)(2,1)S(1)}, bf16[2,2,32,3200]{3,2,1,0:T(8,128)(2,1)}, u32[]{:S(2)}, u32[]{:S(2)}) collective-permute-start(bf16[2,2,32,3200]{3,2,1,0:T(8,128)(2,1)S(1)} %pad_maximum_fusion.7.refs_2_), channel_id=1, source_target_pairs={{0,1},{1,0},{2,3},{3,2},{4,5},{5,4},{6,7},{7,6},{8,9},{9,8},{10,11... | collective-permute-start | bytes 2457608 | tf_op jit(solution)/shard_map/ppermute | solution.py:898
  78.9 37.4 %copy-start.46 = (s32[4]{0:T(128)S(1)}, s32[4]{0:T(128)}, u32[]{:S(2)}) copy-start(s32[4]{0:T(128)} %constant.48.clone) | copy-start | bytes 52
  78.9 33.9 %collective-permute-start.5 = (bf16[2,2,32,3200]{3,2,1,0:T(8,128)(2,1)}, bf16[2,2,32,3200]{3,2,1,0:T(8,128)(2,1)}, u32[]{:S(2)}, u32[]{:S(2)}) collective-permute-start(bf16[2,2,32,3200]{3,2,1,0:T(8,128)(2,1)} %pad_maximum_fusion.6.refs_0_), channel_id=1, source_target_pairs={{0,2},{1,3},{2,0},{3,1},{4,6},{5,7},{6,4},{7,5},{8,10},{9,11},{10,... | collective-permute-start | bytes 2457608 | tf_op jit(solution)/shard_map/ppermute | solution.py:898
  79.7 23.6 %collective-permute-start.7 = (bf16[32,5120]{1,0:T(8,128)(2,1)S(1)}, bf16[32,5120]{1,0:T(8,128)(2,1)S(1)}, u32[]{:S(2)}, u32[]{:S(2)}) collective-permute-start(bf16[32,5120]{1,0:T(8,128)(2,1)S(1)} %constant_dynamic-update-slice_fusion), channel_id=1, source_target_pairs={{0,8},{1,9},{2,10},{3,11},{4,12},{5,13},{6,14},{7,15},{8,0},{9,1},... | collective-permute-start | bytes 983048 | tf_op jit(solution)/shard_map/ppermute | solution.py:898
  79.7 33.0 %collective-permute-start.8 = (bf16[32,5120]{1,0:T(8,128)(2,1)S(1)}, bf16[32,5120]{1,0:T(8,128)(2,1)S(1)}, u32[]{:S(2)}, u32[]{:S(2)}) collective-permute-start(bf16[32,5120]{1,0:T(8,128)(2,1)S(1)} %constant_dynamic-update-slice_fusion), channel_id=1, source_target_pairs={{0,16},{1,17},{2,18},{3,19},{4,20},{5,21},{6,22},{7,23},{8,24},{9,... | collective-permute-start | bytes 983048 | tf_op jit(solution)/shard_map/ppermute | solution.py:898
  82.8 30.0 %collective-permute-start.9 = (bf16[32,5120]{1,0:T(8,128)(2,1)S(1)}, bf16[32,5120]{1,0:T(8,128)(2,1)S(1)}, u32[]{:S(2)}, u32[]{:S(2)}) collective-permute-start(bf16[32,5120]{1,0:T(8,128)(2,1)S(1)} %constant_dynamic-update-slice_fusion), channel_id=1, source_target_pairs={{0,24},{1,25},{2,26},{3,27},{4,28},{5,29},{6,30},{7,31},{8,16},{9,... | collective-permute-start | bytes 983048 | tf_op jit(solution)/shard_map/ppermute | solution.py:898
  115.2 4.6 collective-permute-start.10
  115.2 5.7 collective-permute-start.11
  115.7 5.2 collective-permute-start.12
  115.7 6.8 %collective-permute-start.13 = (bf16[2,2,32,3200]{3,2,1,0:T(8,128)(2,1)}, bf16[2,2,32,3200]{3,2,1,0:T(8,128)(2,1)}, u32[]{:S(2)}, u32[]{:S(2)}) collective-permute-start(bf16[2,2,32,3200]{3,2,1,0:T(8,128)(2,1)} %collective-permute-done.6.refs_3_), channel_id=1, source_target_pairs={{0,4},{1,5},{2,6},{3,7},{4,0},{5,1},{6,2},{7,3},{8,12},{9,13},{10,... | collective-permute-start | bytes 2457608 | tf_op jit(solution)/shard_map/ppermute | solution.py:898
  118.4 31.4 %collective-permute-start.14 = (bf16[2,32,5120]{2,1,0:T(8,128)(2,1)}, bf16[2,32,5120]{2,1,0:T(8,128)(2,1)}, u32[]{:S(2)}, u32[]{:S(2)}) collective-permute-start(bf16[2,32,5120]{2,1,0:T(8,128)(2,1)} %get-tuple-element.231), channel_id=1, source_target_pairs={{0,1},{1,0},{2,3},{3,2},{4,5},{5,4},{6,7},{7,6},{8,9},{9,8},{10,11... | collective-permute-start | bytes 1966088 | tf_op jit(solution)/shard_map/ppermute | solution.py:898
  119.8 31.5 %collective-permute-start.15 = (bf16[2,32,5120]{2,1,0:T(8,128)(2,1)}, bf16[2,32,5120]{2,1,0:T(8,128)(2,1)}, u32[]{:S(2)}, u32[]{:S(2)}) collective-permute-start(bf16[2,32,5120]{2,1,0:T(8,128)(2,1)} %get-tuple-element.232), channel_id=1, source_target_pairs={{0,2},{1,3},{2,0},{3,1},{4,6},{5,7},{6,4},{7,5},{8,10},{9,11},{10,... | collective-permute-start | bytes 1966088 | tf_op jit(solution)/shard_map/ppermute | solution.py:898
  132.9 18.4 %copy-start.4 = (bf16[1,2,32,5120]{3,2,1,0:T(8,128)(2,1)S(1)}, bf16[1,2,32,5120]{3,2,1,0:T(8,128)(2,1)}, u32[]{:S(2)}) copy-start(bf16[1,2,32,5120]{3,2,1,0:T(8,128)(2,1)} %get-tuple-element.432) | copy-start | bytes 1966084
  155.9 37.4 %copy-start.47 = (s32[4]{0:T(128)S(1)}, s32[4]{0:T(128)}, u32[]{:S(2)}) copy-start(s32[4]{0:T(128)} %param.26) | copy-start | bytes 52
  155.9 36.7 %collective-permute-start.16 = (bf16[2,2,32,5120]{3,2,1,0:T(8,128)(2,1)}, bf16[2,2,32,5120]{3,2,1,0:T(8,128)(2,1)}, u32[]{:S(2)}, u32[]{:S(2)}) collective-permute-start(bf16[2,2,32,5120]{3,2,1,0:T(8,128)(2,1)} %pad_maximum_fusion.3.refs_0_), channel_id=1, source_target_pairs={{0,2},{1,3},{2,0},{3,1},{4,6},{5,7},{6,4},{7,5},{8,10},{9,11},{10,... | collective-permute-start | bytes 3932168 | tf_op jit(solution)/shard_map/ppermute | solution.py:898
  157.1 35.7 %collective-permute-start.17 = (bf16[2,2,32,5120]{3,2,1,0:T(8,128)(2,1)}, bf16[2,2,32,5120]{3,2,1,0:T(8,128)(2,1)}, u32[]{:S(2)}, u32[]{:S(2)}) collective-permute-start(bf16[2,2,32,5120]{3,2,1,0:T(8,128)(2,1)} %pad_maximum_fusion.4.refs_2_), channel_id=1, source_target_pairs={{0,1},{1,0},{2,3},{3,2},{4,5},{5,4},{6,7},{7,6},{8,9},{9,8},{10,11... | collective-permute-start | bytes 3932168 | tf_op jit(solution)/shard_map/ppermute | solution.py:898
  157.8 37.1 %collective-permute-start.20 = (bf16[2,2,32,5120]{3,2,1,0:T(8,128)(2,1)}, bf16[2,2,32,5120]{3,2,1,0:T(8,128)(2,1)}, u32[]{:S(2)}, u32[]{:S(2)}) collective-permute-start(bf16[2,2,32,5120]{3,2,1,0:T(8,128)(2,1)} %pad_maximum_fusion.4.refs_2_), channel_id=1, source_target_pairs={{0,4},{1,5},{2,6},{3,7},{4,0},{5,1},{6,2},{7,3},{8,12},{9,13},{10,... | collective-permute-start | bytes 3932168 | tf_op jit(solution)/shard_map/ppermute | solution.py:898
  157.8 37.1 %collective-permute-start.18 = (bf16[2,2,32,5120]{3,2,1,0:T(8,128)(2,1)}, bf16[2,2,32,5120]{3,2,1,0:T(8,128)(2,1)}, u32[]{:S(2)}, u32[]{:S(2)}) collective-permute-start(bf16[2,2,32,5120]{3,2,1,0:T(8,128)(2,1)} %pad_maximum_fusion.3.refs_0_), channel_id=1, source_target_pairs={{0,4},{1,5},{2,6},{3,7},{4,0},{5,1},{6,2},{7,3},{8,12},{9,13},{10,... | collective-permute-start | bytes 3932168 | tf_op jit(solution)/shard_map/ppermute | solution.py:898
  192.8 3.4 collective-permute-start.19
  192.8 5.2 collective-permute-start.21
  230.5 42.8 %all-to-all-start.1 = ((bf16[4,256,1024]{2,1,0:T(8,128)(2,1)}), bf16[4,256,1024]{2,1,0:T(8,128)(2,1)S(1)}, u32[]{:S(2)}, u32[]{:S(2)}) async-start(bf16[4,256,1024]{2,1,0:T(8,128)(2,1)} %param.27), calls=%async_computation.1 | async-start | bytes 4194304 | tf_op jit(solution)/shard_map/all_to_all | solution.py:1110
  274.6 46.7 %all-to-all-start.2 = ((bf16[4,256,1024]{2,1,0:T(8,128)(2,1)}), bf16[4,256,1024]{2,1,0:T(8,128)(2,1)}, u32[]{:S(2)}, u32[]{:S(2)}) async-start(bf16[4,256,1024]{2,1,0:T(8,128)(2,1)} %bitcast.221), calls=%async_computation.2 | async-start | bytes 4194304 | tf_op jit(solution)/shard_map/all_to_all | solution.py:1127
  279.1 293.3 %reduce-scatter.5.cloned.1.call-start = ((), (), s32[]{:S(2)}) async-start(), calls=%async_computation.10 | async-start | bytes 2621440 | tf_op jit(solution)/shard_map/reduce_scatter | solution.py:961
  321.3 21.4 %collective-permute-start.22 = (bf16[2,2,2,2,32,8192]{5,4,3,2,1,0:T(8,128)(2,1)}, bf16[2,2,2,2,32,8192]{5,4,3,2,1,0:T(8,128)(2,1)}, u32[]{:S(2)}, u32[]{:S(2)}) collective-permute-start(bf16[2,2,2,2,32,8192]{5,4,3,2,1,0:T(8,128)(2,1)} %bitcast.248), channel_id=1, source_target_pairs={{0,4},{1,5},{2,6},{3,7},{4,0},{5,1},{6,2},{7,3},{8,12},{9,13},{10,... | collective-permute-start | bytes 25165832 | tf_op jit(solution)/shard_map/ppermute | solution.py:898
  347.7 48.4 %collective-permute-start.23 = (bf16[2,2,32,8192]{3,2,1,0:T(8,128)(2,1)}, bf16[2,2,32,8192]{3,2,1,0:T(8,128)(2,1)S(1)}, u32[]{:S(2)}, u32[]{:S(2)}) collective-permute-start(bf16[2,2,32,8192]{3,2,1,0:T(8,128)(2,1)} %get-tuple-element.288), channel_id=1, source_target_pairs={{0,2},{1,3},{2,0},{3,1},{4,6},{5,7},{6,4},{7,5},{8,10},{9,11},{10,... | collective-permute-start | bytes 6291464 | tf_op jit(solution)/shard_map/ppermute | solution.py:898
  349.6 47.7 %collective-permute-start.24 = (bf16[2,2,32,8192]{3,2,1,0:T(8,128)(2,1)S(1)}, bf16[2,2,32,8192]{3,2,1,0:T(8,128)(2,1)S(1)}, u32[]{:S(2)}, u32[]{:S(2)}) collective-permute-start(bf16[2,2,32,8192]{3,2,1,0:T(8,128)(2,1)S(1)} %get-tuple-element.289), channel_id=1, source_target_pairs={{0,1},{1,0},{2,3},{3,2},{4,5},{5,4},{6,7},{7,6},{8,9},{9,8},{10,11... | collective-permute-start | bytes 6291464 | tf_op jit(solution)/shard_map/ppermute | solution.py:898
  398.6 37.9 %slice-start = ((s8[5242880]{0:T(1024)(128)(4,1)}), s8[4194304]{0:T(1024)(128)(4,1)S(1)}, s32[]{:S(2)}) async-start(s8[5242880]{0:T(1024)(128)(4,1)} %bitcast.216), calls=%async_computation.11 | async-start | bytes 8388608
  403.5 27.0 %collective-permute-start.25 = (bf16[2,2,2,2,32,5120]{5,4,3,2,1,0:T(8,128)(2,1)}, bf16[2,2,2,2,32,5120]{5,4,3,2,1,0:T(8,128)(2,1)}, u32[]{:S(2)}, u32[]{:S(2)}) collective-permute-start(bf16[2,2,2,2,32,5120]{5,4,3,2,1,0:T(8,128)(2,1)} %bitcast.249), channel_id=1, source_target_pairs={{0,4},{1,5},{2,6},{3,7},{4,0},{5,1},{6,2},{7,3},{8,12},{9,13},{10,... | collective-permute-start | bytes 15728648 | tf_op jit(solution)/shard_map/ppermute | solution.py:898
  403.5 25.9 %collective-permute-start.26 = (bf16[2,32,8192]{2,1,0:T(8,128)(2,1)}, bf16[2,32,8192]{2,1,0:T(8,128)(2,1)}, u32[]{:S(2)}, u32[]{:S(2)}) collective-permute-start(bf16[2,32,8192]{2,1,0:T(8,128)(2,1)} %get-tuple-element.302), channel_id=1, source_target_pairs={{0,1},{1,0},{2,3},{3,2},{4,5},{5,4},{6,7},{7,6},{8,9},{9,8},{10,11... | collective-permute-start | bytes 3145736 | tf_op jit(solution)/shard_map/ppermute | solution.py:898
  404.9 25.6 %collective-permute-start.27 = (bf16[2,32,8192]{2,1,0:T(8,128)(2,1)}, bf16[2,32,8192]{2,1,0:T(8,128)(2,1)}, u32[]{:S(2)}, u32[]{:S(2)}) collective-permute-start(bf16[2,32,8192]{2,1,0:T(8,128)(2,1)} %get-tuple-element.303), channel_id=1, source_target_pairs={{0,2},{1,3},{2,0},{3,1},{4,6},{5,7},{6,4},{7,5},{8,10},{9,11},{10,... | collective-permute-start | bytes 3145736 | tf_op jit(solution)/shard_map/ppermute | solution.py:898
  405.5 31.0 %slice-start.1 = ((s8[5242880]{0:T(1024)(128)(4,1)}), s8[1048576]{0:T(1024)(128)(4,1)S(1)}, s32[]{:S(2)}) async-start(s8[5242880]{0:T(1024)(128)(4,1)} %bitcast.216), calls=%async_computation.12 | async-start | bytes 2097152
  449.3 31.5 %copy-start.8 = (bf16[512,1536]{1,0:T(8,128)(2,1)S(1)}, bf16[512,1536]{1,0:T(8,128)(2,1)}, u32[]{:S(2)}) copy-start(bf16[512,1536]{1,0:T(8,128)(2,1)} %get-tuple-element.315) | copy-start | bytes 4718596
  449.3 31.5 %collective-permute-start.28 = (bf16[2,2,2,2,32,1536]{5,4,3,2,1,0:T(8,128)(2,1)}, bf16[2,2,2,2,32,1536]{5,4,3,2,1,0:T(8,128)(2,1)S(1)}, u32[]{:S(2)}, u32[]{:S(2)}) collective-permute-start(bf16[2,2,2,2,32,1536]{5,4,3,2,1,0:T(8,128)(2,1)} %bitcast.251), channel_id=1, source_target_pairs={{0,4},{1,5},{2,6},{3,7},{4,0},{5,1},{6,2},{7,3},{8,12},{9,13},{10,... | collective-permute-start | bytes 4718600 | tf_op jit(solution)/shard_map/ppermute | solution.py:898
  449.3 31.4 %collective-permute-start.29 = (bf16[2,2,32,5120]{3,2,1,0:T(8,128)(2,1)}, bf16[2,2,32,5120]{3,2,1,0:T(8,128)(2,1)S(1)}, u32[]{:S(2)}, u32[]{:S(2)}) collective-permute-start(bf16[2,2,32,5120]{3,2,1,0:T(8,128)(2,1)} %get-tuple-element.323), channel_id=1, source_target_pairs={{0,2},{1,3},{2,0},{3,1},{4,6},{5,7},{6,4},{7,5},{8,10},{9,11},{10,... | collective-permute-start | bytes 3932168 | tf_op jit(solution)/shard_map/ppermute | solution.py:898
  449.9 30.8 %collective-permute-start.30 = (bf16[2,2,32,5120]{3,2,1,0:T(8,128)(2,1)S(1)}, bf16[2,2,32,5120]{3,2,1,0:T(8,128)(2,1)S(1)}, u32[]{:S(2)}, u32[]{:S(2)}) collective-permute-start(bf16[2,2,32,5120]{3,2,1,0:T(8,128)(2,1)S(1)} %copy-done.14), channel_id=1, source_target_pairs={{0,1},{1,0},{2,3},{3,2},{4,5},{5,4},{6,7},{7,6},{8,9},{9,8},{10,11... | collective-permute-start | bytes 3932168 | tf_op jit(solution)/shard_map/ppermute | solution.py:898
  485.4 25.4 %collective-permute-start.33 = (bf16[2,32,5120]{2,1,0:T(8,128)(2,1)}, bf16[2,32,5120]{2,1,0:T(8,128)(2,1)}, u32[]{:S(2)}, u32[]{:S(2)}) collective-permute-start(bf16[2,32,5120]{2,1,0:T(8,128)(2,1)} %get-tuple-element.337), channel_id=1, source_target_pairs={{0,1},{1,0},{2,3},{3,2},{4,5},{5,4},{6,7},{7,6},{8,9},{9,8},{10,11... | collective-permute-start | bytes 1966088 | tf_op jit(solution)/shard_map/ppermute | solution.py:898
  486.0 24.8 %collective-permute-start.34 = (bf16[2,32,5120]{2,1,0:T(8,128)(2,1)}, bf16[2,32,5120]{2,1,0:T(8,128)(2,1)}, u32[]{:S(2)}, u32[]{:S(2)}) collective-permute-start(bf16[2,32,5120]{2,1,0:T(8,128)(2,1)} %get-tuple-element.338), channel_id=1, source_target_pairs={{0,2},{1,3},{2,0},{3,1},{4,6},{5,7},{6,4},{7,5},{8,10},{9,11},{10,... | collective-permute-start | bytes 1966088 | tf_op jit(solution)/shard_map/ppermute | solution.py:898
  487.8 22.9 %collective-permute-start.31 = (bf16[2,2,32,1536]{3,2,1,0:T(8,128)(2,1)}, bf16[2,2,32,1536]{3,2,1,0:T(8,128)(2,1)}, u32[]{:S(2)}, u32[]{:S(2)}) collective-permute-start(bf16[2,2,32,1536]{3,2,1,0:T(8,128)(2,1)} %get-tuple-element.334), channel_id=1, source_target_pairs={{0,2},{1,3},{2,0},{3,1},{4,6},{5,7},{6,4},{7,5},{8,10},{9,11},{10,... | collective-permute-start | bytes 1179656 | tf_op jit(solution)/shard_map/ppermute | solution.py:898
  488.4 22.4 %collective-permute-start.32 = (bf16[2,2,32,1536]{3,2,1,0:T(8,128)(2,1)}, bf16[2,2,32,1536]{3,2,1,0:T(8,128)(2,1)}, u32[]{:S(2)}, u32[]{:S(2)}) collective-permute-start(bf16[2,2,32,1536]{3,2,1,0:T(8,128)(2,1)} %get-tuple-element.335), channel_id=1, source_target_pairs={{0,1},{1,0},{2,3},{3,2},{4,5},{5,4},{6,7},{7,6},{8,9},{9,8},{10,11... | collective-permute-start | bytes 1179656 | tf_op jit(solution)/shard_map/ppermute | solution.py:898
  517.2 27.6 %collective-permute-start.37 = (bf16[2,2,2,2,32,1536]{5,4,3,2,1,0:T(8,128)(2,1)}, bf16[2,2,2,2,32,1536]{5,4,3,2,1,0:T(8,128)(2,1)S(1)}, u32[]{:S(2)}, u32[]{:S(2)}) collective-permute-start(bf16[2,2,2,2,32,1536]{5,4,3,2,1,0:T(8,128)(2,1)} %bitcast.250), channel_id=1, source_target_pairs={{0,4},{1,5},{2,6},{3,7},{4,0},{5,1},{6,2},{7,3},{8,12},{9,13},{10,... | collective-permute-start | bytes 4718600 | tf_op jit(solution)/shard_map/ppermute | solution.py:898
  517.9 26.8 %all-to-all-start.3 = ((f32[32,1,416]{2,1,0:T(1,128)}), f32[32,1,416]{2,1,0:T(1,128)S(1)}, u32[]{:S(2)}, u32[]{:S(2)}) async-start(f32[32,1,416]{2,1,0:T(1,128)} %copy.82), calls=%async_computation.3 | async-start | bytes 131072 | tf_op jit(solution)/shard_map/all_to_all | solution.py:1241
  523.2 68.8 %reduce-scatter.3.cloned.1.call-start = ((), (), s32[]{:S(2)}) async-start(), calls=%async_computation.9 | async-start | bytes 1638400 | tf_op jit(solution)/shard_map/reduce_scatter | solution.py:961
  523.3 21.5 %collective-permute-start.35 = (bf16[2,32,1536]{2,1,0:T(8,128)(2,1)S(1)}, bf16[2,32,1536]{2,1,0:T(8,128)(2,1)S(1)}, u32[]{:S(2)}, u32[]{:S(2)}) collective-permute-start(bf16[2,32,1536]{2,1,0:T(8,128)(2,1)S(1)} %copy-done.26), channel_id=1, source_target_pairs={{0,1},{1,0},{2,3},{3,2},{4,5},{5,4},{6,7},{7,6},{8,9},{9,8},{10,11... | collective-permute-start | bytes 589832 | tf_op jit(solution)/shard_map/ppermute | solution.py:898
  525.1 19.7 %collective-permute-start.36 = (bf16[2,32,1536]{2,1,0:T(8,128)(2,1)S(1)}, bf16[2,32,1536]{2,1,0:T(8,128)(2,1)S(1)}, u32[]{:S(2)}, u32[]{:S(2)}) collective-permute-start(bf16[2,32,1536]{2,1,0:T(8,128)(2,1)S(1)} %copy-done.24), channel_id=1, source_target_pairs={{0,2},{1,3},{2,0},{3,1},{4,6},{5,7},{6,4},{7,5},{8,10},{9,11},{10,... | collective-permute-start | bytes 589832 | tf_op jit(solution)/shard_map/ppermute | solution.py:898
  549.8 12.5 %collective-permute-start.38 = (bf16[2,2,32,1536]{3,2,1,0:T(8,128)(2,1)}, bf16[2,2,32,1536]{3,2,1,0:T(8,128)(2,1)S(1)}, u32[]{:S(2)}, u32[]{:S(2)}) collective-permute-start(bf16[2,2,32,1536]{3,2,1,0:T(8,128)(2,1)} %get-tuple-element.365), channel_id=1, source_target_pairs={{0,2},{1,3},{2,0},{3,1},{4,6},{5,7},{6,4},{7,5},{8,10},{9,11},{10,... | collective-permute-start | bytes 1179656 | tf_op jit(solution)/shard_map/ppermute | solution.py:898
  550.4 11.9 %collective-permute-start.39 = (bf16[2,2,32,1536]{3,2,1,0:T(8,128)(2,1)}, bf16[2,2,32,1536]{3,2,1,0:T(8,128)(2,1)S(1)}, u32[]{:S(2)}, u32[]{:S(2)}) collective-permute-start(bf16[2,2,32,1536]{3,2,1,0:T(8,128)(2,1)} %get-tuple-element.366), channel_id=1, source_target_pairs={{0,1},{1,0},{2,3},{3,2},{4,5},{5,4},{6,7},{7,6},{8,9},{9,8},{10,11... | collective-permute-start | bytes 1179656 | tf_op jit(solution)/shard_map/ppermute | solution.py:898
  554.1 41.1 %all-to-all-start.4 = ((bf16[4,288,1024]{2,1,0:T(8,128)(2,1)}), bf16[4,288,1024]{2,1,0:T(8,128)(2,1)S(1)}, u32[]{:S(2)}, u32[]{:S(2)}) async-start(bf16[4,288,1024]{2,1,0:T(8,128)(2,1)} %pad_maximum_fusion.1), calls=%async_computation.4 | async-start | bytes 4718592 | tf_op jit(solution)/shard_map/all_to_all | solution.py:1261
  568.1 22.2 %collective-permute-start.42 = (bf16[32,1536]{1,0:T(8,128)(2,1)}, bf16[32,1536]{1,0:T(8,128)(2,1)}, u32[]{:S(2)}, u32[]{:S(2)}) collective-permute-start(bf16[32,1536]{1,0:T(8,128)(2,1)} %fusion.41), channel_id=1, source_target_pairs={{0,8},{1,9},{2,10},{3,11},{4,12},{5,13},{6,14},{7,15},{8,0},{9,1},... | collective-permute-start | bytes 294920 | tf_op jit(solution)/shard_map/ppermute | solution.py:898
  569.2 21.1 %collective-permute-start.43 = (bf16[32,1536]{1,0:T(8,128)(2,1)}, bf16[32,1536]{1,0:T(8,128)(2,1)}, u32[]{:S(2)}, u32[]{:S(2)}) collective-permute-start(bf16[32,1536]{1,0:T(8,128)(2,1)} %get-tuple-element.381), channel_id=1, source_target_pairs={{0,16},{1,17},{2,18},{3,19},{4,20},{5,21},{6,22},{7,23},{8,24},{9,... | collective-permute-start | bytes 294920 | tf_op jit(solution)/shard_map/ppermute | solution.py:898
  571.5 18.8 %collective-permute-start.44 = (bf16[32,1536]{1,0:T(8,128)(2,1)}, bf16[32,1536]{1,0:T(8,128)(2,1)}, u32[]{:S(2)}, u32[]{:S(2)}) collective-permute-start(bf16[32,1536]{1,0:T(8,128)(2,1)} %get-tuple-element.382), channel_id=1, source_target_pairs={{0,24},{1,25},{2,26},{3,27},{4,28},{5,29},{6,30},{7,31},{8,16},{9,... | collective-permute-start | bytes 294920 | tf_op jit(solution)/shard_map/ppermute | solution.py:898
  588.0 7.2 %collective-permute-start.40 = (bf16[2,32,1536]{2,1,0:T(8,128)(2,1)S(1)}, bf16[2,32,1536]{2,1,0:T(8,128)(2,1)}, u32[]{:S(2)}, u32[]{:S(2)}) collective-permute-start(bf16[2,32,1536]{2,1,0:T(8,128)(2,1)S(1)} %copy-done.25), channel_id=1, source_target_pairs={{0,1},{1,0},{2,3},{3,2},{4,5},{5,4},{6,7},{7,6},{8,9},{9,8},{10,11... | collective-permute-start | bytes 589832 | tf_op jit(solution)/shard_map/ppermute | solution.py:898
  588.8 6.5 %collective-permute-start.41 = (bf16[2,32,1536]{2,1,0:T(8,128)(2,1)S(1)}, bf16[2,32,1536]{2,1,0:T(8,128)(2,1)S(1)}, u32[]{:S(2)}, u32[]{:S(2)}) collective-permute-start(bf16[2,32,1536]{2,1,0:T(8,128)(2,1)S(1)} %copy-done.23), channel_id=1, source_target_pairs={{0,2},{1,3},{2,0},{3,1},{4,6},{5,7},{6,4},{7,5},{8,10},{9,11},{10,... | collective-permute-start | bytes 589832 | tf_op jit(solution)/shard_map/ppermute | solution.py:898
  598.6 11.2 %all-to-all-start.5 = ((f32[32,1,128]{2,1,0:T(1,128)}), f32[32,1,128]{2,1,0:T(1,128)S(1)}, u32[]{:S(2)}, u32[]{:S(2)}) async-start(f32[32,1,128]{2,1,0:T(1,128)} %bitcast.85), calls=%async_computation.5 | async-start | bytes 32768 | tf_op jit(solution)/shard_map/all_to_all | solution.py:1270
  603.6 7.5 %collective-permute-start.45 = (bf16[32,1536]{1,0:T(8,128)(2,1)S(1)}, bf16[32,1536]{1,0:T(8,128)(2,1)S(1)}, u32[]{:S(2)}, u32[]{:S(2)}) collective-permute-start(bf16[32,1536]{1,0:T(8,128)(2,1)S(1)} %fusion.44), channel_id=1, source_target_pairs={{0,8},{1,9},{2,10},{3,11},{4,12},{5,13},{6,14},{7,15},{8,0},{9,1},... | collective-permute-start | bytes 294920 | tf_op jit(solution)/shard_map/ppermute | solution.py:898
  605.5 10.8 %collective-permute-start.46 = (bf16[32,1536]{1,0:T(8,128)(2,1)S(1)}, bf16[32,1536]{1,0:T(8,128)(2,1)S(1)}, u32[]{:S(2)}, u32[]{:S(2)}) collective-permute-start(bf16[32,1536]{1,0:T(8,128)(2,1)S(1)} %get-tuple-element.449), channel_id=1, source_target_pairs={{0,16},{1,17},{2,18},{3,19},{4,20},{5,21},{6,22},{7,23},{8,24},{9,... | collective-permute-start | bytes 294920 | tf_op jit(solution)/shard_map/ppermute | solution.py:898
  608.0 8.3 %collective-permute-start.47 = (bf16[32,1536]{1,0:T(8,128)(2,1)S(1)}, bf16[32,1536]{1,0:T(8,128)(2,1)S(1)}, u32[]{:S(2)}, u32[]{:S(2)}) collective-permute-start(bf16[32,1536]{1,0:T(8,128)(2,1)S(1)} %get-tuple-element.450), channel_id=1, source_target_pairs={{0,24},{1,25},{2,26},{3,27},{4,28},{5,29},{6,30},{7,31},{8,16},{9,... | collective-permute-start | bytes 294920 | tf_op jit(solution)/shard_map/ppermute | solution.py:898
  (43 other events, 257.4 us)
Sparse Core Ops, SparseCore 0:
  14.2 172.1 all-gather.1
  491.3 44.9 reduce-scatter.4
  538.6 30.5 reduce-scatter.2

commit v3 on v2

--- a/solution.py
+++ b/solution.py
@@ -427,6 +427,15 @@
     return jnp.where(keep, rows, jnp.zeros_like(rows))
 
 
+def ahead(items, start):
+    later = start(items[0])
+    for at, item in enumerate(items):
+        value = later
+        if at + 1 < len(items):
+            later = start(items[at + 1])
+        yield item, value
+
+
 def whole(shape, index=None, single=True):
     where = index or (0,) * len(shape)
     mode = {"pipeline_mode": pl.Buffered(1)} if single else {}
@@ -456,28 +465,31 @@
     block = min(QB, length)
     vx_ref[:, :PAIR] = v_ref[...]
     vx_ref[:, PAIR:] = jnp.ones((keys, PAIR), BF16)
-    for start in range(0, length, block):
+    items = list(itertools.product(range(0, length, block), range(2)))
+
+    def products(item):
+        start, head = item
+        rows = head_lanes(q_ref[start : start + block, :], head)
+        return mm(rows, k_ref[: start + block, :], NT)
+
+    for (start, head), scores in ahead(items, products):
         limit = start + block
-        rows = q_ref[start:limit, :]
-        both = []
-        for head in range(2):
-            scores = mm(head_lanes(rows, head), k_ref[:limit, :], NT)
-            last = scores[:, start:]
-            col = lax.broadcasted_iota(jnp.int32, last.shape, 1)
-            row = lax.broadcasted_iota(jnp.int32, last.shape, 0)
-            last = jnp.where(col <= row, last, NEGATIVE)
-            if start:
-                scores = jnp.concatenate([scores[:, :start], last], axis=1)
-            else:
-                scores = last
-            top = jnp.max(scores, axis=1, keepdims=True)
-            weights = jnp.exp2(scores - top).astype(BF16)
-            total = mm(weights, vx_ref[:limit, :])
-            both.append(total[:, :PAIR] / total[:, PAIR:])
-            stat = (top + jnp.log2(total[:, PAIR:])).T
-            lse_ref[0, head : head + 1, start:limit] = stat[:1, :]
-        lane = lax.broadcasted_iota(jnp.int32, both[0].shape, 1)
-        o_ref[start:limit, :] = jnp.where(lane < HEAD_DIM, both[0], both[1]).astype(BF16)
+        last = scores[:, start:]
+        col = lax.broadcasted_iota(jnp.int32, last.shape, 1)
+        row = lax.broadcasted_iota(jnp.int32, last.shape, 0)
+        last = jnp.where(col <= row, last, NEGATIVE)
+        scores = jnp.concatenate([scores[:, :start], last], axis=1) if start else last
+        top = jnp.max(scores, axis=1, keepdims=True)
+        weights = jnp.exp2(scores - top).astype(BF16)
+        total = mm(weights, vx_ref[:limit, :])
+        out = total[:, :PAIR] / total[:, PAIR:]
+        stat = (top + jnp.log2(total[:, PAIR:])).T
+        lse_ref[0, head : head + 1, start:limit] = stat[:1, :]
+        if head == 0:
+            kept = out
+        else:
+            lane = lax.broadcasted_iota(jnp.int32, out.shape, 1)
+            o_ref[start:limit, :] = jnp.where(lane < HEAD_DIM, kept, out).astype(BF16)
 
 
 def attend_back_kernel(
@@ -491,32 +503,38 @@
         jnp.sum(product[head * HEAD_DIM : (head + 1) * HEAD_DIM, :], axis=0, keepdims=True)
         for head in range(2)
     ]
-    for start in range(0, keys, block):
-        key_rows = k_ref[start : start + block, :]
-        value_rows = v_ref[start : start + block, :]
-        grad_keys = grad_values = None
-        for head in range(2):
-            queries = head_lanes(q_ref[start:, :], head)
-            grads = head_lanes(do_ref[start:, :], head)
-            scores = mm(key_rows, queries, NT)
-            probs = jnp.exp2(scores - lse_ref[0, head : head + 1, start:])
-            edge = probs[:, :block]
-            row = lax.broadcasted_iota(jnp.int32, edge.shape, 0)
-            col = lax.broadcasted_iota(jnp.int32, edge.shape, 1)
-            edge = jnp.where(row <= col, edge, 0.0)
-            if start + block < keys:
-                probs = jnp.concatenate([edge, probs[:, block:]], axis=1)
-            else:
-                probs = edge
-            back = mm(value_rows, grads, NT)
-            scored = (probs * (back - delta[head][:, start:])).astype(BF16)
-            term_v = mm(probs.astype(BF16), grads)
-            term_k = mm(scored, queries)
-            grad_values = term_v if grad_values is None else grad_values + term_v
-            grad_keys = term_k if grad_keys is None else grad_keys + term_k
-            acc_ref[start:, :] += mm(scored, head_lanes(key_rows, head), TN)
-        dk_ref[start : start + block, :] = (grad_keys * LN2).astype(BF16)
-        dv_ref[start : start + block, :] = grad_values.astype(BF16)
+    items = list(itertools.product(range(0, keys, block), range(2)))
+
+    def products(item):
+        start, head = item
+        queries = head_lanes(q_ref[start:, :], head)
+        grads = head_lanes(do_ref[start:, :], head)
+        return (
+            queries,
+            grads,
+            mm(k_ref[start : start + block, :], queries, NT),
+            mm(v_ref[start : start + block, :], grads, NT),
+        )
+
+    for (start, head), (queries, grads, scores, back) in ahead(items, products):
+        probs = jnp.exp2(scores - lse_ref[0, head : head + 1, start:])
+        edge = probs[:, :block]
+        row = lax.broadcasted_iota(jnp.int32, edge.shape, 0)
+        col = lax.broadcasted_iota(jnp.int32, edge.shape, 1)
+        edge = jnp.where(row <= col, edge, 0.0)
+        if start + block < keys:
+            probs = jnp.concatenate([edge, probs[:, block:]], axis=1)
+        else:
+            probs = edge
+        scored = (probs * (back - delta[head][:, start:])).astype(BF16)
+        term_v = mm(probs.astype(BF16), grads)
+        term_k = mm(scored, queries)
+        acc_ref[start:, :] += mm(scored, head_lanes(k_ref[start : start + block, :], head), TN)
+        if head == 0:
+            grad_keys, grad_values = (term_k, term_v)
+        else:
+            dk_ref[start : start + block, :] = ((grad_keys + term_k) * LN2).astype(BF16)
+            dv_ref[start : start + block, :] = (grad_values + term_v).astype(BF16)
     dq_ref[...] = (acc_ref[...] * SCALING).astype(BF16)
 
 
@@ -594,14 +612,14 @@
 def gelu_pair(values):
     root = 0.7978845608028654
     square = values * values
-    bend = jnp.tanh(values * (root + (0.044715 * root) * square))
-    half = 0.5 + 0.5 * bend
-    slope = half + values * (0.5 - 0.5 * bend * bend) * (root + (0.134145 * root) * square)
-    return (values * half, slope)
+    part = 0.5 + 0.5 * jnp.tanh(values * (root + (0.044715 * root) * square))
+    out = values * part
+    slope = part + (out - out * part) * (2.0 * root + (0.26829 * root) * square)
+    return (out, slope)
 
 
 def qkv_kernel(x_ref, w_ref, vec_ref, h_ref, qkv_ref):
-    normed, _ = normed_of(x_ref[...].astype(F32))
+    normed, _ = normed_of(x_ref[0].astype(F32))
     low = (normed * vec_ref[0:1, :] + vec_ref[1:2, :]).astype(BF16)
     h_ref[...] = low
     for part in range(3):
@@ -621,16 +639,19 @@
     x1_ref, h2_ref, q2_ref, o2_ref, x2_ref, h3_ref, lse_ref,
 ):
     keys = kv_ref.shape[0]
-    after = x_ref[...].astype(F32) + mm(o_ref[...], ws_ref[...]) + vec_ref[0:1, :]
+    after = x_ref[0].astype(F32) + mm(o_ref[...], ws_ref[...]) + vec_ref[0:1, :]
     x1_ref[...] = after
     normed, _ = normed_of(after)
     low = (normed * vec_ref[1:2, :] + vec_ref[2:3, :]).astype(BF16)
     h2_ref[...] = low
     q2_ref[...] = ((mm(low, wq_ref[...]) + vec_ref[3:4, :]) * (SCALING * LOG2E)).astype(BF16)
     ones = jnp.ones((keys, PAIR), BF16)
-    for pair in range(HEADS // 2):
-        at = pair * PAIR
-        scores = mm(q2_ref[:, at : at + PAIR], pair_keys(kv_ref, at, keys), NT)
+
+    def products(at):
+        return mm(q2_ref[:, at : at + PAIR], pair_keys(kv_ref, at, keys), NT)
+
+    for at, scores in ahead(list(range(0, D, PAIR)), products):
+        pair = at // PAIR
         col = lax.broadcasted_iota(jnp.int32, (scores.shape[0], keys), 1)
         inside = col < len_ref[0]
         halves, tops = ([], [])
@@ -661,35 +682,30 @@
 
 def mlp_kernel(h_ref, wi_ref, wo_ref, bias_ref, x2_ref, last_ref, act_ref, slope_ref, out_ref, acc_ref):
     step = pl.program_id(0)
-    length = h_ref.shape[0]
-    for start in range(0, length, QB):
-        rows = slice(start, start + QB)
-        act, slope = gelu_pair(mm(h_ref[rows, :], wi_ref[...]) + bias_ref[0])
+
+    @pl.when(step == 0)
+    def _():
+        acc_ref[...] = x2_ref[...] + last_ref[...]
+
+    tile = min(512, h_ref.shape[0])
+    parts = [slice(at, at + tile) for at in range(0, h_ref.shape[0], tile)]
+    for rows, mixed in ahead(parts, lambda rows: mm(h_ref[rows, :], wi_ref[...])):
+        act, slope = gelu_pair(mixed + bias_ref[0])
         act = act.astype(BF16)
         act_ref[rows, :] = act
         slope_ref[rows, :] = slope.astype(BF16)
-        term = mm(act, wo_ref[...])
-
-        @pl.when(step == 0)
-        def _():
-            acc_ref[rows, :] = x2_ref[rows, :] + last_ref[...] + term
-
-        @pl.when(step > 0)
-        def _():
-            acc_ref[rows, :] += term
-
-        @pl.when(step == pl.num_programs(0) - 1)
-        def _():
-            out_ref[rows, :] = acc_ref[rows, :].astype(BF16)
+        acc_ref[rows, :] += mm(act, wo_ref[...])
+
+    @pl.when(step == pl.num_programs(0) - 1)
+    def _():
+        out_ref[...] = acc_ref[...].astype(BF16)
 
 
 def du_kernel(g_ref, wo_ref, slope_ref, du_ref, sum_ref):
-    length = g_ref.shape[0]
     total = None
-    for start in range(0, length, QB):
-        rows = slice(start, start + QB)
-        grad = mm(g_ref[rows, :], wo_ref[...], NT) * slope_ref[rows, :].astype(F32)
-        low = grad.astype(BF16)
+    parts = [slice(at, at + QB) for at in range(0, g_ref.shape[0], QB)]
+    for rows, grad in ahead(parts, lambda rows: mm(g_ref[rows, :], wo_ref[...], NT)):
+        low = (grad * slope_ref[rows, :].astype(F32)).astype(BF16)
         du_ref[rows, :] = low
         part = sums(low.astype(F32))
         total = part if total is None else total + part
@@ -728,14 +744,22 @@
         acc_ref[...] = jnp.zeros_like(acc_ref)
 
     lane = lax.broadcasted_iota(jnp.int32, (keys, PAIR), 1)
-    for pair in range(HEADS // 2):
-        at = pair * PAIR
+
+    def products(at):
         queries = q_ref[:, at : at + PAIR]
         grads = do_ref[:, at : at + PAIR]
+        both_keys = pair_keys(kv_ref, at, keys)
+        return (
+            queries,
+            grads,
+            both_keys,
+            mm(both_keys, queries, NT),
+            mm(pair_keys(kv_ref, D + at, keys), grads, NT),
+        )
+
+    for at, (queries, grads, both_keys, scores, back) in ahead(list(range(0, D, PAIR)), products):
+        pair = at // PAIR
         product = (grads.astype(F32) * o_ref[:, at : at + PAIR].astype(F32)).T
-        both_keys = pair_keys(kv_ref, at, keys)
-        scores = mm(both_keys, queries, NT)
-        back = mm(pair_keys(kv_ref, D + at, keys), grads, NT)
         row = lax.broadcasted_iota(jnp.int32, (keys, scores.shape[1]), 0)
         inside = row < len_ref[0]
         probs, scored = ([], [])
@@ -774,7 +798,7 @@
 
 
 def norm1_kernel(*refs):
-    *grad_refs, w_ref, x_ref, dx1_ref, gain_ref, out_ref, vec_ref = refs
+    *grad_refs, w_ref, x_ref, dx1_ref, gain_ref, text_ref, out_ref, vec_ref = refs
     first = pl.program_id(0) == 0
     grads, at = (None, 0)
     groups = len(grad_refs) // 3
@@ -788,9 +812,11 @@
             grads = term if grads is None else grads + term
         rows_q.append(sums(grad_refs[3 * group][...].astype(F32)))
         rows_v.append(sums(grad_refs[3 * group + 2][...].astype(F32)))
-    normed, inverse = normed_of(x_ref[...].astype(F32))
+    normed, inverse = normed_of(x_ref[0].astype(F32))
     back = norm_input_grad(grads, normed, inverse, gain_ref[...])
-    out_ref[...] = (dx1_ref[...] + back).astype(BF16)
+    tile = back.shape[0]
+    out_ref[0, :tile, :] = (dx1_ref[...] + back).astype(BF16)
+    out_ref[0, tile:, :] = text_ref[...]
     add_row(vec_ref, 0, sums(grads * normed), first)
     add_row(vec_ref, 1, sums(grads), first)
     add_row(vec_ref, 2, jnp.concatenate(rows_q, axis=1), first)
@@ -1038,7 +1064,6 @@
     at_once(w_first)
     first = w_first.done(places)
 
-    tokens = moved[:, :part].reshape(length, D)
     texts = moved[:, part:].reshape(prompt, D)
     prompt_length = lax.dynamic_slice_in_dim(text_lengths, ring.seq, 1, 0)
 
@@ -1052,9 +1077,10 @@
     (g1, b1, bias_out, g2, b2, bias_cross, g3, b3, bias_last, bias_qv, bias_qv2) = full
     zero = jnp.zeros((D,), F32)
 
-    tile = min(QB, length)
-    grid = (length // tile,)
+    tile = part
+    grid = (n_seq,)
     row_tile = pl.BlockSpec((tile, D), lambda i, *_: (i, 0))
+    token_tile = pl.BlockSpec((1, tile, D), lambda i, *_: (i, 0, 0))
     vec8, vec1 = (whole((8, D)), whole((1, D)))
     sum8 = pl.BlockSpec((8, D), lambda *_: (0, 0))
     square = (D, D)
@@ -1074,10 +1100,10 @@
 
     h1, qkv = kernel_call(
         qkv_kernel, "qkv", grid,
-        [row_tile, whole((D, 3 * D)), vec8],
+        [token_tile, whole((D, 3 * D)), vec8],
         [row_tile, columns(3 * D)],
         [(flat, BF16), ((length, 3 * D), BF16)],
-        (tokens, first, line(g1, b1, bias_qv[:D], zero, bias_qv[D:])),
+        (moved, first, line(g1, b1, bias_qv[:D], zero, bias_qv[D:])),
         flops=3 * unit, moved=16 * length * D,
     )
     now = [qkv, h1]
@@ -1097,12 +1123,12 @@
     kv2 = (mm(texts, second[:, 2 * D : 4 * D]) + jnp.concatenate([zero, bias_qv2[D:]])).astype(BF16)
     x1, h2, q2, o2, x2, h3, lse2 = kernel_call(
         cross_kernel, "cross", grid,
-        [row_tile, row_tile, weight_block(0), weight_block(1), weight_block(4),
+        [token_tile, row_tile, weight_block(0), weight_block(1), weight_block(4),
          whole((prompt, 2 * D)), vec8],
         [row_tile] * 6 + [stat_tile],
         [(flat, F32), (flat, BF16), (flat, BF16), (flat, BF16), (flat, F32), (flat, BF16),
          ((HEADS, length), F32)],
-        (prompt_length, tokens, o1, second, second, second, kv2,
+        (prompt_length, moved, o1, second, second, second, kv2,
          line(bias_out, g2, b2, bias_qv2[:D], bias_cross, g3, b3)),
         flops=5 * unit, moved=30 * length * D, prefetch=1,
     )
@@ -1121,11 +1147,18 @@
         flops=2 * fours * unit, moved=40 * length * D,
     )
 
-    now = [out, act, slope, grad_rows]
-    at_once(now)
-    out, act, slope, grad_rows = now
+    full_flat = whole(flat)
+    r_out = Steps(
+        ring,
+        weight_grads(
+            flat_places, (act, grad_rows), [by_unit, full_flat], [(0, 1)] * fours, D, "d_mlp_out"
+        ),
+    )
+    now = [out, slope, grad_rows]
+    at_once(now, r_out)
+    out, slope, grad_rows = now
     leaving_out = [lax.all_to_all(out.reshape(n_seq, part, D), "seq", 0, 0, tiled=True)]
-    full_flat = whole(flat)
+    r_out.launch()
     du, du_sum = kernel_call(
         du_kernel, "du", (fours,),
         [full_flat, streamed(fours), by_unit],
@@ -1134,28 +1167,21 @@
         (grad_rows, mlp, slope),
         flops=fours * unit, moved=26 * length * D,
     )
-    last = fours - 1
-    r_mlp = Steps(
+    now = [du, h3]
+    at_once(now, r_out)
+    r_out.near()
+    at_once(now, r_out)
+    r_out.launch()
+    du, h3 = now
+    r_in = Steps(
         ring,
-        weight_grads(
-            flat_places,
-            (act, grad_rows, h3, du),
-            [
-                pl.BlockSpec((length, D), lambda t, *_: (0, jnp.minimum(t, last))),
-                full_flat,
-                full_flat,
-                pl.BlockSpec((length, D), lambda t, *_: (0, jnp.maximum(t - fours, 0))),
-            ],
-            [(0, 1)] * fours + [(2, 3)] * fours,
-            D,
-            "d_mlp",
-        ),
+        weight_grads(flat_places, (h3, du), [full_flat, by_unit], [(0, 1)] * fours, D, "d_mlp_in"),
     )
     now = [du]
-    at_once(now, leaving_out, r_mlp)
+    at_once(now, leaving_out, r_in)
     (du,) = now
     (block_output,) = leaving_out
-    r_mlp.launch()
+    r_in.launch()
     dx2, dc, do2, sums3 = kernel_call(
         norm3_kernel, "norm3_back", grid,
         [columns(fours * D), whole((D, fours * D)), row_tile, row_tile, vec1, weight_block(4)],
@@ -1165,10 +1191,12 @@
         flops=(fours + 1) * unit, moved=32 * length * D,
     )
     now = [dx2, dc, do2]
-    at_once(now, r_mlp)
-    r_mlp.near()
-    at_once(now, r_mlp)
-    r_mlp.launch()
+    at_once(now, r_in, r_out)
+    r_out.far()
+    r_in.near()
+    at_once(now, r_in, r_out)
+    r_out.launch()
+    r_in.launch()
     dx2, dc, do2 = now
     dq2, dkv2, dx1, da, do1, sums2 = kernel_call(
         cross_back_kernel, "cross_back", grid,
@@ -1184,7 +1212,7 @@
     r_mid = Steps(
         ring,
         weight_grads(
-            flat_places,
+            places,
             (o1, da, o2, dc, h2, dq2, texts, dkv2, dkv2),
             [full_flat] * 6 + [whole((prompt, D))] + text_block,
             [(0, 1), (2, 3), (4, 5), (6, 7), (6, 8)],
@@ -1193,39 +1221,36 @@
         ),
     )
     now = [do1, dx1, dkv2]
-    at_once(now, r_mid, r_mlp)
-    r_mlp.far()
-    at_once(now, r_mid, r_mlp)
+    at_once(now, r_mid, r_in, r_out)
+    r_in.far()
+    r_out.scatter()
+    at_once(now, r_mid, r_in, r_out)
     do1, dx1, dkv2 = now
     r_mid.launch()
-    r_mlp.launch()
+    r_in.launch()
+    r_out.launch_scatter()
     count = HEADS // 4
     back_a = list(attend_back(qkv, o1, do1, lse1, 0, count))
     now = [do1]
-    at_once(now, back_a, r_mid, r_mlp)
+    at_once(now, back_a, r_mid, r_in)
     r_mid.near()
-    r_mlp.scatter()
-    at_once(now, back_a, r_mid, r_mlp)
+    r_in.scatter()
+    at_once(now, back_a, r_mid, r_in)
     (do1,) = now
     r_mid.launch()
-    r_mlp.launch_scatter()
-    narrow = [full_flat] + [whole((length, count * PAIR))] * 3
-    units = [(0, 1), (0, 2), (0, 3)]
-    r_a = Steps(ring, weight_grads(places, (h1, *back_a), narrow, units, count * PAIR, "d_qkv_a"))
-    now = [do1]
-    at_once(now, r_a)
-    r_a.launch()
-    back_b = list(attend_back(qkv, o1, now[0], lse1, count, count))
-    at_once(back_b, r_a, r_mid)
+    r_in.launch_scatter()
+    back_b = list(attend_back(qkv, o1, do1, lse1, count, count))
+    narrow = [full_flat] + [whole((length, count * PAIR))] * 6
+    r_qkv = Steps(
+        ring,
+        weight_grads(
+            places, (h1, *back_a, *back_b), narrow, [(0, 1 + i) for i in range(6)],
+            count * PAIR, "d_qkv",
+        ),
+    )
+    at_once(back_b, r_qkv, r_mid)
+    r_qkv.launch()
     r_mid.far()
-    r_a.near()
-    at_once(back_b, r_a, r_mid)
-    r_mid.launch()
-    r_a.launch()
-    r_b = Steps(ring, weight_grads(places, (h1, *back_b), narrow, units, count * PAIR, "d_qkv_b"))
-    at_once(back_b, r_a, r_b, r_mid)
-    r_mid.scatter()
-    r_a.far()
     dv2_sum = jnp.sum(dkv2[:, D:].astype(F32), axis=0)
     early = [
         sums2[2], sums2[0], sums2[1], sums3[2], sums3[0], sums3[1], sums3[3],
@@ -1234,54 +1259,48 @@
     ]
     early = [across(early)]
     text_grad = mm(dkv2, second[:, 2 * D : 4 * D], NT).astype(BF16)
-    at_once(back_b, r_a, r_b, r_mid, early)
-    r_b.launch()
-    r_a.launch()
-    r_mid.launch_scatter()
-    early = [lax.all_to_all(early[0], AXES, 0, 0, tiled=True)]
-    image_grad, sums1 = kernel_call(
+    now = [text_grad]
+    at_once(back_b, r_qkv, r_mid, early, now)
+    r_mid.launch()
+    r_qkv.near()
+    at_once(back_b, r_qkv, early, now)
+    (text_grad,) = now
+    r_qkv.launch()
+    leaving, sums1 = kernel_call(
         norm1_kernel, "norm1_back", grid,
-        [columns(count * PAIR)] * 6 + [whole((D, 3 * D)), row_tile, row_tile, vec1],
-        [row_tile, sum8],
-        [(flat, BF16), ((8, D), F32)],
-        (*back_a, *back_b, first, tokens, dx1, g1.reshape(1, D)),
+        [columns(count * PAIR)] * 6 + [whole((D, 3 * D)), token_tile, row_tile, vec1]
+        + [pl.BlockSpec((text_part, D), lambda i, *_: (i, 0))],
+        [pl.BlockSpec((1, part + text_part, D), lambda i, *_: (i, 0, 0)), sum8],
+        [(moved.shape, BF16), ((8, D), F32)],
+        (*back_a, *back_b, first, moved, dx1, g1.reshape(1, D), text_grad),
         flops=3 * unit, moved=18 * length * D,
     )
-    now = [image_grad, text_grad, sums1]
-    at_once(now, r_a, r_b, early)
-    image_grad, text_grad, sums1 = now
-    r_b.near()
-    leaving = jnp.concatenate(
-        [image_grad.reshape(n_seq, part, D), text_grad.reshape(n_seq, text_part, D)], axis=1
-    )
-    now = [leaving]
-    at_once(now, r_b)
-    r_b.launch()
-    (leaving,) = now
     leaving = [lax.all_to_all(leaving, "seq", 0, 0, tiled=True)]
-    at_once(r_b, r_a)
-    r_a.deep()
-    r_b.far()
+    at_once(r_qkv, r_mid)
+    r_qkv.far()
+    r_mid.deep()
+    at_once(r_qkv, r_mid)
+    r_qkv.launch()
+    r_mid.launch()
     late = [across([sums1[0], sums1[1], jnp.concatenate([sums1[2], sums1[3]])])]
-    at_once(r_a, r_b, late)
-    r_b.launch()
-    r_a.launch()
-    at_once(r_b, leaving, late)
-    late = lax.all_to_all(late[0], AXES, 0, 0, tiled=True)
-    r_b.deep()
-    r_b.launch()
+    mlp_out_grad = r_out.done().reshape(rows, fours, D).transpose(1, 0, 2).reshape(-1, D)
+    mlp_in_grad = r_in.done().reshape(rows, fours, ring.count, rows)
+    mlp_in_grad = mlp_in_grad.transpose(0, 2, 1, 3).reshape(rows, -1)
+    now = [mlp_out_grad, mlp_in_grad]
+    at_once(r_qkv, r_mid, late, leaving, now)
+    mlp_out_grad, mlp_in_grad = now
+    r_qkv.deep()
+    at_once(r_qkv, late, early)
+    r_qkv.launch()
+    small = jnp.concatenate([early[0], late[0]], axis=1)
+    small = jnp.sum(lax.all_to_all(small, AXES, 0, 0, tiled=True), axis=0)
     leaving = leaving[0].astype(F32)
-    mlp_grad = r_mlp.done()
-    mlp_out_grad = mlp_grad[:, : fours * D].reshape(rows, fours, D).transpose(1, 0, 2).reshape(-1, D)
-    mlp_in_grad = mlp_grad[:, fours * D :].reshape(rows, fours, ring.count, rows)
-    mlp_in_grad = mlp_in_grad.transpose(0, 2, 1, 3).reshape(rows, -1)
-    mid, last_a, last_b = (r_mid.done(), r_a.done(), r_b.done())
+    mid, last = (r_mid.done(), r_qkv.done())
     wide = count * PAIR
     self_qkv_grad = jnp.concatenate(
-        [half[:, i * wide : (i + 1) * wide] for i in range(3) for half in (last_a, last_b)], axis=1
-    )
-
-    small = jnp.concatenate([jnp.sum(early[0], axis=0), jnp.sum(late, axis=0)])
+        [last[:, (3 * j + i) * wide : (3 * j + i + 1) * wide] for i in range(3) for j in range(2)],
+        axis=1,
+    )
 
     def mine(total, at, wide):
         return total[at * rows : at * rows + wide]

time: 635 us -> 606 us (0.954)
  Pallas kernels: 285 us -> 268 us
  local copies, waits for them, and re-layouts: 58.5 us -> 42.8 us
    pallas_call x16, Pallas kernels: 285 us -> 268 us  [kernel_call(): pl.pallas_call(body, grid_spec=pltpu.PrefetchScalarGridSpec(num_scalar_pr...]
    reshape x1 -> x3, local copies, waits for them, and re-layouts: 4.48 us -> 12.1 us  [whole_images(): mlp_in_grad = mlp_in_grad.transpose(0, 2, 1, 3).reshape(rows, -1)]
  transfers between devices with their start and end apart: 57 -> 56, of which waited for: 24 -> 22; matrix products, arithmetic and copies ran while one was open for 13% -> 12% of each run, Pallas kernels for 44% -> 42%
where the time goes in v3:
time: 606 us; the launch traced here: 600 us
  Pallas kernels  268 us (44%)
  waiting for transfers between devices  129 us (21%)
  starting transfers between devices  76.2 us (13%)
  other arithmetic  61 us (10%)
  local copies, waits for them, and re-layouts  42.8 us (7%)
  between operations  14.9 us (2%)
  matrix products  8.11 us (1%)
    pallas_call x16, Pallas kernels, kernel_call(): pl.pallas_call(body, grid_spec=pltpu.PrefetchScalarGridSpec(num_scalar_pr...  268 us
    ppermute x48, waiting for transfers between devices, swap(): return lax.ppermute(array, AXES, [(i, i ^ bits) for i in range(self.count)])  126 us
    ppermute x48, starting transfers between devices, swap(): return lax.ppermute(array, AXES, [(i, i ^ bits) for i in range(self.count)])  52.6 us
    convert_element_type x4, other arithmetic, near(): total_of(self.kept[i, 1], self.got[i, 1]).astype(BF16)  14.4 us
  transfers between devices with their start and end apart: 56, of which 22 were waited for; matrix products, arithmetic and copies ran while one was open for 12% of the time, Pallas kernels for 42%

profile of v3, /device:TPU:0, one launch (start us, length us, event | category | flops | bytes accessed | tf_op | source)
XLA Modules:
  0.0 599.9 jit_solution(16522832400747502836)
XLA Ops:
  14.1 2.6 pad_maximum_fusion
  16.8 5.8 all-to-all-start
  23.1 3.7 collective-permute-start.2
  31.0 4.4 collective-permute-done.2
  35.4 15.7 %collective-permute-done.1 = bf16[32,3200]{1,0:T(8,128)(2,1)S(1)} collective-permute-done((bf16[32,3200]{1,0:T(8,128)(2,1)S(1)}, bf16[32,3200]{1,0:T(8,128)(2,1)S(1)}, u32[]{:S(2)}, u32[]{:S(2)}) %collective-permute-start.1) | collective-permute-done | bytes 204832 | tf_op jit(solution)/shard_map/ppermute | solution.py:924
  51.1 2.9 all-to-all-done.x_ref.refs_7_
  55.6 3.5 collective-permute-start.3
  60.6 15.3 %collective-permute-done.3 = bf16[2,32,3200]{2,1,0:T(8,128)(2,1)S(1)} collective-permute-done((bf16[2,32,3200]{2,1,0:T(8,128)(2,1)S(1)}, bf16[2,32,3200]{2,1,0:T(8,128)(2,1)S(1)}, u32[]{:S(2)}, u32[]{:S(2)}) %collective-permute-start.3) | collective-permute-done | bytes 409632 | tf_op jit(solution)/shard_map/ppermute | solution.py:924
  80.3 3.0 collective-permute-start.8
  84.7 19.0 %collective-permute-done.7 = bf16[32,5120]{1,0:T(8,128)(2,1)S(1)} collective-permute-done((bf16[32,5120]{1,0:T(8,128)(2,1)S(1)}, bf16[32,5120]{1,0:T(8,128)(2,1)S(1)}, u32[]{:S(2)}, u32[]{:S(2)}) %collective-permute-start.7) | collective-permute-done | bytes 327712 | tf_op jit(solution)/shard_map/ppermute | solution.py:924
  103.7 9.3 %collective-permute-done.8 = bf16[32,5120]{1,0:T(8,128)(2,1)S(1)} collective-permute-done((bf16[32,5120]{1,0:T(8,128)(2,1)S(1)}, bf16[32,5120]{1,0:T(8,128)(2,1)S(1)}, u32[]{:S(2)}, u32[]{:S(2)}) %collective-permute-start.8) | collective-permute-done | bytes 327712 | tf_op jit(solution)/shard_map/ppermute | solution.py:924
  122.2 8.1 %put_in_order.2.w_ref.refs_6_ = bf16[1024,3200]{1,0:T(8,128)(2,1)} custom-call(s32[4]{0:T(128)} %get-tuple-element.407.place_ref, bf16[2,2,32,3200]{3,2,1,0:T(8,128)(2,1)} %pad_maximum_fusion.5.refs_0_, bf16[2,2,32,3200]{3,2,1,0:T(8,128)(2,1)} %collective-permute-done.5.refs_1_, bf16[2,2,32,3200]{3,2,1,0:T(8,128)(2,1)} %copy-done.9, ...), custom_call_target="tpu_custom_call" | custom-call | bytes 409600 | tf_op jit(solution)/shard_map/put_in_order/pallas_call | solution.py:446
  132.6 12.5 %qkv.1 = (bf16[1024,1024]{1,0:T(8,128)(2,1)}, bf16[1024,3072]{1,0:T(8,128)(2,1)}) custom-call(bf16[4,288,1024]{2,1,0:T(8,128)(2,1)} %copy-done, bf16[1024,3200]{1,0:T(8,128)(2,1)} %put_in_order.2.w_ref.refs_6_, f32[8,1024]{1,0:T(8,128)} %pad.14.vec_ref), custom_call_target="tpu_custom_call" | custom-call | flops 201326592 | bytes 524288 | tf_op jit(solution)/shard_map/qkv/pallas_call | solution.py:446
  145.1 2.0 collective-permute-done.14
  147.1 3.1 collective-permute-done.15
  157.0 18.5 %attend.1 = (bf16[1024,1024]{1,0:T(8,128)(2,1)}, f32[8,2,1024]{2,1,0:T(2,128)}) custom-call(bf16[1024,3072]{1,0:T(8,128)(2,1)} %get-tuple-element.240.q_ref.k_ref.v_ref, bf16[1024,3072]{1,0:T(8,128)(2,1)} %get-tuple-element.240.q_ref.k_ref.v_ref, bf16[1024,3072]{1,0:T(8,128)(2,1)} %get-tuple-element.240.q_ref.k_ref.v_ref), custom_call_target="tpu_custom_call" | custom-call | flops 268435456 | bytes 262144 | tf_op jit(solution)/shard_map/attend/pallas_call | solution.py:446
  175.4 18.2 %collective-permute-done.16.refs_1_ = bf16[2,2,32,5120]{3,2,1,0:T(8,128)(2,1)} collective-permute-done((bf16[2,2,32,5120]{3,2,1,0:T(8,128)(2,1)S(1)}, bf16[2,2,32,5120]{3,2,1,0:T(8,128)(2,1)}, u32[]{:S(2)}, u32[]{:S(2)}) %collective-permute-start.16) | collective-permute-done | bytes 1310752 | tf_op jit(solution)/shard_map/ppermute | solution.py:924
  197.1 1.9 collective-permute-done.21.refs_7_
  198.9 10.4 %put_in_order.3.ws_ref.wq_ref.wc_ref = bf16[1024,5120]{1,0:T(8,128)(2,1)} custom-call(s32[4]{0:T(128)} %get-tuple-element.407.place_ref, bf16[2,2,32,5120]{3,2,1,0:T(8,128)(2,1)} %copy-done.4, bf16[2,2,32,5120]{3,2,1,0:T(8,128)(2,1)} %collective-permute-done.16.refs_1_, bf16[2,2,32,5120]{3,2,1,0:T(8,128)(2,1)} %copy-done.5, ...), custom_call_target="tpu_custom_call" | custom-call | bytes 655360 | tf_op jit(solution)/shard_map/put_in_order/pallas_call | solution.py:446
  209.3 3.7 fusion.7.kv_ref
  213.0 18.4 %cross.1 = (f32[1024,1024]{1,0:T(8,128)}, bf16[1024,1024]{1,0:T(8,128)(2,1)}, bf16[1024,1024]{1,0:T(8,128)(2,1)}, bf16[1024,1024]{1,0:T(8,128)(2,1)}, f32[1024,1...) custom-call(s32[1]{0:T(128)} %dynamic_slice.3.len_ref, bf16[4,288,1024]{2,1,0:T(8,128)(2,1)} %copy-done, ...), custom_call_target="tpu_custom_call" | custom-call | flops 335544320 | bytes 983040 | tf_op jit(solution)/shard_map/cross/pallas_call | solution.py:446
  231.5 3.8 all-to-all-start.1
  236.5 30.4 %mlp.1 = (bf16[1024,4096]{1,0:T(8,128)(2,1)}, bf16[1024,4096]{1,0:T(8,128)(2,1)}, bf16[1024,1024]{1,0:T(8,128)(2,1)}) custom-call(bf16[1024,1024]{1,0:T(8,128)(2,1)} %get-tuple-element.270.h_ref.refs_0_, bf16[1024,8192]{1,0:T(8,128)(2,1)} %all-gather.2.cloned.1.call-done.wi_ref.wo_ref, bf16[1024,8192]{1,0:T(8,128)(2,1)} %all-gather.2.cloned.1.call-done.wi_ref.wo_ref, ...), custom_call_target="tpu_custom_call" | custom-call | flops 536870912 | bytes 1310720 | tf_op jit(solution)/shard_map/mlp/pallas_call | solution.py:446
  268.2 14.7 %d_mlp_out.1 = (bf16[512,4096]{1,0:T(8,128)(2,1)}, bf16[512,4096]{1,0:T(8,128)(2,1)}) custom-call(s32[4]{0:T(128)} %get-tuple-element.406.place_ref, bf16[1024,4096]{1,0:T(8,128)(2,1)} %get-tuple-element.258.refs_0_, bf16[1024,1024]{1,0:T(8,128)(2,1)} %bitcast.196), custom_call_target="tpu_custom_call" | custom-call | flops 268435456 | bytes 327680 | tf_op jit(solution)/shard_map/d_mlp_out/pallas_call | solution.py:446
  283.1 4.0 all-to-all-start.2
  287.3 15.3 %du.1 = (bf16[1024,4096]{1,0:T(8,128)(2,1)}, f32[4,1,1024]{2,1,0:T(1,128)}) custom-call(bf16[1024,1024]{1,0:T(8,128)(2,1)} %bitcast.197, bf16[1024,8192]{1,0:T(8,128)(2,1)} %all-gather.2.cloned.1.call-done.wi_ref.wo_ref, bf16[1024,4096]{1,0:T(8,128)(2,1)} %get-tuple-element.261.slope_ref), custom_call_target="tpu_custom_call" | custom-call | flops 268435456 | bytes 851968 | tf_op jit(solution)/shard_map/du/pallas_call | solution.py:446
  302.7 3.8 fusion.20
  306.5 14.6 %d_mlp_in.1 = (bf16[512,4096]{1,0:T(8,128)(2,1)}, bf16[512,4096]{1,0:T(8,128)(2,1)}) custom-call(s32[4]{0:T(128)} %get-tuple-element.406.place_ref, bf16[1024,1024]{1,0:T(8,128)(2,1)} %get-tuple-element.270.h_ref.refs_0_, bf16[1024,4096]{1,0:T(8,128)(2,1)} %get-tuple-element.276.refs_1_.du_ref), custom_call_target="tpu_custom_call" | custom-call | flops 268435456 | bytes 327680 | tf_op jit(solution)/shard_map/d_mlp_in/pallas_call | solution.py:446
  321.4 1.9 collective-permute-start.24
  324.8 21.2 %norm3_back.1 = (f32[1024,1024]{1,0:T(8,128)}, bf16[1024,1024]{1,0:T(8,128)(2,1)}, bf16[1024,1024]{1,0:T(8,128)(2,1)}, f32[8,1024]{1,0:T(8,128)}) custom-call(bf16[1024,4096]{1,0:T(8,128)(2,1)} %get-tuple-element.276.refs_1_.du_ref, bf16[1024,8192]{1,0:T(8,128)(2,1)} %all-gather.2.cloned.1.call-done.wi_ref.wo_ref, bf16[1024,1024]{1,0:T(8,128)(2,1)} %bitcast.198, ...), custom_call_target="tpu_custom_call" | custom-call | flops 335544320 | bytes 1048576 | tf_op jit(solution)/shard_map/norm3_back/pallas_call | solution.py:446
  348.8 2.0 copy-done.7
  350.8 3.3 fusion.29
  354.1 3.7 fusion.22
  361.9 21.5 %cross_back.1 = (bf16[1024,1024]{1,0:T(8,128)(2,1)}, bf16[128,2048]{1,0:T(8,128)(2,1)}, f32[1024,1024]{1,0:T(8,128)}, bf16[1024,1024]{1,0:T(8,128)(2,1)}, bf16[1024,1024]{1,0:T(8,128)(2,1)}, /*index=5*/f32[8,1024]{1,0:T(8,128)}) custom-call(s32[1]{0:T(128)} %dynamic_slice.3.len_ref, bf16[1024,1024]{1,0:T(8,128)(2,1)} %get-tuple-element.274.q_ref, ...), custom_call_target="tpu_custom_call" | custom-call | flops 335544320 | bytes 1114112 | tf_op jit(solution)/shard_map/cross_back/pallas_call | solution.py:446
  383.4 17.2 %d_mid.1 = (bf16[512,5120]{1,0:T(8,128)(2,1)}, bf16[512,5120]{1,0:T(8,128)(2,1)}) custom-call(s32[4]{0:T(128)} %get-tuple-element.407.place_ref, bf16[1024,1024]{1,0:T(8,128)(2,1)} %get-tuple-element.247.o_ref.refs_0_, bf16[1024,1024]{1,0:T(8,128)(2,1)} %get-tuple-element.297.refs_1_, bf16[1024,1024]{1,0:T(8,128)(2,1)} %get-tuple-element.275.o_ref.refs_2_, ...), custom_call_target="tpu_custom_call" | custom-call | flops 335544320 | bytes 393216 | tf_op jit(solution)/shard_map/d_mid/pallas_call | solution.py:446
  400.7 2.5 add_convert_fusion.11
  404.3 2.7 fusion.27
  409.1 18.2 %attend_back.2 = (bf16[1024,512]{1,0:T(8,128)(2,1)}, bf16[1024,512]{1,0:T(8,128)(2,1)}, bf16[1024,512]{1,0:T(8,128)(2,1)}) custom-call(bf16[1024,3072]{1,0:T(8,128)(2,1)} %get-tuple-element.240.q_ref.k_ref.v_ref, bf16[1024,3072]{1,0:T(8,128)(2,1)} %get-tuple-element.240.q_ref.k_ref.v_ref, bf16[1024,3072]{1,0:T(8,128)(2,1)} %get-tuple-element.240.q_ref.k_ref.v_ref, ...), custom_call_target="tpu_custom_call" | custom-call | flops 335544320 | bytes 262144 | tf_op jit(solution)/shard_map/attend_back/pallas_call | solution.py:446
  427.3 2.3 add_convert_fusion.9
  430.7 3.8 fusion.11
  436.5 17.9 %attend_back.3 = (bf16[1024,512]{1,0:T(8,128)(2,1)}, bf16[1024,512]{1,0:T(8,128)(2,1)}, bf16[1024,512]{1,0:T(8,128)(2,1)}) custom-call(bf16[1024,3072]{1,0:T(8,128)(2,1)} %get-tuple-element.240.q_ref.k_ref.v_ref, bf16[1024,3072]{1,0:T(8,128)(2,1)} %get-tuple-element.240.q_ref.k_ref.v_ref, bf16[1024,3072]{1,0:T(8,128)(2,1)} %get-tuple-element.240.q_ref.k_ref.v_ref, ...), custom_call_target="tpu_custom_call" | custom-call | flops 335544320 | bytes 262144 | tf_op jit(solution)/shard_map/attend_back/pallas_call | solution.py:446
  454.4 14.1 %d_qkv.1 = (bf16[512,3072]{1,0:T(8,128)(2,1)}, bf16[512,3072]{1,0:T(8,128)(2,1)}) custom-call(s32[4]{0:T(128)} %get-tuple-element.407.place_ref, bf16[1024,1024]{1,0:T(8,128)(2,1)} %get-tuple-element.273.refs_0_, bf16[1024,512]{1,0:T(8,128)(2,1)} %get-tuple-element.330.refs_1_.refs_0_, bf16[1024,512]{1,0:T(8,128)(2,1)} %get-tuple-element.331.refs_2_.refs_1_, ...), custom_call_target="tpu_custom_call" | custom-call | flops 201326592 | bytes 262144 | tf_op jit(solution)/shard_map/d_qkv/pallas_call | solution.py:446
  470.5 4.4 fusion.16.refs_10_
  474.9 5.4 fusion.12
  480.3 3.1 fusion.32
  487.5 14.6 %norm1_back.1 = (bf16[4,288,1024]{2,1,0:T(8,128)(2,1)}, f32[8,1024]{1,0:T(8,128)}) custom-call(bf16[1024,512]{1,0:T(8,128)(2,1)} %get-tuple-element.330.refs_1_.refs_0_, bf16[1024,512]{1,0:T(8,128)(2,1)} %get-tuple-element.331.refs_2_.refs_1_, bf16[1024,512]{1,0:T(8,128)(2,1)} %get-tuple-element.332.refs_3_.refs_2_, ...), custom_call_target="tpu_custom_call" | custom-call | flops 201326592 | bytes 589824 | tf_op jit(solution)/shard_map/norm1_back/pallas_call | solution.py:446
  502.2 3.9 all-to-all-start.3
  506.1 12.5 %collective-permute-done.38 = bf16[2,32,5120]{2,1,0:T(8,128)(2,1)} collective-permute-done((bf16[2,32,5120]{2,1,0:T(8,128)(2,1)}, bf16[2,32,5120]{2,1,0:T(8,128)(2,1)}, u32[]{:S(2)}, u32[]{:S(2)}) %collective-permute-start.38) | collective-permute-done | bytes 655392 | tf_op jit(solution)/shard_map/ppermute | solution.py:924
  518.6 1.8 fusion.41
  520.4 4.1 fusion.33
  524.5 2.1 fusion.43
  529.8 1.8 collective-permute-start.42
  531.6 2.1 collective-permute-start.43
  536.7 3.0 reshape.410
  539.6 4.7 copy.83
  544.3 4.4 reshape.402
  549.2 8.4 %collective-permute-done.43 = bf16[32,5120]{1,0:T(8,128)(2,1)} collective-permute-done((bf16[32,5120]{1,0:T(8,128)(2,1)}, bf16[32,5120]{1,0:T(8,128)(2,1)}, u32[]{:S(2)}, u32[]{:S(2)}) %collective-permute-start.43) | collective-permute-done | bytes 327712 | tf_op jit(solution)/shard_map/ppermute | solution.py:924
  558.4 2.5 slice.670
  560.9 1.9 fusion.46
  565.2 5.7 all-to-all-start.4
  571.0 1.8 collective-permute-start.45
  572.8 2.4 collective-permute-start.46
  580.9 2.6 collective-permute-done.45
  583.5 6.7 %collective-permute-done.46 = bf16[32,3072]{1,0:T(8,128)(2,1)} collective-permute-done((bf16[32,3072]{1,0:T(8,128)(2,1)}, bf16[32,3072]{1,0:T(8,128)(2,1)}, u32[]{:S(2)}, u32[]{:S(2)}) %collective-permute-start.46) | collective-permute-done | bytes 196640 | tf_op jit(solution)/shard_map/ppermute | solution.py:924
  (276 shorter events, 83.9 us)
Async XLA Ops:
  7.2 229.3 %all-gather.2.cloned.1.call-start = ((), (), s32[]{:S(2)}) async-start(), calls=%async_computation.7 | async-start | bytes 17301504 | tf_op jit(solution)/shard_map/all_gather | solution.py:1021
  16.8 37.2 %all-to-all-start = ((bf16[4,288,1024]{2,1,0:T(8,128)(2,1)}), bf16[4,288,1024]{2,1,0:T(8,128)(2,1)S(1)}, u32[]{:S(2)}, u32[]{:S(2)}) async-start(bf16[4,288,1024]{2,1,0:T(8,128)(2,1)} %pad_maximum_fusion), calls=%async_computation | async-start | bytes 4718592 | tf_op jit(solution)/shard_map/all_to_all | solution.py:1045
  23.1 12.3 %collective-permute-start.2 = (bf16[32,3200]{1,0:T(8,128)(2,1)S(1)}, bf16[32,3200]{1,0:T(8,128)(2,1)S(1)}, u32[]{:S(2)}, u32[]{:S(2)}) collective-permute-start(bf16[32,3200]{1,0:T(8,128)(2,1)S(1)} %get-tuple-element.461), channel_id=1, source_target_pairs={{0,24},{1,25},{2,26},{3,27},{4,28},{5,29},{6,30},{7,31},{8,16},{9,... | collective-permute-start | bytes 614408 | tf_op jit(solution)/shard_map/ppermute | solution.py:924
  26.7 24.4 %collective-permute-start.1 = (bf16[32,3200]{1,0:T(8,128)(2,1)S(1)}, bf16[32,3200]{1,0:T(8,128)(2,1)S(1)}, u32[]{:S(2)}, u32[]{:S(2)}) collective-permute-start(bf16[32,3200]{1,0:T(8,128)(2,1)S(1)} %get-tuple-element.461), channel_id=1, source_target_pairs={{0,16},{1,17},{2,18},{3,19},{4,20},{5,21},{6,22},{7,23},{8,24},{9,... | collective-permute-start | bytes 614408 | tf_op jit(solution)/shard_map/ppermute | solution.py:924
  26.7 24.4 %collective-permute-start = (bf16[32,3200]{1,0:T(8,128)(2,1)S(1)}, bf16[32,3200]{1,0:T(8,128)(2,1)S(1)}, u32[]{:S(2)}, u32[]{:S(2)}) collective-permute-start(bf16[32,3200]{1,0:T(8,128)(2,1)S(1)} %get-tuple-element.461), channel_id=1, source_target_pairs={{0,8},{1,9},{2,10},{3,11},{4,12},{5,13},{6,14},{7,15},{8,0},{9,1},... | collective-permute-start | bytes 614408 | tf_op jit(solution)/shard_map/ppermute | solution.py:924
  54.0 25.5 %copy-start = (bf16[4,288,1024]{2,1,0:T(8,128)(2,1)}, bf16[4,288,1024]{2,1,0:T(8,128)(2,1)S(1)}, u32[]{:S(2)}) copy-start(bf16[4,288,1024]{2,1,0:T(8,128)(2,1)S(1)} %all-to-all-done.x_ref.refs_7_) | copy-start | bytes 7077892
  55.6 20.3 %collective-permute-start.3 = (bf16[2,32,3200]{2,1,0:T(8,128)(2,1)S(1)}, bf16[2,32,3200]{2,1,0:T(8,128)(2,1)S(1)}, u32[]{:S(2)}, u32[]{:S(2)}) collective-permute-start(bf16[2,32,3200]{2,1,0:T(8,128)(2,1)S(1)} %get-tuple-element.212), channel_id=1, source_target_pairs={{0,1},{1,0},{2,3},{3,2},{4,5},{5,4},{6,7},{7,6},{8,9},{9,8},{10,11... | collective-permute-start | bytes 1228808 | tf_op jit(solution)/shard_map/ppermute | solution.py:924
  59.1 17.7 %collective-permute-start.4 = (bf16[2,32,3200]{2,1,0:T(8,128)(2,1)S(1)}, bf16[2,32,3200]{2,1,0:T(8,128)(2,1)S(1)}, u32[]{:S(2)}, u32[]{:S(2)}) collective-permute-start(bf16[2,32,3200]{2,1,0:T(8,128)(2,1)S(1)} %get-tuple-element.213), channel_id=1, source_target_pairs={{0,2},{1,3},{2,0},{3,1},{4,6},{5,7},{6,4},{7,5},{8,10},{9,11},{10,... | collective-permute-start | bytes 1228808 | tf_op jit(solution)/shard_map/ppermute | solution.py:924
  76.9 38.9 %copy-start.9 = (bf16[2,2,32,3200]{3,2,1,0:T(8,128)(2,1)}, bf16[2,2,32,3200]{3,2,1,0:T(8,128)(2,1)S(1)}, u32[]{:S(2)}) copy-start(bf16[2,2,32,3200]{3,2,1,0:T(8,128)(2,1)S(1)} %pad_maximum_fusion.6.refs_2_) | copy-start | bytes 2457604
  76.9 36.2 %collective-permute-start.6 = (bf16[2,2,32,3200]{3,2,1,0:T(8,128)(2,1)S(1)}, bf16[2,2,32,3200]{3,2,1,0:T(8,128)(2,1)}, u32[]{:S(2)}, u32[]{:S(2)}) collective-permute-start(bf16[2,2,32,3200]{3,2,1,0:T(8,128)(2,1)S(1)} %pad_maximum_fusion.6.refs_2_), channel_id=1, source_target_pairs={{0,1},{1,0},{2,3},{3,2},{4,5},{5,4},{6,7},{7,6},{8,9},{9,8},{10,11... | collective-permute-start | bytes 2457608 | tf_op jit(solution)/shard_map/ppermute | solution.py:924
  79.5 36.8 %copy-start.42 = (s32[4]{0:T(128)S(1)}, s32[4]{0:T(128)}, u32[]{:S(2)}) copy-start(s32[4]{0:T(128)} %constant.48.clone) | copy-start | bytes 52
  79.5 33.6 %collective-permute-start.5 = (bf16[2,2,32,3200]{3,2,1,0:T(8,128)(2,1)}, bf16[2,2,32,3200]{3,2,1,0:T(8,128)(2,1)}, u32[]{:S(2)}, u32[]{:S(2)}) collective-permute-start(bf16[2,2,32,3200]{3,2,1,0:T(8,128)(2,1)} %pad_maximum_fusion.5.refs_0_), channel_id=1, source_target_pairs={{0,2},{1,3},{2,0},{3,1},{4,6},{5,7},{6,4},{7,5},{8,10},{9,11},{10,... | collective-permute-start | bytes 2457608 | tf_op jit(solution)/shard_map/ppermute | solution.py:924
  80.3 23.4 %collective-permute-start.7 = (bf16[32,5120]{1,0:T(8,128)(2,1)S(1)}, bf16[32,5120]{1,0:T(8,128)(2,1)S(1)}, u32[]{:S(2)}, u32[]{:S(2)}) collective-permute-start(bf16[32,5120]{1,0:T(8,128)(2,1)S(1)} %constant_dynamic-update-slice_fusion), channel_id=1, source_target_pairs={{0,8},{1,9},{2,10},{3,11},{4,12},{5,13},{6,14},{7,15},{8,0},{9,1},... | collective-permute-start | bytes 983048 | tf_op jit(solution)/shard_map/ppermute | solution.py:924
  80.3 32.7 %collective-permute-start.8 = (bf16[32,5120]{1,0:T(8,128)(2,1)S(1)}, bf16[32,5120]{1,0:T(8,128)(2,1)S(1)}, u32[]{:S(2)}, u32[]{:S(2)}) collective-permute-start(bf16[32,5120]{1,0:T(8,128)(2,1)S(1)} %constant_dynamic-update-slice_fusion), channel_id=1, source_target_pairs={{0,16},{1,17},{2,18},{3,19},{4,20},{5,21},{6,22},{7,23},{8,24},{9,... | collective-permute-start | bytes 983048 | tf_op jit(solution)/shard_map/ppermute | solution.py:924
  83.4 29.7 %collective-permute-start.9 = (bf16[32,5120]{1,0:T(8,128)(2,1)S(1)}, bf16[32,5120]{1,0:T(8,128)(2,1)S(1)}, u32[]{:S(2)}, u32[]{:S(2)}) collective-permute-start(bf16[32,5120]{1,0:T(8,128)(2,1)S(1)} %constant_dynamic-update-slice_fusion), channel_id=1, source_target_pairs={{0,24},{1,25},{2,26},{3,27},{4,28},{5,29},{6,30},{7,31},{8,16},{9,... | collective-permute-start | bytes 983048 | tf_op jit(solution)/shard_map/ppermute | solution.py:924
  115.2 3.7 collective-permute-start.10
  115.2 5.1 collective-permute-start.11
  115.8 5.4 collective-permute-start.12
  115.8 6.5 %collective-permute-start.13 = (bf16[2,2,32,3200]{3,2,1,0:T(8,128)(2,1)}, bf16[2,2,32,3200]{3,2,1,0:T(8,128)(2,1)}, u32[]{:S(2)}, u32[]{:S(2)}) collective-permute-start(bf16[2,2,32,3200]{3,2,1,0:T(8,128)(2,1)} %collective-permute-done.6.refs_3_), channel_id=1, source_target_pairs={{0,4},{1,5},{2,6},{3,7},{4,0},{5,1},{6,2},{7,3},{8,12},{9,13},{10,... | collective-permute-start | bytes 2457608 | tf_op jit(solution)/shard_map/ppermute | solution.py:924
  116.9 30.2 %collective-permute-start.14 = (bf16[2,32,5120]{2,1,0:T(8,128)(2,1)}, bf16[2,32,5120]{2,1,0:T(8,128)(2,1)}, u32[]{:S(2)}, u32[]{:S(2)}) collective-permute-start(bf16[2,32,5120]{2,1,0:T(8,128)(2,1)} %get-tuple-element.234), channel_id=1, source_target_pairs={{0,1},{1,0},{2,3},{3,2},{4,5},{5,4},{6,7},{7,6},{8,9},{9,8},{10,11... | collective-permute-start | bytes 1966088 | tf_op jit(solution)/shard_map/ppermute | solution.py:924
  118.9 31.3 %collective-permute-start.15 = (bf16[2,32,5120]{2,1,0:T(8,128)(2,1)}, bf16[2,32,5120]{2,1,0:T(8,128)(2,1)}, u32[]{:S(2)}, u32[]{:S(2)}) collective-permute-start(bf16[2,32,5120]{2,1,0:T(8,128)(2,1)} %get-tuple-element.235), channel_id=1, source_target_pairs={{0,2},{1,3},{2,0},{3,1},{4,6},{5,7},{6,4},{7,5},{8,10},{9,11},{10,... | collective-permute-start | bytes 1966088 | tf_op jit(solution)/shard_map/ppermute | solution.py:924
  151.4 24.0 %copy-start.4 = (bf16[2,2,32,5120]{3,2,1,0:T(8,128)(2,1)}, bf16[2,2,32,5120]{3,2,1,0:T(8,128)(2,1)S(1)}, u32[]{:S(2)}) copy-start(bf16[2,2,32,5120]{3,2,1,0:T(8,128)(2,1)S(1)} %pad_maximum_fusion.1.refs_0_) | copy-start | bytes 3932164
  153.2 22.3 %copy-start.5 = (bf16[2,2,32,5120]{3,2,1,0:T(8,128)(2,1)}, bf16[2,2,32,5120]{3,2,1,0:T(8,128)(2,1)S(1)}, u32[]{:S(2)}) copy-start(bf16[2,2,32,5120]{3,2,1,0:T(8,128)(2,1)S(1)} %pad_maximum_fusion.2.refs_2_) | copy-start | bytes 3932164
  153.2 41.0 %copy-start.43 = (s32[4]{0:T(128)S(1)}, s32[4]{0:T(128)}, u32[]{:S(2)}) copy-start(s32[4]{0:T(128)} %param.26) | copy-start | bytes 52
  153.2 40.5 %collective-permute-start.16 = (bf16[2,2,32,5120]{3,2,1,0:T(8,128)(2,1)S(1)}, bf16[2,2,32,5120]{3,2,1,0:T(8,128)(2,1)}, u32[]{:S(2)}, u32[]{:S(2)}) collective-permute-start(bf16[2,2,32,5120]{3,2,1,0:T(8,128)(2,1)S(1)} %pad_maximum_fusion.1.refs_0_), channel_id=1, source_target_pairs={{0,2},{1,3},{2,0},{3,1},{4,6},{5,7},{6,4},{7,5},{8,10},{9,11},{10,... | collective-permute-start | bytes 3932168 | tf_op jit(solution)/shard_map/ppermute | solution.py:924
  154.9 38.7 %collective-permute-start.17 = (bf16[2,2,32,5120]{3,2,1,0:T(8,128)(2,1)S(1)}, bf16[2,2,32,5120]{3,2,1,0:T(8,128)(2,1)}, u32[]{:S(2)}, u32[]{:S(2)}) collective-permute-start(bf16[2,2,32,5120]{3,2,1,0:T(8,128)(2,1)S(1)} %pad_maximum_fusion.2.refs_2_), channel_id=1, source_target_pairs={{0,1},{1,0},{2,3},{3,2},{4,5},{5,4},{6,7},{7,6},{8,9},{9,8},{10,11... | collective-permute-start | bytes 3932168 | tf_op jit(solution)/shard_map/ppermute | solution.py:924
  156.5 40.3 %collective-permute-start.20 = (bf16[2,2,32,5120]{3,2,1,0:T(8,128)(2,1)S(1)}, bf16[2,2,32,5120]{3,2,1,0:T(8,128)(2,1)}, u32[]{:S(2)}, u32[]{:S(2)}) collective-permute-start(bf16[2,2,32,5120]{3,2,1,0:T(8,128)(2,1)S(1)} %pad_maximum_fusion.2.refs_2_), channel_id=1, source_target_pairs={{0,4},{1,5},{2,6},{3,7},{4,0},{5,1},{6,2},{7,3},{8,12},{9,13},{10,... | collective-permute-start | bytes 3932168 | tf_op jit(solution)/shard_map/ppermute | solution.py:924
  156.5 40.3 %collective-permute-start.18 = (bf16[2,2,32,5120]{3,2,1,0:T(8,128)(2,1)S(1)}, bf16[2,2,32,5120]{3,2,1,0:T(8,128)(2,1)}, u32[]{:S(2)}, u32[]{:S(2)}) collective-permute-start(bf16[2,2,32,5120]{3,2,1,0:T(8,128)(2,1)S(1)} %pad_maximum_fusion.1.refs_0_), channel_id=1, source_target_pairs={{0,4},{1,5},{2,6},{3,7},{4,0},{5,1},{6,2},{7,3},{8,12},{9,13},{10,... | collective-permute-start | bytes 3932168 | tf_op jit(solution)/shard_map/ppermute | solution.py:924
  193.7 3.4 collective-permute-start.19
  193.7 5.2 collective-permute-start.21
  231.5 35.4 %all-to-all-start.1 = ((bf16[4,256,1024]{2,1,0:T(8,128)(2,1)}), bf16[4,256,1024]{2,1,0:T(8,128)(2,1)S(1)}, u32[]{:S(2)}, u32[]{:S(2)}) async-start(bf16[4,256,1024]{2,1,0:T(8,128)(2,1)} %param.27), calls=%async_computation.1 | async-start | bytes 4194304 | tf_op jit(solution)/shard_map/all_to_all | solution.py:1136
  282.9 19.7 %collective-permute-start.22 = (bf16[2,2,2,2,32,4096]{5,4,3,2,1,0:T(8,128)(2,1)}, bf16[2,2,2,2,32,4096]{5,4,3,2,1,0:T(8,128)(2,1)}, u32[]{:S(2)}, u32[]{:S(2)}) collective-permute-start(bf16[2,2,2,2,32,4096]{5,4,3,2,1,0:T(8,128)(2,1)} %bitcast.237), channel_id=1, source_target_pairs={{0,4},{1,5},{2,6},{3,7},{4,0},{5,1},{6,2},{7,3},{8,12},{9,13},{10,... | collective-permute-start | bytes 12582920 | tf_op jit(solution)/shard_map/ppermute | solution.py:924
  283.1 38.1 %all-to-all-start.2 = ((bf16[4,256,1024]{2,1,0:T(8,128)(2,1)}), bf16[4,256,1024]{2,1,0:T(8,128)(2,1)S(1)}, u32[]{:S(2)}, u32[]{:S(2)}) async-start(bf16[4,256,1024]{2,1,0:T(8,128)(2,1)} %bitcast.215), calls=%async_computation.2 | async-start | bytes 4194304 | tf_op jit(solution)/shard_map/all_to_all | solution.py:1160
  287.1 247.1 %reduce-scatter.3.cloned.1.call-start = ((), (), s32[]{:S(2)}) async-start(), calls=%async_computation.8 | async-start | bytes 1310720 | tf_op jit(solution)/shard_map/reduce_scatter | solution.py:987
  321.1 24.8 %copy-start.2 = (bf16[4,256,1024]{2,1,0:T(8,128)(2,1)}, bf16[4,256,1024]{2,1,0:T(8,128)(2,1)S(1)}, u32[]{:S(2)}) copy-start(bf16[4,256,1024]{2,1,0:T(8,128)(2,1)S(1)} %all-to-all-done.2) | copy-start | bytes 6291460
  321.1 27.7 %collective-permute-start.23 = (bf16[2,2,2,2,32,4096]{5,4,3,2,1,0:T(8,128)(2,1)}, bf16[2,2,2,2,32,4096]{5,4,3,2,1,0:T(8,128)(2,1)S(1)}, u32[]{:S(2)}, u32[]{:S(2)}) collective-permute-start(bf16[2,2,2,2,32,4096]{5,4,3,2,1,0:T(8,128)(2,1)} %bitcast.236), channel_id=1, source_target_pairs={{0,4},{1,5},{2,6},{3,7},{4,0},{5,1},{6,2},{7,3},{8,12},{9,13},{10,... | collective-permute-start | bytes 12582920 | tf_op jit(solution)/shard_map/ppermute | solution.py:924
  321.4 25.8 %collective-permute-start.24 = (bf16[2,2,32,4096]{3,2,1,0:T(8,128)(2,1)}, bf16[2,2,32,4096]{3,2,1,0:T(8,128)(2,1)S(1)}, u32[]{:S(2)}, u32[]{:S(2)}) collective-permute-start(bf16[2,2,32,4096]{3,2,1,0:T(8,128)(2,1)} %get-tuple-element.281), channel_id=1, source_target_pairs={{0,2},{1,3},{2,0},{3,1},{4,6},{5,7},{6,4},{7,5},{8,10},{9,11},{10,... | collective-permute-start | bytes 3145736 | tf_op jit(solution)/shard_map/ppermute | solution.py:924
  323.3 25.5 %collective-permute-start.25 = (bf16[2,2,32,4096]{3,2,1,0:T(8,128)(2,1)}, bf16[2,2,32,4096]{3,2,1,0:T(8,128)(2,1)}, u32[]{:S(2)}, u32[]{:S(2)}) collective-permute-start(bf16[2,2,32,4096]{3,2,1,0:T(8,128)(2,1)} %get-tuple-element.282), channel_id=1, source_target_pairs={{0,1},{1,0},{2,3},{3,2},{4,5},{5,4},{6,7},{7,6},{8,9},{9,8},{10,11... | collective-permute-start | bytes 3145736 | tf_op jit(solution)/shard_map/ppermute | solution.py:924
  357.8 42.9 %collective-permute-start.26 = (bf16[2,2,32,4096]{3,2,1,0:T(8,128)(2,1)}, bf16[2,2,32,4096]{3,2,1,0:T(8,128)(2,1)S(1)}, u32[]{:S(2)}, u32[]{:S(2)}) collective-permute-start(bf16[2,2,32,4096]{3,2,1,0:T(8,128)(2,1)} %get-tuple-element.302), channel_id=1, source_target_pairs={{0,2},{1,3},{2,0},{3,1},{4,6},{5,7},{6,4},{7,5},{8,10},{9,11},{10,... | collective-permute-start | bytes 3145736 | tf_op jit(solution)/shard_map/ppermute | solution.py:924
  358.2 42.5 %collective-permute-start.27 = (bf16[2,2,32,4096]{3,2,1,0:T(8,128)(2,1)}, bf16[2,2,32,4096]{3,2,1,0:T(8,128)(2,1)S(1)}, u32[]{:S(2)}, u32[]{:S(2)}) collective-permute-start(bf16[2,2,32,4096]{3,2,1,0:T(8,128)(2,1)} %get-tuple-element.303), channel_id=1, source_target_pairs={{0,1},{1,0},{2,3},{3,2},{4,5},{5,4},{6,7},{7,6},{8,9},{9,8},{10,11... | collective-permute-start | bytes 3145736 | tf_op jit(solution)/shard_map/ppermute | solution.py:924
  359.8 40.8 %collective-permute-start.28 = (bf16[2,32,4096]{2,1,0:T(8,128)(2,1)}, bf16[2,32,4096]{2,1,0:T(8,128)(2,1)S(1)}, u32[]{:S(2)}, u32[]{:S(2)}) collective-permute-start(bf16[2,32,4096]{2,1,0:T(8,128)(2,1)} %get-tuple-element.304), channel_id=1, source_target_pairs={{0,1},{1,0},{2,3},{3,2},{4,5},{5,4},{6,7},{7,6},{8,9},{9,8},{10,11... | collective-permute-start | bytes 1572872 | tf_op jit(solution)/shard_map/ppermute | solution.py:924
  360.2 40.5 %collective-permute-start.29 = (bf16[2,32,4096]{2,1,0:T(8,128)(2,1)}, bf16[2,32,4096]{2,1,0:T(8,128)(2,1)}, u32[]{:S(2)}, u32[]{:S(2)}) collective-permute-start(bf16[2,32,4096]{2,1,0:T(8,128)(2,1)} %get-tuple-element.305), channel_id=1, source_target_pairs={{0,2},{1,3},{2,0},{3,1},{4,6},{5,7},{6,4},{7,5},{8,10},{9,11},{10,... | collective-permute-start | bytes 1572872 | tf_op jit(solution)/shard_map/ppermute | solution.py:924
  404.3 26.4 %slice-start = ((s8[5242880]{0:T(1024)(128)(4,1)}), s8[1048576]{0:T(1024)(128)(4,1)S(1)}, s32[]{:S(2)}) async-start(s8[5242880]{0:T(1024)(128)(4,1)} %bitcast.201), calls=%async_computation.10 | async-start | bytes 2097152
  407.0 20.2 %collective-permute-start.30 = (bf16[2,2,2,2,32,5120]{5,4,3,2,1,0:T(8,128)(2,1)}, bf16[2,2,2,2,32,5120]{5,4,3,2,1,0:T(8,128)(2,1)}, u32[]{:S(2)}, u32[]{:S(2)}) collective-permute-start(bf16[2,2,2,2,32,5120]{5,4,3,2,1,0:T(8,128)(2,1)} %bitcast.235), channel_id=1, source_target_pairs={{0,4},{1,5},{2,6},{3,7},{4,0},{5,1},{6,2},{7,3},{8,12},{9,13},{10,... | collective-permute-start | bytes 15728648 | tf_op jit(solution)/shard_map/ppermute | solution.py:924
  407.0 20.2 %collective-permute-start.31 = (bf16[2,32,4096]{2,1,0:T(8,128)(2,1)}, bf16[2,32,4096]{2,1,0:T(8,128)(2,1)S(1)}, u32[]{:S(2)}, u32[]{:S(2)}) collective-permute-start(bf16[2,32,4096]{2,1,0:T(8,128)(2,1)} %get-tuple-element.320), channel_id=1, source_target_pairs={{0,1},{1,0},{2,3},{3,2},{4,5},{5,4},{6,7},{7,6},{8,9},{9,8},{10,11... | collective-permute-start | bytes 1572872 | tf_op jit(solution)/shard_map/ppermute | solution.py:924
  408.5 18.7 %collective-permute-start.32 = (bf16[2,32,4096]{2,1,0:T(8,128)(2,1)}, bf16[2,32,4096]{2,1,0:T(8,128)(2,1)}, u32[]{:S(2)}, u32[]{:S(2)}) collective-permute-start(bf16[2,32,4096]{2,1,0:T(8,128)(2,1)} %get-tuple-element.321), channel_id=1, source_target_pairs={{0,2},{1,3},{2,0},{3,1},{4,6},{5,7},{6,4},{7,5},{8,10},{9,11},{10,... | collective-permute-start | bytes 1572872 | tf_op jit(solution)/shard_map/ppermute | solution.py:924
  434.5 34.0 %collective-permute-start.33 = (bf16[2,2,32,5120]{3,2,1,0:T(8,128)(2,1)}, bf16[2,2,32,5120]{3,2,1,0:T(8,128)(2,1)S(1)}, u32[]{:S(2)}, u32[]{:S(2)}) collective-permute-start(bf16[2,2,32,5120]{3,2,1,0:T(8,128)(2,1)} %get-tuple-element.339), channel_id=1, source_target_pairs={{0,2},{1,3},{2,0},{3,1},{4,6},{5,7},{6,4},{7,5},{8,10},{9,11},{10,... | collective-permute-start | bytes 3932168 | tf_op jit(solution)/shard_map/ppermute | solution.py:924
  435.9 32.5 %collective-permute-start.34 = (bf16[2,2,32,5120]{3,2,1,0:T(8,128)(2,1)S(1)}, bf16[2,2,32,5120]{3,2,1,0:T(8,128)(2,1)}, u32[]{:S(2)}, u32[]{:S(2)}) collective-permute-start(bf16[2,2,32,5120]{3,2,1,0:T(8,128)(2,1)S(1)} %get-tuple-element.340), channel_id=1, source_target_pairs={{0,1},{1,0},{2,3},{3,2},{4,5},{5,4},{6,7},{7,6},{8,9},{9,8},{10,11... | collective-permute-start | bytes 3932168 | tf_op jit(solution)/shard_map/ppermute | solution.py:924
  468.5 11.8 %collective-permute-start.35 = (bf16[2,2,2,2,32,3072]{5,4,3,2,1,0:T(8,128)(2,1)}, bf16[2,2,2,2,32,3072]{5,4,3,2,1,0:T(8,128)(2,1)}, u32[]{:S(2)}, u32[]{:S(2)}) collective-permute-start(bf16[2,2,2,2,32,3072]{5,4,3,2,1,0:T(8,128)(2,1)} %bitcast.238), channel_id=1, source_target_pairs={{0,4},{1,5},{2,6},{3,7},{4,0},{5,1},{6,2},{7,3},{8,12},{9,13},{10,... | collective-permute-start | bytes 9437192 | tf_op jit(solution)/shard_map/ppermute | solution.py:924
  469.6 67.1 %reduce-scatter.5.cloned.1.call-start = ((), (), s32[]{:S(2)}) async-start(), calls=%async_computation.9 | async-start | bytes 1310720 | tf_op jit(solution)/shard_map/reduce_scatter | solution.py:987
  483.5 35.1 %collective-permute-start.36 = (bf16[2,2,32,3072]{3,2,1,0:T(8,128)(2,1)}, bf16[2,2,32,3072]{3,2,1,0:T(8,128)(2,1)}, u32[]{:S(2)}, u32[]{:S(2)}) collective-permute-start(bf16[2,2,32,3072]{3,2,1,0:T(8,128)(2,1)} %get-tuple-element.357), channel_id=1, source_target_pairs={{0,2},{1,3},{2,0},{3,1},{4,6},{5,7},{6,4},{7,5},{8,10},{9,11},{10,... | collective-permute-start | bytes 2359304 | tf_op jit(solution)/shard_map/ppermute | solution.py:924
  483.8 34.7 %collective-permute-start.37 = (bf16[2,2,32,3072]{3,2,1,0:T(8,128)(2,1)}, bf16[2,2,32,3072]{3,2,1,0:T(8,128)(2,1)}, u32[]{:S(2)}, u32[]{:S(2)}) collective-permute-start(bf16[2,2,32,3072]{3,2,1,0:T(8,128)(2,1)} %get-tuple-element.358), channel_id=1, source_target_pairs={{0,1},{1,0},{2,3},{3,2},{4,5},{5,4},{6,7},{7,6},{8,9},{9,8},{10,11... | collective-permute-start | bytes 2359304 | tf_op jit(solution)/shard_map/ppermute | solution.py:924
  485.5 33.1 %collective-permute-start.38 = (bf16[2,32,5120]{2,1,0:T(8,128)(2,1)}, bf16[2,32,5120]{2,1,0:T(8,128)(2,1)}, u32[]{:S(2)}, u32[]{:S(2)}) collective-permute-start(bf16[2,32,5120]{2,1,0:T(8,128)(2,1)} %get-tuple-element.359), channel_id=1, source_target_pairs={{0,1},{1,0},{2,3},{3,2},{4,5},{5,4},{6,7},{7,6},{8,9},{9,8},{10,11... | collective-permute-start | bytes 1966088 | tf_op jit(solution)/shard_map/ppermute | solution.py:924
  485.9 32.7 %collective-permute-start.39 = (bf16[2,32,5120]{2,1,0:T(8,128)(2,1)}, bf16[2,32,5120]{2,1,0:T(8,128)(2,1)}, u32[]{:S(2)}, u32[]{:S(2)}) collective-permute-start(bf16[2,32,5120]{2,1,0:T(8,128)(2,1)} %get-tuple-element.360), channel_id=1, source_target_pairs={{0,2},{1,3},{2,0},{3,1},{4,6},{5,7},{6,4},{7,5},{8,10},{9,11},{10,... | collective-permute-start | bytes 1966088 | tf_op jit(solution)/shard_map/ppermute | solution.py:924
  502.2 55.4 %all-to-all-start.3 = ((bf16[4,288,1024]{2,1,0:T(8,128)(2,1)}), bf16[4,288,1024]{2,1,0:T(8,128)(2,1)S(1)}, u32[]{:S(2)}, u32[]{:S(2)}) async-start(bf16[4,288,1024]{2,1,0:T(8,128)(2,1)} %get-tuple-element.376), calls=%async_computation.3 | async-start | bytes 4718592 | tf_op jit(solution)/shard_map/all_to_all | solution.py:1278
  526.6 30.9 %collective-permute-start.40 = (bf16[2,32,3072]{2,1,0:T(8,128)(2,1)}, bf16[2,32,3072]{2,1,0:T(8,128)(2,1)}, u32[]{:S(2)}, u32[]{:S(2)}) collective-permute-start(bf16[2,32,3072]{2,1,0:T(8,128)(2,1)} %get-tuple-element.365), channel_id=1, source_target_pairs={{0,1},{1,0},{2,3},{3,2},{4,5},{5,4},{6,7},{7,6},{8,9},{9,8},{10,11... | collective-permute-start | bytes 1179656 | tf_op jit(solution)/shard_map/ppermute | solution.py:924
  528.3 29.3 %collective-permute-start.41 = (bf16[2,32,3072]{2,1,0:T(8,128)(2,1)}, bf16[2,32,3072]{2,1,0:T(8,128)(2,1)}, u32[]{:S(2)}, u32[]{:S(2)}) collective-permute-start(bf16[2,32,3072]{2,1,0:T(8,128)(2,1)} %get-tuple-element.366), channel_id=1, source_target_pairs={{0,2},{1,3},{2,0},{3,1},{4,6},{5,7},{6,4},{7,5},{8,10},{9,11},{10,... | collective-permute-start | bytes 1179656 | tf_op jit(solution)/shard_map/ppermute | solution.py:924
  529.8 19.4 %collective-permute-start.42 = (bf16[32,5120]{1,0:T(8,128)(2,1)}, bf16[32,5120]{1,0:T(8,128)(2,1)}, u32[]{:S(2)}, u32[]{:S(2)}) collective-permute-start(bf16[32,5120]{1,0:T(8,128)(2,1)} %fusion.41), channel_id=1, source_target_pairs={{0,8},{1,9},{2,10},{3,11},{4,12},{5,13},{6,14},{7,15},{8,0},{9,1},... | collective-permute-start | bytes 983048 | tf_op jit(solution)/shard_map/ppermute | solution.py:924
  531.6 25.9 %collective-permute-start.43 = (bf16[32,5120]{1,0:T(8,128)(2,1)}, bf16[32,5120]{1,0:T(8,128)(2,1)}, u32[]{:S(2)}, u32[]{:S(2)}) collective-permute-start(bf16[32,5120]{1,0:T(8,128)(2,1)} %get-tuple-element.368), channel_id=1, source_target_pairs={{0,16},{1,17},{2,18},{3,19},{4,20},{5,21},{6,22},{7,23},{8,24},{9,... | collective-permute-start | bytes 983048 | tf_op jit(solution)/shard_map/ppermute | solution.py:924
  533.7 23.9 %collective-permute-start.44 = (bf16[32,5120]{1,0:T(8,128)(2,1)}, bf16[32,5120]{1,0:T(8,128)(2,1)}, u32[]{:S(2)}, u32[]{:S(2)}) collective-permute-start(bf16[32,5120]{1,0:T(8,128)(2,1)} %get-tuple-element.369), channel_id=1, source_target_pairs={{0,24},{1,25},{2,26},{3,27},{4,28},{5,29},{6,30},{7,31},{8,16},{9,... | collective-permute-start | bytes 983048 | tf_op jit(solution)/shard_map/ppermute | solution.py:924
  565.2 13.8 %all-to-all-start.4 = ((f32[32,1,544]{2,1,0:T(1,128)}), f32[32,1,544]{2,1,0:T(1,128)S(1)}, u32[]{:S(2)}, u32[]{:S(2)}) async-start(f32[32,1,544]{2,1,0:T(1,128)} %copy.84), calls=%async_computation.6 | async-start | bytes 163840 | tf_op jit(solution)/shard_map/all_to_all | solution.py:1296
  571.0 12.6 %collective-permute-start.45 = (bf16[32,3072]{1,0:T(8,128)(2,1)}, bf16[32,3072]{1,0:T(8,128)(2,1)}, u32[]{:S(2)}, u32[]{:S(2)}) collective-permute-start(bf16[32,3072]{1,0:T(8,128)(2,1)} %fusion.44), channel_id=1, source_target_pairs={{0,8},{1,9},{2,10},{3,11},{4,12},{5,13},{6,14},{7,15},{8,0},{9,1},... | collective-permute-start | bytes 589832 | tf_op jit(solution)/shard_map/ppermute | solution.py:924
  572.8 17.4 %collective-permute-start.46 = (bf16[32,3072]{1,0:T(8,128)(2,1)}, bf16[32,3072]{1,0:T(8,128)(2,1)}, u32[]{:S(2)}, u32[]{:S(2)}) collective-permute-start(bf16[32,3072]{1,0:T(8,128)(2,1)} %get-tuple-element.387), channel_id=1, source_target_pairs={{0,16},{1,17},{2,18},{3,19},{4,20},{5,21},{6,22},{7,23},{8,24},{9,... | collective-permute-start | bytes 589832 | tf_op jit(solution)/shard_map/ppermute | solution.py:924
  575.2 15.0 %collective-permute-start.47 = (bf16[32,3072]{1,0:T(8,128)(2,1)}, bf16[32,3072]{1,0:T(8,128)(2,1)}, u32[]{:S(2)}, u32[]{:S(2)}) collective-permute-start(bf16[32,3072]{1,0:T(8,128)(2,1)} %get-tuple-element.388), channel_id=1, source_target_pairs={{0,24},{1,25},{2,26},{3,27},{4,28},{5,29},{6,30},{7,31},{8,16},{9,... | collective-permute-start | bytes 589832 | tf_op jit(solution)/shard_map/ppermute | solution.py:924
  (38 other events, 283.2 us)
Sparse Core Ops, SparseCore 0:
  14.2 176.9 all-gather.1
  469.7 27.2 reduce-scatter.2
  499.4 25.7 reduce-scatter.4

commit v4 on v3

--- a/solution.py
+++ b/solution.py
@@ -1251,6 +1251,8 @@
     at_once(back_b, r_qkv, r_mid)
     r_qkv.launch()
     r_mid.far()
+    at_once(back_b, r_mid)
+    r_mid.launch()
     dv2_sum = jnp.sum(dkv2[:, D:].astype(F32), axis=0)
     early = [
         sums2[2], sums2[0], sums2[1], sums3[2], sums3[0], sums3[1], sums3[3],
@@ -1261,11 +1263,12 @@
     text_grad = mm(dkv2, second[:, 2 * D : 4 * D], NT).astype(BF16)
     now = [text_grad]
     at_once(back_b, r_qkv, r_mid, early, now)
-    r_mid.launch()
     r_qkv.near()
-    at_once(back_b, r_qkv, early, now)
+    r_mid.deep()
+    at_once(back_b, r_qkv, r_mid, early, now)
     (text_grad,) = now
     r_qkv.launch()
+    r_mid.launch()
     leaving, sums1 = kernel_call(
         norm1_kernel, "norm1_back", grid,
         [columns(count * PAIR)] * 6 + [whole((D, 3 * D)), token_tile, row_tile, vec1]
@@ -1276,12 +1279,10 @@
         flops=3 * unit, moved=18 * length * D,
     )
     leaving = [lax.all_to_all(leaving, "seq", 0, 0, tiled=True)]
-    at_once(r_qkv, r_mid)
+    at_once(r_qkv)
     r_qkv.far()
-    r_mid.deep()
-    at_once(r_qkv, r_mid)
+    at_once(r_qkv)
     r_qkv.launch()
-    r_mid.launch()
     late = [across([sums1[0], sums1[1], jnp.concatenate([sums1[2], sums1[3]])])]
     mlp_out_grad = r_out.done().reshape(rows, fours, D).transpose(1, 0, 2).reshape(-1, D)
     mlp_in_grad = r_in.done().reshape(rows, fours, ring.count, rows)

time: 606 us -> 604 us (level)
  transfers between devices with their start and end apart: 56 -> 56, of which waited for: 22 -> 23; matrix products, arithmetic and copies ran while one was open for 12% -> 12% of each run, Pallas kernels for 42% -> 42%
where the time goes in v4:
time: 604 us; the launch traced here: 598 us
  Pallas kernels  268 us (44%)
  waiting for transfers between devices  128 us (21%)
  starting transfers between devices  75.4 us (12%)
  other arithmetic  60.1 us (10%)
  local copies, waits for them, and re-layouts  43 us (7%)
  between operations  14.9 us (2%)
  matrix products  8.11 us (1%)
    pallas_call x16, Pallas kernels, kernel_call(): pl.pallas_call(body, grid_spec=pltpu.PrefetchScalarGridSpec(num_scalar_pr...  268 us
    ppermute x48, waiting for transfers between devices, swap(): return lax.ppermute(array, AXES, [(i, i ^ bits) for i in range(self.count)])  125 us
    ppermute x48, starting transfers between devices, swap(): return lax.ppermute(array, AXES, [(i, i ^ bits) for i in range(self.count)])  51.7 us
    convert_element_type x4, other arithmetic, near(): total_of(self.kept[i, 1], self.got[i, 1]).astype(BF16)  14.8 us
  transfers between devices with their start and end apart: 56, of which 23 were waited for; matrix products, arithmetic and copies ran while one was open for 12% of the time, Pallas kernels for 42%

profile of v4, /device:TPU:0, one launch (start us, length us, event | category | flops | bytes accessed | tf_op | source)
XLA Modules:
  0.0 597.9 jit_solution(2339198430388488538)
XLA Ops:
  14.1 2.6 pad_maximum_fusion
  16.8 5.8 all-to-all-start
  23.1 3.7 collective-permute-start.2
  31.0 4.4 collective-permute-done.2
  35.4 15.7 %collective-permute-done.1 = bf16[32,3200]{1,0:T(8,128)(2,1)S(1)} collective-permute-done((bf16[32,3200]{1,0:T(8,128)(2,1)S(1)}, bf16[32,3200]{1,0:T(8,128)(2,1)S(1)}, u32[]{:S(2)}, u32[]{:S(2)}) %collective-permute-start.1) | collective-permute-done | bytes 204832 | tf_op jit(solution)/shard_map/ppermute | solution.py:924
  51.1 2.9 all-to-all-done.x_ref.refs_7_
  55.6 3.5 collective-permute-start.3
  60.6 15.3 %collective-permute-done.3 = bf16[2,32,3200]{2,1,0:T(8,128)(2,1)S(1)} collective-permute-done((bf16[2,32,3200]{2,1,0:T(8,128)(2,1)S(1)}, bf16[2,32,3200]{2,1,0:T(8,128)(2,1)S(1)}, u32[]{:S(2)}, u32[]{:S(2)}) %collective-permute-start.3) | collective-permute-done | bytes 409632 | tf_op jit(solution)/shard_map/ppermute | solution.py:924
  80.3 3.0 collective-permute-start.8
  84.7 19.0 %collective-permute-done.7 = bf16[32,5120]{1,0:T(8,128)(2,1)S(1)} collective-permute-done((bf16[32,5120]{1,0:T(8,128)(2,1)S(1)}, bf16[32,5120]{1,0:T(8,128)(2,1)S(1)}, u32[]{:S(2)}, u32[]{:S(2)}) %collective-permute-start.7) | collective-permute-done | bytes 327712 | tf_op jit(solution)/shard_map/ppermute | solution.py:924
  103.7 9.3 %collective-permute-done.8 = bf16[32,5120]{1,0:T(8,128)(2,1)S(1)} collective-permute-done((bf16[32,5120]{1,0:T(8,128)(2,1)S(1)}, bf16[32,5120]{1,0:T(8,128)(2,1)S(1)}, u32[]{:S(2)}, u32[]{:S(2)}) %collective-permute-start.8) | collective-permute-done | bytes 327712 | tf_op jit(solution)/shard_map/ppermute | solution.py:924
  122.2 8.2 %put_in_order.2.w_ref.refs_6_ = bf16[1024,3200]{1,0:T(8,128)(2,1)} custom-call(s32[4]{0:T(128)} %get-tuple-element.413.place_ref, bf16[2,2,32,3200]{3,2,1,0:T(8,128)(2,1)} %pad_maximum_fusion.5.refs_0_, bf16[2,2,32,3200]{3,2,1,0:T(8,128)(2,1)} %collective-permute-done.5.refs_1_, bf16[2,2,32,3200]{3,2,1,0:T(8,128)(2,1)} %copy-done.9, ...), custom_call_target="tpu_custom_call" | custom-call | bytes 409600 | tf_op jit(solution)/shard_map/put_in_order/pallas_call | solution.py:446
  132.6 12.5 %qkv.1 = (bf16[1024,1024]{1,0:T(8,128)(2,1)}, bf16[1024,3072]{1,0:T(8,128)(2,1)}) custom-call(bf16[4,288,1024]{2,1,0:T(8,128)(2,1)} %copy-done, bf16[1024,3200]{1,0:T(8,128)(2,1)} %put_in_order.2.w_ref.refs_6_, f32[8,1024]{1,0:T(8,128)} %pad.14.vec_ref), custom_call_target="tpu_custom_call" | custom-call | flops 201326592 | bytes 524288 | tf_op jit(solution)/shard_map/qkv/pallas_call | solution.py:446
  145.1 2.0 collective-permute-done.14
  147.1 3.1 collective-permute-done.15
  157.0 18.5 %attend.1 = (bf16[1024,1024]{1,0:T(8,128)(2,1)}, f32[8,2,1024]{2,1,0:T(2,128)}) custom-call(bf16[1024,3072]{1,0:T(8,128)(2,1)} %get-tuple-element.243.q_ref.k_ref.v_ref, bf16[1024,3072]{1,0:T(8,128)(2,1)} %get-tuple-element.243.q_ref.k_ref.v_ref, bf16[1024,3072]{1,0:T(8,128)(2,1)} %get-tuple-element.243.q_ref.k_ref.v_ref), custom_call_target="tpu_custom_call" | custom-call | flops 268435456 | bytes 262144 | tf_op jit(solution)/shard_map/attend/pallas_call | solution.py:446
  175.4 18.2 %collective-permute-done.16.refs_1_ = bf16[2,2,32,5120]{3,2,1,0:T(8,128)(2,1)} collective-permute-done((bf16[2,2,32,5120]{3,2,1,0:T(8,128)(2,1)S(1)}, bf16[2,2,32,5120]{3,2,1,0:T(8,128)(2,1)}, u32[]{:S(2)}, u32[]{:S(2)}) %collective-permute-start.16) | collective-permute-done | bytes 1310752 | tf_op jit(solution)/shard_map/ppermute | solution.py:924
  197.1 1.9 collective-permute-done.21.refs_7_
  198.9 10.4 %put_in_order.3.ws_ref.wq_ref.wc_ref = bf16[1024,5120]{1,0:T(8,128)(2,1)} custom-call(s32[4]{0:T(128)} %get-tuple-element.413.place_ref, bf16[2,2,32,5120]{3,2,1,0:T(8,128)(2,1)} %copy-done.4, bf16[2,2,32,5120]{3,2,1,0:T(8,128)(2,1)} %collective-permute-done.16.refs_1_, bf16[2,2,32,5120]{3,2,1,0:T(8,128)(2,1)} %copy-done.5, ...), custom_call_target="tpu_custom_call" | custom-call | bytes 655360 | tf_op jit(solution)/shard_map/put_in_order/pallas_call | solution.py:446
  209.3 3.7 fusion.7.kv_ref
  213.0 18.4 %cross.1 = (f32[1024,1024]{1,0:T(8,128)}, bf16[1024,1024]{1,0:T(8,128)(2,1)}, bf16[1024,1024]{1,0:T(8,128)(2,1)}, bf16[1024,1024]{1,0:T(8,128)(2,1)}, f32[1024,1...) custom-call(s32[1]{0:T(128)} %dynamic_slice.3.len_ref, bf16[4,288,1024]{2,1,0:T(8,128)(2,1)} %copy-done, ...), custom_call_target="tpu_custom_call" | custom-call | flops 335544320 | bytes 983040 | tf_op jit(solution)/shard_map/cross/pallas_call | solution.py:446
  231.5 3.8 all-to-all-start.1
  236.5 30.4 %mlp.1 = (bf16[1024,4096]{1,0:T(8,128)(2,1)}, bf16[1024,4096]{1,0:T(8,128)(2,1)}, bf16[1024,1024]{1,0:T(8,128)(2,1)}) custom-call(bf16[1024,1024]{1,0:T(8,128)(2,1)} %get-tuple-element.273.h_ref.refs_0_, bf16[1024,8192]{1,0:T(8,128)(2,1)} %all-gather.2.cloned.1.call-done.wi_ref.wo_ref, bf16[1024,8192]{1,0:T(8,128)(2,1)} %all-gather.2.cloned.1.call-done.wi_ref.wo_ref, ...), custom_call_target="tpu_custom_call" | custom-call | flops 536870912 | bytes 1310720 | tf_op jit(solution)/shard_map/mlp/pallas_call | solution.py:446
  268.3 14.8 %d_mlp_out.1 = (bf16[512,4096]{1,0:T(8,128)(2,1)}, bf16[512,4096]{1,0:T(8,128)(2,1)}) custom-call(s32[4]{0:T(128)} %get-tuple-element.412.place_ref, bf16[1024,4096]{1,0:T(8,128)(2,1)} %get-tuple-element.261.refs_0_, bf16[1024,1024]{1,0:T(8,128)(2,1)} %bitcast.196), custom_call_target="tpu_custom_call" | custom-call | flops 268435456 | bytes 327680 | tf_op jit(solution)/shard_map/d_mlp_out/pallas_call | solution.py:446
  283.2 4.0 all-to-all-start.2
  287.5 15.4 %du.1 = (bf16[1024,4096]{1,0:T(8,128)(2,1)}, f32[4,1,1024]{2,1,0:T(1,128)}) custom-call(bf16[1024,1024]{1,0:T(8,128)(2,1)} %bitcast.197, bf16[1024,8192]{1,0:T(8,128)(2,1)} %all-gather.2.cloned.1.call-done.wi_ref.wo_ref, bf16[1024,4096]{1,0:T(8,128)(2,1)} %get-tuple-element.264.slope_ref), custom_call_target="tpu_custom_call" | custom-call | flops 268435456 | bytes 851968 | tf_op jit(solution)/shard_map/du/pallas_call | solution.py:446
  302.9 3.8 fusion.20
  306.7 14.6 %d_mlp_in.1 = (bf16[512,4096]{1,0:T(8,128)(2,1)}, bf16[512,4096]{1,0:T(8,128)(2,1)}) custom-call(s32[4]{0:T(128)} %get-tuple-element.412.place_ref, bf16[1024,1024]{1,0:T(8,128)(2,1)} %get-tuple-element.273.h_ref.refs_0_, bf16[1024,4096]{1,0:T(8,128)(2,1)} %get-tuple-element.279.refs_1_.du_ref), custom_call_target="tpu_custom_call" | custom-call | flops 268435456 | bytes 327680 | tf_op jit(solution)/shard_map/d_mlp_in/pallas_call | solution.py:446
  321.7 1.9 collective-permute-start.24
  325.0 21.2 %norm3_back.1 = (f32[1024,1024]{1,0:T(8,128)}, bf16[1024,1024]{1,0:T(8,128)(2,1)}, bf16[1024,1024]{1,0:T(8,128)(2,1)}, f32[8,1024]{1,0:T(8,128)}) custom-call(bf16[1024,4096]{1,0:T(8,128)(2,1)} %get-tuple-element.279.refs_1_.du_ref, bf16[1024,8192]{1,0:T(8,128)(2,1)} %all-gather.2.cloned.1.call-done.wi_ref.wo_ref, bf16[1024,1024]{1,0:T(8,128)(2,1)} %bitcast.198, ...), custom_call_target="tpu_custom_call" | custom-call | flops 335544320 | bytes 1048576 | tf_op jit(solution)/shard_map/norm3_back/pallas_call | solution.py:446
  349.1 2.0 copy-done.7
  351.1 3.3 fusion.29
  354.3 3.7 fusion.22
  362.1 21.5 %cross_back.1 = (bf16[1024,1024]{1,0:T(8,128)(2,1)}, bf16[128,2048]{1,0:T(8,128)(2,1)}, f32[1024,1024]{1,0:T(8,128)}, bf16[1024,1024]{1,0:T(8,128)(2,1)}, bf16[1024,1024]{1,0:T(8,128)(2,1)}, /*index=5*/f32[8,1024]{1,0:T(8,128)}) custom-call(s32[1]{0:T(128)} %dynamic_slice.3.len_ref, bf16[1024,1024]{1,0:T(8,128)(2,1)} %get-tuple-element.277.q_ref, ...), custom_call_target="tpu_custom_call" | custom-call | flops 335544320 | bytes 1114112 | tf_op jit(solution)/shard_map/cross_back/pallas_call | solution.py:446
  383.7 17.2 %d_mid.1 = (bf16[512,5120]{1,0:T(8,128)(2,1)}, bf16[512,5120]{1,0:T(8,128)(2,1)}) custom-call(s32[4]{0:T(128)} %get-tuple-element.413.place_ref, bf16[1024,1024]{1,0:T(8,128)(2,1)} %get-tuple-element.250.o_ref.refs_0_, bf16[1024,1024]{1,0:T(8,128)(2,1)} %get-tuple-element.300.refs_1_, bf16[1024,1024]{1,0:T(8,128)(2,1)} %get-tuple-element.278.o_ref.refs_2_, ...), custom_call_target="tpu_custom_call" | custom-call | flops 335544320 | bytes 393216 | tf_op jit(solution)/shard_map/d_mid/pallas_call | solution.py:446
  400.9 2.5 add_convert_fusion.11
  404.5 2.7 fusion.27
  409.3 18.2 %attend_back.2 = (bf16[1024,512]{1,0:T(8,128)(2,1)}, bf16[1024,512]{1,0:T(8,128)(2,1)}, bf16[1024,512]{1,0:T(8,128)(2,1)}) custom-call(bf16[1024,3072]{1,0:T(8,128)(2,1)} %get-tuple-element.243.q_ref.k_ref.v_ref, bf16[1024,3072]{1,0:T(8,128)(2,1)} %get-tuple-element.243.q_ref.k_ref.v_ref, bf16[1024,3072]{1,0:T(8,128)(2,1)} %get-tuple-element.243.q_ref.k_ref.v_ref, ...), custom_call_target="tpu_custom_call" | custom-call | flops 335544320 | bytes 262144 | tf_op jit(solution)/shard_map/attend_back/pallas_call | solution.py:446
  427.5 2.3 add_convert_fusion.9
  430.9 4.1 fusion.11
  437.1 17.9 %attend_back.3 = (bf16[1024,512]{1,0:T(8,128)(2,1)}, bf16[1024,512]{1,0:T(8,128)(2,1)}, bf16[1024,512]{1,0:T(8,128)(2,1)}) custom-call(bf16[1024,3072]{1,0:T(8,128)(2,1)} %get-tuple-element.243.q_ref.k_ref.v_ref, bf16[1024,3072]{1,0:T(8,128)(2,1)} %get-tuple-element.243.q_ref.k_ref.v_ref, bf16[1024,3072]{1,0:T(8,128)(2,1)} %get-tuple-element.243.q_ref.k_ref.v_ref, ...), custom_call_target="tpu_custom_call" | custom-call | flops 335544320 | bytes 262144 | tf_op jit(solution)/shard_map/attend_back/pallas_call | solution.py:446
  454.9 14.1 %d_qkv.1 = (bf16[512,3072]{1,0:T(8,128)(2,1)}, bf16[512,3072]{1,0:T(8,128)(2,1)}) custom-call(s32[4]{0:T(128)} %get-tuple-element.413.place_ref, bf16[1024,1024]{1,0:T(8,128)(2,1)} %get-tuple-element.276.refs_0_, bf16[1024,512]{1,0:T(8,128)(2,1)} %get-tuple-element.333.refs_1_.refs_0_, bf16[1024,512]{1,0:T(8,128)(2,1)} %get-tuple-element.334.refs_2_.refs_1_, ...), custom_call_target="tpu_custom_call" | custom-call | flops 201326592 | bytes 262144 | tf_op jit(solution)/shard_map/d_qkv/pallas_call | solution.py:446
  469.9 5.0 fusion.12
  477.5 4.4 fusion.16.refs_10_
  481.9 10.4 %collective-permute-done.36 = bf16[2,32,5120]{2,1,0:T(8,128)(2,1)} collective-permute-done((bf16[2,32,5120]{2,1,0:T(8,128)(2,1)}, bf16[2,32,5120]{2,1,0:T(8,128)(2,1)}, u32[]{:S(2)}, u32[]{:S(2)}) %collective-permute-start.36) | collective-permute-done | bytes 655392 | tf_op jit(solution)/shard_map/ppermute | solution.py:924
  493.5 2.3 fusion.43
  495.8 1.9 fusion.41
  497.7 3.1 fusion.32
  501.7 14.8 %norm1_back.1 = (bf16[4,288,1024]{2,1,0:T(8,128)(2,1)}, f32[8,1024]{1,0:T(8,128)}) custom-call(bf16[1024,512]{1,0:T(8,128)(2,1)} %get-tuple-element.333.refs_1_.refs_0_, bf16[1024,512]{1,0:T(8,128)(2,1)} %get-tuple-element.334.refs_2_.refs_1_, bf16[1024,512]{1,0:T(8,128)(2,1)} %get-tuple-element.335.refs_3_.refs_2_, ...), custom_call_target="tpu_custom_call" | custom-call | flops 201326592 | bytes 589824 | tf_op jit(solution)/shard_map/norm1_back/pallas_call | solution.py:446
  516.5 3.9 all-to-all-start.3
  521.3 3.9 fusion.33
  525.2 2.0 collective-permute-start.40
  530.5 2.1 collective-permute-start.43
  535.5 3.0 reshape.410
  538.5 4.7 copy.83
  543.2 4.4 reshape.402
  548.0 8.4 %collective-permute-done.43 = bf16[32,5120]{1,0:T(8,128)(2,1)} collective-permute-done((bf16[32,5120]{1,0:T(8,128)(2,1)}, bf16[32,5120]{1,0:T(8,128)(2,1)}, u32[]{:S(2)}, u32[]{:S(2)}) %collective-permute-start.43) | collective-permute-done | bytes 327712 | tf_op jit(solution)/shard_map/ppermute | solution.py:924
  557.3 2.5 slice.670
  559.8 1.9 fusion.46
  563.4 5.8 all-to-all-start.4
  569.2 1.8 collective-permute-start.45
  571.1 2.4 collective-permute-start.46
  579.1 2.5 collective-permute-done.45
  581.6 6.7 %collective-permute-done.46 = bf16[32,3072]{1,0:T(8,128)(2,1)S(1)} collective-permute-done((bf16[32,3072]{1,0:T(8,128)(2,1)}, bf16[32,3072]{1,0:T(8,128)(2,1)S(1)}, u32[]{:S(2)}, u32[]{:S(2)}) %collective-permute-start.46) | collective-permute-done | bytes 196640 | tf_op jit(solution)/shard_map/ppermute | solution.py:924
  (274 shorter events, 83.4 us)
Async XLA Ops:
  7.2 229.3 %all-gather.2.cloned.1.call-start = ((), (), s32[]{:S(2)}) async-start(), calls=%async_computation.7 | async-start | bytes 17301504 | tf_op jit(solution)/shard_map/all_gather | solution.py:1021
  16.8 37.2 %all-to-all-start = ((bf16[4,288,1024]{2,1,0:T(8,128)(2,1)}), bf16[4,288,1024]{2,1,0:T(8,128)(2,1)S(1)}, u32[]{:S(2)}, u32[]{:S(2)}) async-start(bf16[4,288,1024]{2,1,0:T(8,128)(2,1)} %pad_maximum_fusion), calls=%async_computation | async-start | bytes 4718592 | tf_op jit(solution)/shard_map/all_to_all | solution.py:1045
  23.1 12.3 %collective-permute-start.2 = (bf16[32,3200]{1,0:T(8,128)(2,1)S(1)}, bf16[32,3200]{1,0:T(8,128)(2,1)S(1)}, u32[]{:S(2)}, u32[]{:S(2)}) collective-permute-start(bf16[32,3200]{1,0:T(8,128)(2,1)S(1)} %get-tuple-element.467), channel_id=1, source_target_pairs={{0,24},{1,25},{2,26},{3,27},{4,28},{5,29},{6,30},{7,31},{8,16},{9,... | collective-permute-start | bytes 614408 | tf_op jit(solution)/shard_map/ppermute | solution.py:924
  26.7 24.4 %collective-permute-start.1 = (bf16[32,3200]{1,0:T(8,128)(2,1)S(1)}, bf16[32,3200]{1,0:T(8,128)(2,1)S(1)}, u32[]{:S(2)}, u32[]{:S(2)}) collective-permute-start(bf16[32,3200]{1,0:T(8,128)(2,1)S(1)} %get-tuple-element.467), channel_id=1, source_target_pairs={{0,16},{1,17},{2,18},{3,19},{4,20},{5,21},{6,22},{7,23},{8,24},{9,... | collective-permute-start | bytes 614408 | tf_op jit(solution)/shard_map/ppermute | solution.py:924
  26.7 24.4 %collective-permute-start = (bf16[32,3200]{1,0:T(8,128)(2,1)S(1)}, bf16[32,3200]{1,0:T(8,128)(2,1)S(1)}, u32[]{:S(2)}, u32[]{:S(2)}) collective-permute-start(bf16[32,3200]{1,0:T(8,128)(2,1)S(1)} %get-tuple-element.467), channel_id=1, source_target_pairs={{0,8},{1,9},{2,10},{3,11},{4,12},{5,13},{6,14},{7,15},{8,0},{9,1},... | collective-permute-start | bytes 614408 | tf_op jit(solution)/shard_map/ppermute | solution.py:924
  54.0 25.5 %copy-start = (bf16[4,288,1024]{2,1,0:T(8,128)(2,1)}, bf16[4,288,1024]{2,1,0:T(8,128)(2,1)S(1)}, u32[]{:S(2)}) copy-start(bf16[4,288,1024]{2,1,0:T(8,128)(2,1)S(1)} %all-to-all-done.x_ref.refs_7_) | copy-start | bytes 7077892
  55.6 20.3 %collective-permute-start.3 = (bf16[2,32,3200]{2,1,0:T(8,128)(2,1)S(1)}, bf16[2,32,3200]{2,1,0:T(8,128)(2,1)S(1)}, u32[]{:S(2)}, u32[]{:S(2)}) collective-permute-start(bf16[2,32,3200]{2,1,0:T(8,128)(2,1)S(1)} %get-tuple-element.215), channel_id=1, source_target_pairs={{0,1},{1,0},{2,3},{3,2},{4,5},{5,4},{6,7},{7,6},{8,9},{9,8},{10,11... | collective-permute-start | bytes 1228808 | tf_op jit(solution)/shard_map/ppermute | solution.py:924
  59.1 17.7 %collective-permute-start.4 = (bf16[2,32,3200]{2,1,0:T(8,128)(2,1)S(1)}, bf16[2,32,3200]{2,1,0:T(8,128)(2,1)S(1)}, u32[]{:S(2)}, u32[]{:S(2)}) collective-permute-start(bf16[2,32,3200]{2,1,0:T(8,128)(2,1)S(1)} %get-tuple-element.216), channel_id=1, source_target_pairs={{0,2},{1,3},{2,0},{3,1},{4,6},{5,7},{6,4},{7,5},{8,10},{9,11},{10,... | collective-permute-start | bytes 1228808 | tf_op jit(solution)/shard_map/ppermute | solution.py:924
  76.9 38.9 %copy-start.9 = (bf16[2,2,32,3200]{3,2,1,0:T(8,128)(2,1)}, bf16[2,2,32,3200]{3,2,1,0:T(8,128)(2,1)S(1)}, u32[]{:S(2)}) copy-start(bf16[2,2,32,3200]{3,2,1,0:T(8,128)(2,1)S(1)} %pad_maximum_fusion.6.refs_2_) | copy-start | bytes 2457604
  76.9 36.2 %collective-permute-start.6 = (bf16[2,2,32,3200]{3,2,1,0:T(8,128)(2,1)S(1)}, bf16[2,2,32,3200]{3,2,1,0:T(8,128)(2,1)}, u32[]{:S(2)}, u32[]{:S(2)}) collective-permute-start(bf16[2,2,32,3200]{3,2,1,0:T(8,128)(2,1)S(1)} %pad_maximum_fusion.6.refs_2_), channel_id=1, source_target_pairs={{0,1},{1,0},{2,3},{3,2},{4,5},{5,4},{6,7},{7,6},{8,9},{9,8},{10,11... | collective-permute-start | bytes 2457608 | tf_op jit(solution)/shard_map/ppermute | solution.py:924
  79.5 36.8 %copy-start.41 = (s32[4]{0:T(128)S(1)}, s32[4]{0:T(128)}, u32[]{:S(2)}) copy-start(s32[4]{0:T(128)} %constant.48.clone) | copy-start | bytes 52
  79.5 33.6 %collective-permute-start.5 = (bf16[2,2,32,3200]{3,2,1,0:T(8,128)(2,1)}, bf16[2,2,32,3200]{3,2,1,0:T(8,128)(2,1)}, u32[]{:S(2)}, u32[]{:S(2)}) collective-permute-start(bf16[2,2,32,3200]{3,2,1,0:T(8,128)(2,1)} %pad_maximum_fusion.5.refs_0_), channel_id=1, source_target_pairs={{0,2},{1,3},{2,0},{3,1},{4,6},{5,7},{6,4},{7,5},{8,10},{9,11},{10,... | collective-permute-start | bytes 2457608 | tf_op jit(solution)/shard_map/ppermute | solution.py:924
  80.3 23.4 %collective-permute-start.7 = (bf16[32,5120]{1,0:T(8,128)(2,1)S(1)}, bf16[32,5120]{1,0:T(8,128)(2,1)S(1)}, u32[]{:S(2)}, u32[]{:S(2)}) collective-permute-start(bf16[32,5120]{1,0:T(8,128)(2,1)S(1)} %constant_dynamic-update-slice_fusion), channel_id=1, source_target_pairs={{0,8},{1,9},{2,10},{3,11},{4,12},{5,13},{6,14},{7,15},{8,0},{9,1},... | collective-permute-start | bytes 983048 | tf_op jit(solution)/shard_map/ppermute | solution.py:924
  80.3 32.7 %collective-permute-start.8 = (bf16[32,5120]{1,0:T(8,128)(2,1)S(1)}, bf16[32,5120]{1,0:T(8,128)(2,1)S(1)}, u32[]{:S(2)}, u32[]{:S(2)}) collective-permute-start(bf16[32,5120]{1,0:T(8,128)(2,1)S(1)} %constant_dynamic-update-slice_fusion), channel_id=1, source_target_pairs={{0,16},{1,17},{2,18},{3,19},{4,20},{5,21},{6,22},{7,23},{8,24},{9,... | collective-permute-start | bytes 983048 | tf_op jit(solution)/shard_map/ppermute | solution.py:924
  83.4 29.7 %collective-permute-start.9 = (bf16[32,5120]{1,0:T(8,128)(2,1)S(1)}, bf16[32,5120]{1,0:T(8,128)(2,1)S(1)}, u32[]{:S(2)}, u32[]{:S(2)}) collective-permute-start(bf16[32,5120]{1,0:T(8,128)(2,1)S(1)} %constant_dynamic-update-slice_fusion), channel_id=1, source_target_pairs={{0,24},{1,25},{2,26},{3,27},{4,28},{5,29},{6,30},{7,31},{8,16},{9,... | collective-permute-start | bytes 983048 | tf_op jit(solution)/shard_map/ppermute | solution.py:924
  115.2 3.7 collective-permute-start.10
  115.2 5.1 collective-permute-start.11
  115.8 5.4 collective-permute-start.12
  115.8 6.5 %collective-permute-start.13 = (bf16[2,2,32,3200]{3,2,1,0:T(8,128)(2,1)}, bf16[2,2,32,3200]{3,2,1,0:T(8,128)(2,1)}, u32[]{:S(2)}, u32[]{:S(2)}) collective-permute-start(bf16[2,2,32,3200]{3,2,1,0:T(8,128)(2,1)} %collective-permute-done.6.refs_3_), channel_id=1, source_target_pairs={{0,4},{1,5},{2,6},{3,7},{4,0},{5,1},{6,2},{7,3},{8,12},{9,13},{10,... | collective-permute-start | bytes 2457608 | tf_op jit(solution)/shard_map/ppermute | solution.py:924
  116.9 30.2 %collective-permute-start.14 = (bf16[2,32,5120]{2,1,0:T(8,128)(2,1)}, bf16[2,32,5120]{2,1,0:T(8,128)(2,1)}, u32[]{:S(2)}, u32[]{:S(2)}) collective-permute-start(bf16[2,32,5120]{2,1,0:T(8,128)(2,1)} %get-tuple-element.237), channel_id=1, source_target_pairs={{0,1},{1,0},{2,3},{3,2},{4,5},{5,4},{6,7},{7,6},{8,9},{9,8},{10,11... | collective-permute-start | bytes 1966088 | tf_op jit(solution)/shard_map/ppermute | solution.py:924
  118.9 31.3 %collective-permute-start.15 = (bf16[2,32,5120]{2,1,0:T(8,128)(2,1)}, bf16[2,32,5120]{2,1,0:T(8,128)(2,1)}, u32[]{:S(2)}, u32[]{:S(2)}) collective-permute-start(bf16[2,32,5120]{2,1,0:T(8,128)(2,1)} %get-tuple-element.238), channel_id=1, source_target_pairs={{0,2},{1,3},{2,0},{3,1},{4,6},{5,7},{6,4},{7,5},{8,10},{9,11},{10,... | collective-permute-start | bytes 1966088 | tf_op jit(solution)/shard_map/ppermute | solution.py:924
  151.5 24.0 %copy-start.4 = (bf16[2,2,32,5120]{3,2,1,0:T(8,128)(2,1)}, bf16[2,2,32,5120]{3,2,1,0:T(8,128)(2,1)S(1)}, u32[]{:S(2)}) copy-start(bf16[2,2,32,5120]{3,2,1,0:T(8,128)(2,1)S(1)} %pad_maximum_fusion.1.refs_0_) | copy-start | bytes 3932164
  153.2 22.3 %copy-start.5 = (bf16[2,2,32,5120]{3,2,1,0:T(8,128)(2,1)}, bf16[2,2,32,5120]{3,2,1,0:T(8,128)(2,1)S(1)}, u32[]{:S(2)}) copy-start(bf16[2,2,32,5120]{3,2,1,0:T(8,128)(2,1)S(1)} %pad_maximum_fusion.2.refs_2_) | copy-start | bytes 3932164
  153.2 41.0 %copy-start.42 = (s32[4]{0:T(128)S(1)}, s32[4]{0:T(128)}, u32[]{:S(2)}) copy-start(s32[4]{0:T(128)} %param.26) | copy-start | bytes 52
  153.2 40.5 %collective-permute-start.16 = (bf16[2,2,32,5120]{3,2,1,0:T(8,128)(2,1)S(1)}, bf16[2,2,32,5120]{3,2,1,0:T(8,128)(2,1)}, u32[]{:S(2)}, u32[]{:S(2)}) collective-permute-start(bf16[2,2,32,5120]{3,2,1,0:T(8,128)(2,1)S(1)} %pad_maximum_fusion.1.refs_0_), channel_id=1, source_target_pairs={{0,2},{1,3},{2,0},{3,1},{4,6},{5,7},{6,4},{7,5},{8,10},{9,11},{10,... | collective-permute-start | bytes 3932168 | tf_op jit(solution)/shard_map/ppermute | solution.py:924
  155.0 38.7 %collective-permute-start.17 = (bf16[2,2,32,5120]{3,2,1,0:T(8,128)(2,1)S(1)}, bf16[2,2,32,5120]{3,2,1,0:T(8,128)(2,1)}, u32[]{:S(2)}, u32[]{:S(2)}) collective-permute-start(bf16[2,2,32,5120]{3,2,1,0:T(8,128)(2,1)S(1)} %pad_maximum_fusion.2.refs_2_), channel_id=1, source_target_pairs={{0,1},{1,0},{2,3},{3,2},{4,5},{5,4},{6,7},{7,6},{8,9},{9,8},{10,11... | collective-permute-start | bytes 3932168 | tf_op jit(solution)/shard_map/ppermute | solution.py:924
  156.5 40.3 %collective-permute-start.20 = (bf16[2,2,32,5120]{3,2,1,0:T(8,128)(2,1)S(1)}, bf16[2,2,32,5120]{3,2,1,0:T(8,128)(2,1)}, u32[]{:S(2)}, u32[]{:S(2)}) collective-permute-start(bf16[2,2,32,5120]{3,2,1,0:T(8,128)(2,1)S(1)} %pad_maximum_fusion.2.refs_2_), channel_id=1, source_target_pairs={{0,4},{1,5},{2,6},{3,7},{4,0},{5,1},{6,2},{7,3},{8,12},{9,13},{10,... | collective-permute-start | bytes 3932168 | tf_op jit(solution)/shard_map/ppermute | solution.py:924
  156.5 40.3 %collective-permute-start.18 = (bf16[2,2,32,5120]{3,2,1,0:T(8,128)(2,1)S(1)}, bf16[2,2,32,5120]{3,2,1,0:T(8,128)(2,1)}, u32[]{:S(2)}, u32[]{:S(2)}) collective-permute-start(bf16[2,2,32,5120]{3,2,1,0:T(8,128)(2,1)S(1)} %pad_maximum_fusion.1.refs_0_), channel_id=1, source_target_pairs={{0,4},{1,5},{2,6},{3,7},{4,0},{5,1},{6,2},{7,3},{8,12},{9,13},{10,... | collective-permute-start | bytes 3932168 | tf_op jit(solution)/shard_map/ppermute | solution.py:924
  193.7 3.4 collective-permute-start.19
  193.7 5.2 collective-permute-start.21
  231.5 35.5 %all-to-all-start.1 = ((bf16[4,256,1024]{2,1,0:T(8,128)(2,1)}), bf16[4,256,1024]{2,1,0:T(8,128)(2,1)S(1)}, u32[]{:S(2)}, u32[]{:S(2)}) async-start(bf16[4,256,1024]{2,1,0:T(8,128)(2,1)} %param.27), calls=%async_computation.1 | async-start | bytes 4194304 | tf_op jit(solution)/shard_map/all_to_all | solution.py:1136
  283.1 19.8 %collective-permute-start.22 = (bf16[2,2,2,2,32,4096]{5,4,3,2,1,0:T(8,128)(2,1)}, bf16[2,2,2,2,32,4096]{5,4,3,2,1,0:T(8,128)(2,1)}, u32[]{:S(2)}, u32[]{:S(2)}) collective-permute-start(bf16[2,2,2,2,32,4096]{5,4,3,2,1,0:T(8,128)(2,1)} %bitcast.237), channel_id=1, source_target_pairs={{0,4},{1,5},{2,6},{3,7},{4,0},{5,1},{6,2},{7,3},{8,12},{9,13},{10,... | collective-permute-start | bytes 12582920 | tf_op jit(solution)/shard_map/ppermute | solution.py:924
  283.2 38.2 %all-to-all-start.2 = ((bf16[4,256,1024]{2,1,0:T(8,128)(2,1)}), bf16[4,256,1024]{2,1,0:T(8,128)(2,1)S(1)}, u32[]{:S(2)}, u32[]{:S(2)}) async-start(bf16[4,256,1024]{2,1,0:T(8,128)(2,1)} %bitcast.215), calls=%async_computation.2 | async-start | bytes 4194304 | tf_op jit(solution)/shard_map/all_to_all | solution.py:1160
  287.3 245.8 %reduce-scatter.3.cloned.1.call-start = ((), (), s32[]{:S(2)}) async-start(), calls=%async_computation.8 | async-start | bytes 1310720 | tf_op jit(solution)/shard_map/reduce_scatter | solution.py:987
  321.4 24.8 %copy-start.2 = (bf16[4,256,1024]{2,1,0:T(8,128)(2,1)}, bf16[4,256,1024]{2,1,0:T(8,128)(2,1)S(1)}, u32[]{:S(2)}) copy-start(bf16[4,256,1024]{2,1,0:T(8,128)(2,1)S(1)} %all-to-all-done.2) | copy-start | bytes 6291460
  321.4 27.7 %collective-permute-start.23 = (bf16[2,2,2,2,32,4096]{5,4,3,2,1,0:T(8,128)(2,1)}, bf16[2,2,2,2,32,4096]{5,4,3,2,1,0:T(8,128)(2,1)S(1)}, u32[]{:S(2)}, u32[]{:S(2)}) collective-permute-start(bf16[2,2,2,2,32,4096]{5,4,3,2,1,0:T(8,128)(2,1)} %bitcast.236), channel_id=1, source_target_pairs={{0,4},{1,5},{2,6},{3,7},{4,0},{5,1},{6,2},{7,3},{8,12},{9,13},{10,... | collective-permute-start | bytes 12582920 | tf_op jit(solution)/shard_map/ppermute | solution.py:924
  321.7 25.8 %collective-permute-start.24 = (bf16[2,2,32,4096]{3,2,1,0:T(8,128)(2,1)}, bf16[2,2,32,4096]{3,2,1,0:T(8,128)(2,1)S(1)}, u32[]{:S(2)}, u32[]{:S(2)}) collective-permute-start(bf16[2,2,32,4096]{3,2,1,0:T(8,128)(2,1)} %get-tuple-element.284), channel_id=1, source_target_pairs={{0,2},{1,3},{2,0},{3,1},{4,6},{5,7},{6,4},{7,5},{8,10},{9,11},{10,... | collective-permute-start | bytes 3145736 | tf_op jit(solution)/shard_map/ppermute | solution.py:924
  323.5 25.5 %collective-permute-start.25 = (bf16[2,2,32,4096]{3,2,1,0:T(8,128)(2,1)}, bf16[2,2,32,4096]{3,2,1,0:T(8,128)(2,1)}, u32[]{:S(2)}, u32[]{:S(2)}) collective-permute-start(bf16[2,2,32,4096]{3,2,1,0:T(8,128)(2,1)} %get-tuple-element.285), channel_id=1, source_target_pairs={{0,1},{1,0},{2,3},{3,2},{4,5},{5,4},{6,7},{7,6},{8,9},{9,8},{10,11... | collective-permute-start | bytes 3145736 | tf_op jit(solution)/shard_map/ppermute | solution.py:924
  358.0 42.8 %collective-permute-start.26 = (bf16[2,2,32,4096]{3,2,1,0:T(8,128)(2,1)}, bf16[2,2,32,4096]{3,2,1,0:T(8,128)(2,1)S(1)}, u32[]{:S(2)}, u32[]{:S(2)}) collective-permute-start(bf16[2,2,32,4096]{3,2,1,0:T(8,128)(2,1)} %get-tuple-element.305), channel_id=1, source_target_pairs={{0,2},{1,3},{2,0},{3,1},{4,6},{5,7},{6,4},{7,5},{8,10},{9,11},{10,... | collective-permute-start | bytes 3145736 | tf_op jit(solution)/shard_map/ppermute | solution.py:924
  358.4 42.5 %collective-permute-start.27 = (bf16[2,2,32,4096]{3,2,1,0:T(8,128)(2,1)}, bf16[2,2,32,4096]{3,2,1,0:T(8,128)(2,1)S(1)}, u32[]{:S(2)}, u32[]{:S(2)}) collective-permute-start(bf16[2,2,32,4096]{3,2,1,0:T(8,128)(2,1)} %get-tuple-element.306), channel_id=1, source_target_pairs={{0,1},{1,0},{2,3},{3,2},{4,5},{5,4},{6,7},{7,6},{8,9},{9,8},{10,11... | collective-permute-start | bytes 3145736 | tf_op jit(solution)/shard_map/ppermute | solution.py:924
  360.1 40.8 %collective-permute-start.28 = (bf16[2,32,4096]{2,1,0:T(8,128)(2,1)}, bf16[2,32,4096]{2,1,0:T(8,128)(2,1)S(1)}, u32[]{:S(2)}, u32[]{:S(2)}) collective-permute-start(bf16[2,32,4096]{2,1,0:T(8,128)(2,1)} %get-tuple-element.307), channel_id=1, source_target_pairs={{0,1},{1,0},{2,3},{3,2},{4,5},{5,4},{6,7},{7,6},{8,9},{9,8},{10,11... | collective-permute-start | bytes 1572872 | tf_op jit(solution)/shard_map/ppermute | solution.py:924
  360.4 40.4 %collective-permute-start.29 = (bf16[2,32,4096]{2,1,0:T(8,128)(2,1)}, bf16[2,32,4096]{2,1,0:T(8,128)(2,1)}, u32[]{:S(2)}, u32[]{:S(2)}) collective-permute-start(bf16[2,32,4096]{2,1,0:T(8,128)(2,1)} %get-tuple-element.308), channel_id=1, source_target_pairs={{0,2},{1,3},{2,0},{3,1},{4,6},{5,7},{6,4},{7,5},{8,10},{9,11},{10,... | collective-permute-start | bytes 1572872 | tf_op jit(solution)/shard_map/ppermute | solution.py:924
  404.5 26.3 %slice-start = ((s8[5242880]{0:T(1024)(128)(4,1)}), s8[1048576]{0:T(1024)(128)(4,1)S(1)}, s32[]{:S(2)}) async-start(s8[5242880]{0:T(1024)(128)(4,1)} %bitcast.201), calls=%async_computation.10 | async-start | bytes 2097152
  407.3 20.2 %collective-permute-start.30 = (bf16[2,2,2,2,32,5120]{5,4,3,2,1,0:T(8,128)(2,1)}, bf16[2,2,2,2,32,5120]{5,4,3,2,1,0:T(8,128)(2,1)}, u32[]{:S(2)}, u32[]{:S(2)}) collective-permute-start(bf16[2,2,2,2,32,5120]{5,4,3,2,1,0:T(8,128)(2,1)} %bitcast.235), channel_id=1, source_target_pairs={{0,4},{1,5},{2,6},{3,7},{4,0},{5,1},{6,2},{7,3},{8,12},{9,13},{10,... | collective-permute-start | bytes 15728648 | tf_op jit(solution)/shard_map/ppermute | solution.py:924
  407.3 20.2 %collective-permute-start.31 = (bf16[2,32,4096]{2,1,0:T(8,128)(2,1)}, bf16[2,32,4096]{2,1,0:T(8,128)(2,1)S(1)}, u32[]{:S(2)}, u32[]{:S(2)}) collective-permute-start(bf16[2,32,4096]{2,1,0:T(8,128)(2,1)} %get-tuple-element.323), channel_id=1, source_target_pairs={{0,1},{1,0},{2,3},{3,2},{4,5},{5,4},{6,7},{7,6},{8,9},{9,8},{10,11... | collective-permute-start | bytes 1572872 | tf_op jit(solution)/shard_map/ppermute | solution.py:924
  408.7 18.7 %collective-permute-start.32 = (bf16[2,32,4096]{2,1,0:T(8,128)(2,1)}, bf16[2,32,4096]{2,1,0:T(8,128)(2,1)}, u32[]{:S(2)}, u32[]{:S(2)}) collective-permute-start(bf16[2,32,4096]{2,1,0:T(8,128)(2,1)} %get-tuple-element.324), channel_id=1, source_target_pairs={{0,2},{1,3},{2,0},{3,1},{4,6},{5,7},{6,4},{7,5},{8,10},{9,11},{10,... | collective-permute-start | bytes 1572872 | tf_op jit(solution)/shard_map/ppermute | solution.py:924
  435.0 34.0 %collective-permute-start.33 = (bf16[2,2,32,5120]{3,2,1,0:T(8,128)(2,1)}, bf16[2,2,32,5120]{3,2,1,0:T(8,128)(2,1)S(1)}, u32[]{:S(2)}, u32[]{:S(2)}) collective-permute-start(bf16[2,2,32,5120]{3,2,1,0:T(8,128)(2,1)} %get-tuple-element.342), channel_id=1, source_target_pairs={{0,2},{1,3},{2,0},{3,1},{4,6},{5,7},{6,4},{7,5},{8,10},{9,11},{10,... | collective-permute-start | bytes 3932168 | tf_op jit(solution)/shard_map/ppermute | solution.py:924
  436.5 32.5 %collective-permute-start.34 = (bf16[2,2,32,5120]{3,2,1,0:T(8,128)(2,1)}, bf16[2,2,32,5120]{3,2,1,0:T(8,128)(2,1)S(1)}, u32[]{:S(2)}, u32[]{:S(2)}) collective-permute-start(bf16[2,2,32,5120]{3,2,1,0:T(8,128)(2,1)} %get-tuple-element.343), channel_id=1, source_target_pairs={{0,1},{1,0},{2,3},{3,2},{4,5},{5,4},{6,7},{7,6},{8,9},{9,8},{10,11... | collective-permute-start | bytes 3932168 | tf_op jit(solution)/shard_map/ppermute | solution.py:924
  469.1 24.5 %collective-permute-start.35 = (bf16[2,2,2,2,32,3072]{5,4,3,2,1,0:T(8,128)(2,1)}, bf16[2,2,2,2,32,3072]{5,4,3,2,1,0:T(8,128)(2,1)}, u32[]{:S(2)}, u32[]{:S(2)}) collective-permute-start(bf16[2,2,2,2,32,3072]{5,4,3,2,1,0:T(8,128)(2,1)} %bitcast.238), channel_id=1, source_target_pairs={{0,4},{1,5},{2,6},{3,7},{4,0},{5,1},{6,2},{7,3},{8,12},{9,13},{10,... | collective-permute-start | bytes 9437192 | tf_op jit(solution)/shard_map/ppermute | solution.py:924
  469.5 66.1 %reduce-scatter.5.cloned.1.call-start = ((), (), s32[]{:S(2)}) async-start(), calls=%async_computation.9 | async-start | bytes 1310720 | tf_op jit(solution)/shard_map/reduce_scatter | solution.py:987
  474.9 17.4 %collective-permute-start.36 = (bf16[2,32,5120]{2,1,0:T(8,128)(2,1)}, bf16[2,32,5120]{2,1,0:T(8,128)(2,1)}, u32[]{:S(2)}, u32[]{:S(2)}) collective-permute-start(bf16[2,32,5120]{2,1,0:T(8,128)(2,1)} %get-tuple-element.353), channel_id=1, source_target_pairs={{0,1},{1,0},{2,3},{3,2},{4,5},{5,4},{6,7},{7,6},{8,9},{9,8},{10,11... | collective-permute-start | bytes 1966088 | tf_op jit(solution)/shard_map/ppermute | solution.py:924
  476.3 17.2 %collective-permute-start.37 = (bf16[2,32,5120]{2,1,0:T(8,128)(2,1)}, bf16[2,32,5120]{2,1,0:T(8,128)(2,1)}, u32[]{:S(2)}, u32[]{:S(2)}) collective-permute-start(bf16[2,32,5120]{2,1,0:T(8,128)(2,1)} %get-tuple-element.354), channel_id=1, source_target_pairs={{0,2},{1,3},{2,0},{3,1},{4,6},{5,7},{6,4},{7,5},{8,10},{9,11},{10,... | collective-permute-start | bytes 1966088 | tf_op jit(solution)/shard_map/ppermute | solution.py:924
  500.8 19.6 %collective-permute-start.38 = (bf16[2,2,32,3072]{3,2,1,0:T(8,128)(2,1)}, bf16[2,2,32,3072]{3,2,1,0:T(8,128)(2,1)S(1)}, u32[]{:S(2)}, u32[]{:S(2)}) collective-permute-start(bf16[2,2,32,3072]{3,2,1,0:T(8,128)(2,1)} %get-tuple-element.367), channel_id=1, source_target_pairs={{0,2},{1,3},{2,0},{3,1},{4,6},{5,7},{6,4},{7,5},{8,10},{9,11},{10,... | collective-permute-start | bytes 2359304 | tf_op jit(solution)/shard_map/ppermute | solution.py:924
  501.3 20.0 %collective-permute-start.39 = (bf16[2,2,32,3072]{3,2,1,0:T(8,128)(2,1)}, bf16[2,2,32,3072]{3,2,1,0:T(8,128)(2,1)}, u32[]{:S(2)}, u32[]{:S(2)}) collective-permute-start(bf16[2,2,32,3072]{3,2,1,0:T(8,128)(2,1)} %get-tuple-element.368), channel_id=1, source_target_pairs={{0,1},{1,0},{2,3},{3,2},{4,5},{5,4},{6,7},{7,6},{8,9},{9,8},{10,11... | collective-permute-start | bytes 2359304 | tf_op jit(solution)/shard_map/ppermute | solution.py:924
  516.5 39.9 %all-to-all-start.3 = ((bf16[4,288,1024]{2,1,0:T(8,128)(2,1)}), bf16[4,288,1024]{2,1,0:T(8,128)(2,1)S(1)}, u32[]{:S(2)}, u32[]{:S(2)}) async-start(bf16[4,288,1024]{2,1,0:T(8,128)(2,1)} %get-tuple-element.382), calls=%async_computation.3 | async-start | bytes 4718592 | tf_op jit(solution)/shard_map/all_to_all | solution.py:1281
  525.2 31.2 %collective-permute-start.40 = (bf16[2,32,3072]{2,1,0:T(8,128)(2,1)}, bf16[2,32,3072]{2,1,0:T(8,128)(2,1)}, u32[]{:S(2)}, u32[]{:S(2)}) collective-permute-start(bf16[2,32,3072]{2,1,0:T(8,128)(2,1)} %get-tuple-element.371), channel_id=1, source_target_pairs={{0,1},{1,0},{2,3},{3,2},{4,5},{5,4},{6,7},{7,6},{8,9},{9,8},{10,11... | collective-permute-start | bytes 1179656 | tf_op jit(solution)/shard_map/ppermute | solution.py:924
  527.2 29.2 %collective-permute-start.41 = (bf16[2,32,3072]{2,1,0:T(8,128)(2,1)}, bf16[2,32,3072]{2,1,0:T(8,128)(2,1)}, u32[]{:S(2)}, u32[]{:S(2)}) collective-permute-start(bf16[2,32,3072]{2,1,0:T(8,128)(2,1)} %get-tuple-element.372), channel_id=1, source_target_pairs={{0,2},{1,3},{2,0},{3,1},{4,6},{5,7},{6,4},{7,5},{8,10},{9,11},{10,... | collective-permute-start | bytes 1179656 | tf_op jit(solution)/shard_map/ppermute | solution.py:924
  528.7 19.3 %collective-permute-start.42 = (bf16[32,5120]{1,0:T(8,128)(2,1)}, bf16[32,5120]{1,0:T(8,128)(2,1)}, u32[]{:S(2)}, u32[]{:S(2)}) collective-permute-start(bf16[32,5120]{1,0:T(8,128)(2,1)} %fusion.41), channel_id=1, source_target_pairs={{0,8},{1,9},{2,10},{3,11},{4,12},{5,13},{6,14},{7,15},{8,0},{9,1},... | collective-permute-start | bytes 983048 | tf_op jit(solution)/shard_map/ppermute | solution.py:924
  530.5 25.9 %collective-permute-start.43 = (bf16[32,5120]{1,0:T(8,128)(2,1)}, bf16[32,5120]{1,0:T(8,128)(2,1)}, u32[]{:S(2)}, u32[]{:S(2)}) collective-permute-start(bf16[32,5120]{1,0:T(8,128)(2,1)} %get-tuple-element.374), channel_id=1, source_target_pairs={{0,16},{1,17},{2,18},{3,19},{4,20},{5,21},{6,22},{7,23},{8,24},{9,... | collective-permute-start | bytes 983048 | tf_op jit(solution)/shard_map/ppermute | solution.py:924
  532.6 23.8 %collective-permute-start.44 = (bf16[32,5120]{1,0:T(8,128)(2,1)}, bf16[32,5120]{1,0:T(8,128)(2,1)}, u32[]{:S(2)}, u32[]{:S(2)}) collective-permute-start(bf16[32,5120]{1,0:T(8,128)(2,1)} %get-tuple-element.375), channel_id=1, source_target_pairs={{0,24},{1,25},{2,26},{3,27},{4,28},{5,29},{6,30},{7,31},{8,16},{9,... | collective-permute-start | bytes 983048 | tf_op jit(solution)/shard_map/ppermute | solution.py:924
  563.4 13.9 %all-to-all-start.4 = ((f32[32,1,544]{2,1,0:T(1,128)}), f32[32,1,544]{2,1,0:T(1,128)S(1)}, u32[]{:S(2)}, u32[]{:S(2)}) async-start(f32[32,1,544]{2,1,0:T(1,128)} %copy.84), calls=%async_computation.6 | async-start | bytes 163840 | tf_op jit(solution)/shard_map/all_to_all | solution.py:1297
  569.2 12.4 %collective-permute-start.45 = (bf16[32,3072]{1,0:T(8,128)(2,1)S(1)}, bf16[32,3072]{1,0:T(8,128)(2,1)S(1)}, u32[]{:S(2)}, u32[]{:S(2)}) collective-permute-start(bf16[32,3072]{1,0:T(8,128)(2,1)S(1)} %fusion.44), channel_id=1, source_target_pairs={{0,8},{1,9},{2,10},{3,11},{4,12},{5,13},{6,14},{7,15},{8,0},{9,1},... | collective-permute-start | bytes 589832 | tf_op jit(solution)/shard_map/ppermute | solution.py:924
  571.1 17.3 %collective-permute-start.46 = (bf16[32,3072]{1,0:T(8,128)(2,1)}, bf16[32,3072]{1,0:T(8,128)(2,1)S(1)}, u32[]{:S(2)}, u32[]{:S(2)}) collective-permute-start(bf16[32,3072]{1,0:T(8,128)(2,1)} %get-tuple-element.393), channel_id=1, source_target_pairs={{0,16},{1,17},{2,18},{3,19},{4,20},{5,21},{6,22},{7,23},{8,24},{9,... | collective-permute-start | bytes 589832 | tf_op jit(solution)/shard_map/ppermute | solution.py:924
  573.5 14.9 %collective-permute-start.47 = (bf16[32,3072]{1,0:T(8,128)(2,1)S(1)}, bf16[32,3072]{1,0:T(8,128)(2,1)}, u32[]{:S(2)}, u32[]{:S(2)}) collective-permute-start(bf16[32,3072]{1,0:T(8,128)(2,1)S(1)} %get-tuple-element.394), channel_id=1, source_target_pairs={{0,24},{1,25},{2,26},{3,27},{4,28},{5,29},{6,30},{7,31},{8,16},{9,... | collective-permute-start | bytes 589832 | tf_op jit(solution)/shard_map/ppermute | solution.py:924
  (37 other events, 279.9 us)
Sparse Core Ops, SparseCore 0:
  14.2 176.8 all-gather.1
  469.6 27.2 reduce-scatter.2
  499.3 25.7 reduce-scatter.4
